TPU v7x, 32 devices: a whole 2x2x4 slice. The times are simulated.
32 devices in a mesh: gx: 16 (over z, x, core), gy: 2 (over y).
Axes of the slice: x: 2, y: 2, z: 4, core: 2. Of those that a mesh axis runs over, the one named last changes fastest.
Arguments:
- trial_orbitals: bfloat16 [96, 16, 32, 256], P('gx', 'gy'), may hold values from -8 to 8
- potential: float32 [96, 16, 32], P('gx', 'gy'), may hold values from 0.1 to 10
Outputs:
- filtered_orbitals: bfloat16 [96, 16, 32, 256], P('gx', 'gy')
- upper_factor: float32 [256, 256], replicated
All inputs are finite; a program needn't handle non-finite values.
Results may differ from a plain program's by a relative error of at most 0.0005.
The roundings to bfloat16 on the way count: a program that leaves them out, or rounds other values in their place, can miss the bound.
Values may be sent and summed in bfloat16 or wider, within the bound.
No kernel may reach another device: no remote copies, remote signals or barrier semaphores. Data moves between devices by JAX's collectives and lax.ppermute only.
A program may use at most 64 MiB of HBM per device.

v0:
```python
import jax
import jax.numpy as jnp
from jax import lax
from jax.sharding import PartitionSpec as P

DEG = 3


STENCIL_WEIGHTS = (
    -5369.0 / 1800.0,
    12.0 / 7.0,
    -15.0 / 56.0,
    10.0 / 189.0,
    -1.0 / 112.0,
    2.0 / 1925.0,
    -1.0 / 16632.0,
)
stencil_reach = 6
filter_center = 11.5
filter_half = 8.5


def padded_2(block, sides, width):
    for axis, dim in sides:
        count = lax.axis_size(axis)
        forward = [(i, i + 1) for i in range(count - 1)]
        backward = [(target, source) for source, target in forward]
        low = lax.ppermute(
            lax.slice_in_dim(block, block.shape[dim] - width, None, axis=dim), axis, forward
        )
        high = lax.ppermute(lax.slice_in_dim(block, 0, width, axis=dim), axis, backward)
        block = jnp.concatenate([low, block, high], axis=dim)
    return block


def hamiltonian(field, along_x, along_y, potential):
    extent_x = field.shape[0]
    extent_y = field.shape[1]
    extent_z = field.shape[2]
    along_z = jnp.pad(field, ((0, 0), (0, 0), (stencil_reach, stencil_reach), (0, 0)))
    center = field.astype(jnp.float32)
    laplace = 3.0 * STENCIL_WEIGHTS[0] * center
    for offset in range(1, stencil_reach + 1):
        upper = stencil_reach + offset
        lower = stencil_reach - offset
        summed = along_x[upper : upper + extent_x].astype(jnp.float32) + along_x[
            lower : lower + extent_x
        ].astype(jnp.float32)
        summed = (
            summed
            + along_y[:, upper : upper + extent_y].astype(jnp.float32)
            + along_y[:, lower : lower + extent_y].astype(jnp.float32)
        )
        summed = (
            summed
            + along_z[:, :, upper : upper + extent_z].astype(jnp.float32)
            + along_z[:, :, lower : lower + extent_z].astype(jnp.float32)
        )
        laplace = laplace + STENCIL_WEIGHTS[offset] * summed
    return potential[:, :, :, None] * center - 0.5 * laplace


def chebyshev(start, apply_operator):
    previous = start
    current = (
        (apply_operator(start) - filter_center * start.astype(jnp.float32)) / filter_half
    ).astype(jnp.bfloat16)
    for degree in range(1, DEG):
        shifted = apply_operator(current) - filter_center * current.astype(jnp.float32)
        following = (2.0 * shifted / filter_half - previous.astype(jnp.float32)).astype(
            jnp.bfloat16
        )
        previous, current = (current, following)
    return current


def column_cholesky(matrix):
    order = matrix.shape[0]
    index = jnp.arange(order, dtype=jnp.int32)

    def column_step(column, lower):
        row_j = lax.dynamic_slice_in_dim(lower, column, 1, 0)[0]
        target = lax.dynamic_slice_in_dim(matrix, column, 1, 1)[:, 0]
        partial_sum = jnp.dot(
            lower, row_j, precision=lax.Precision.HIGHEST, preferred_element_type=jnp.float32
        )
        residual = target - partial_sum
        pivot = jnp.sqrt(jnp.sum(jnp.where(index == column, residual, jnp.float32(0.0))))
        values = jnp.where(index >= column, residual / pivot, jnp.float32(0.0))
        return lax.dynamic_update_slice_in_dim(lower, values[:, None], column, 1)

    return lax.fori_loop(0, order, column_step, jnp.zeros((order, order), jnp.float32))


def upper_inverse(upper):
    order = upper.shape[0]
    index = jnp.arange(order, dtype=jnp.int32)

    def upper_step(count, result):
        row = order - 1 - count
        upper_row = lax.dynamic_slice_in_dim(upper, row, 1, 0)[0]
        pivot = jnp.sum(jnp.where(index == row, upper_row, jnp.float32(0.0)))
        off_row = jnp.where(index > row, upper_row, jnp.float32(0.0))
        carried = jnp.dot(
            off_row, result, precision=lax.Precision.HIGHEST, preferred_element_type=jnp.float32
        )
        unit = jnp.where(index == row, jnp.float32(1.0), jnp.float32(0.0))
        values = (unit - carried) / pivot
        return lax.dynamic_update_slice_in_dim(result, values[None, :], row, 0)

    return lax.fori_loop(0, order, upper_step, jnp.zeros((order, order), jnp.float32))


def shards(trial_orbitals, potential):
    extent_x = trial_orbitals.shape[0]
    extent_y = trial_orbitals.shape[1]
    columns = trial_orbitals.shape[3]

    def apply_operator(values):
        padded = padded_2(values, (("gx", 0), ("gy", 1)), stencil_reach)
        along_x = padded[:, stencil_reach : stencil_reach + extent_y]
        along_y = padded[stencil_reach : stencil_reach + extent_x, :]
        return hamiltonian(values, along_x, along_y, potential)

    filtered = chebyshev(trial_orbitals, apply_operator)
    rows = filtered.reshape(-1, columns)
    total_cells = rows.shape[0] * lax.axis_size("gx") * lax.axis_size("gy")
    local_gram = lax.dot_general(
        rows, rows, (((0,), (0,)), ((), ())), preferred_element_type=jnp.float32
    )
    gram_matrix = lax.psum(local_gram, ("gx", "gy"))
    lower_factor = column_cholesky(gram_matrix)
    upper_factor = lower_factor.T / jnp.sqrt(jnp.float32(total_cells))
    inverse = upper_inverse(upper_factor)
    rotated = jnp.dot(
        rows.astype(jnp.float32),
        inverse,
        precision=lax.Precision.HIGHEST,
        preferred_element_type=jnp.float32,
    )
    return (rotated.astype(jnp.bfloat16).reshape(trial_orbitals.shape), upper_factor)


def solution(mesh):
    placed = (P("gx", "gy", None, None), P("gx", "gy", None))
    return jax.shard_map(
        shards,
        mesh=mesh,
        in_specs=placed,
        out_specs=(P("gx", "gy", None, None), P()),
        check_vma=False,
    )
```

profile of v0, /device:TPU:0, one launch (start us, length us, event | category | flops | bytes accessed | tf_op | source)
XLA Modules:
  0.0 1371.9 jit_solution(1663202187090404285)
XLA Ops:
  7.2 2.5 collective-permute-start.1
  9.8 1.3 collective-permute-start
  11.1 0.8 collective-permute-done.1
  12.2 4.0 collective-permute-done
  16.8 1.3 collective-permute-start.2
  18.1 4.8 collective-permute-start.3
  22.9 24.0 %collective-permute-done.2 = bf16[18,6,32,256]{3,2,1,0:T(8,128)(2,1)S(1)} collective-permute-done((bf16[18,6,32,256]{3,2,1,0:T(8,128)(2,1)S(1)}, bf16[18,6,32,256]{3,2,1,0:T(8,128)(2,1)S(1)}, u32[]{:S(2)}, u32[]{:S(2)}) %collective-permute-start.2) | collective-permute-done | bytes 1769504 | tf_op jit(solution)/shard_map/ppermute | solution.py:31
  46.9 1.8 collective-permute-done.3
  48.7 5.7 fusion.27
  54.5 1.3 collective-permute-start.4
  55.8 15.7 %collective-permute-start.5 = (bf16[6,8,32,256]{3,2,1,0:T(8,128)(2,1)S(1)}, bf16[6,8,32,256]{3,2,1,0:T(8,128)(2,1)S(1)}, u32[]{:S(2)}, u32[]{:S(2)}) collective-permute-start(bf16[6,8,32,256]{3,2,1,0:T(8,128)(2,1)S(1)} %fusion.27), channel_id=1, source_target_pairs={{0,2},{2,4},{4,6},{6,8},{8,10},{10,12},{12,14},{14,16},{16,18},{18... | collective-permute-start | bytes 2359304 | tf_op jit(solution)/shard_map/ppermute | solution.py:28
  71.5 1.8 collective-permute-done.5
  74.2 1.3 collective-permute-start.6
  75.5 4.8 collective-permute-start.7
  80.2 18.3 %collective-permute-done.6 = bf16[18,6,32,256]{3,2,1,0:T(8,128)(2,1)S(1)} collective-permute-done((bf16[18,6,32,256]{3,2,1,0:T(8,128)(2,1)S(1)}, bf16[18,6,32,256]{3,2,1,0:T(8,128)(2,1)S(1)}, u32[]{:S(2)}, u32[]{:S(2)}) %collective-permute-start.6) | collective-permute-done | bytes 1769504 | tf_op jit(solution)/shard_map/ppermute | solution.py:31
  98.6 1.6 collective-permute-done.7
  100.1 1.4 pad_maximum_fusion
  101.6 5.6 fusion.35
  107.2 1.3 collective-permute-start.8
  108.5 21.7 %collective-permute-start.9 = (bf16[6,8,32,256]{3,2,1,0:T(8,128)(2,1)S(1)}, bf16[6,8,32,256]{3,2,1,0:T(8,128)(2,1)S(1)}, u32[]{:S(2)}, u32[]{:S(2)}) collective-permute-start(bf16[6,8,32,256]{3,2,1,0:T(8,128)(2,1)S(1)} %fusion.35), channel_id=1, source_target_pairs={{0,2},{2,4},{4,6},{6,8},{8,10},{10,12},{12,14},{14,16},{16,18},{18... | collective-permute-start | bytes 2359304 | tf_op jit(solution)/shard_map/ppermute | solution.py:28
  130.2 1.8 collective-permute-done.9
  132.8 1.3 collective-permute-start.10
  134.1 4.8 collective-permute-start.11
  138.9 18.3 %collective-permute-done.10 = bf16[18,6,32,256]{3,2,1,0:T(8,128)(2,1)S(1)} collective-permute-done((bf16[18,6,32,256]{3,2,1,0:T(8,128)(2,1)S(1)}, bf16[18,6,32,256]{3,2,1,0:T(8,128)(2,1)S(1)}, u32[]{:S(2)}, u32[]{:S(2)}) %collective-permute-start.10) | collective-permute-done | bytes 1769504 | tf_op jit(solution)/shard_map/ppermute | solution.py:31
  157.3 1.6 collective-permute-done.11
  158.8 1.4 pad_maximum_fusion.1
  160.3 5.7 fusion.46
  165.9 1.1 convolution_bitcast_fusion
  167.1 169.8 %all-reduce.5.cloned.1.call-done = f32[256,256]{1,0:T(8,128)} async-done(((f32[256,256]{1,0:T(8,128)}), f32[256,256]{1,0:T(8,128)}) %all-reduce.5.cloned.1.call-update) | async-done | bytes 262160 | tf_op jit(solution)/shard_map/psum | solution.py:131
  336.9 1.1 copy.8
  338.0 622.4 %while.32 = (s32[]{:T(128)}, f32[256,256]{1,0:T(8,128)S(1)}, f32[256,256]{0,1:T(8,128)S(1)}, s32[]{:T(128)}, s32[]{:T(128)}) while((s32[]{:T(128)}, f32[256,256]{1,0:T(8,128)S(1)}, f32[256,256]{0,1:T(8,128)S(1)}, s32[]{:T(128)}, s32[]{:T(128)}) %tuple.92), condition=%wide.region_3.4_spmd.clone.clone, body=%wide.region_1.3_spmd.clone.clone.sunk | while | flops 788225 | bytes 275553 | solution.py:92
  960.6 402.7 %while.33 = (s32[]{:T(128)}, f32[256,256]{1,0:T(8,128)S(1)}, f32[256,256]{1,0:T(8,128)S(1)}, s32[]{:T(128)}, s32[]{:T(128)}, /*index=5*/s32[]{:T(128)}, s32[]{:T(128)}) while((s32[]{:T(128)}, f32[256,256]{1,0:T(8,128)S(1)}, f32[256,256]{1,0:T(8,128)S(1)}, s32[]{:T(128)}, s32[]{:T(128)}, /*index=5*/s32[]{:T(128)}, ...), condition=%wide.region_6.7_spmd.clone.clone, body=%wide.region_4.6_spmd.clone.clone.sunk | while | flops 788741 | bytes 272531 | solution.py:111
  961.4 0.7 fusion.101
  963.0 0.7 fusion.101
  964.6 0.7 fusion.101
  974.0 0.7 fusion.101
  975.6 0.7 fusion.101
  977.1 0.7 fusion.101
  978.7 0.7 fusion.101
  980.3 0.7 fusion.101
  988.1 0.7 fusion.101
  989.7 0.7 fusion.101
  991.3 0.7 fusion.101
  992.9 0.7 fusion.101
  994.4 0.7 fusion.101
  1003.9 0.7 fusion.101
  1005.5 0.7 fusion.101
  1363.3 1.7 convolution_convert_fusion
  (2823 shorter events, 817.3 us)
Async XLA Ops:
  7.2 4.8 copy-start
  7.2 329.7 %all-reduce.5.cloned.1.call-start = ((), (), s32[]{:S(2)}) async-start(), calls=%async_computation | async-start | bytes 524288 | tf_op jit(solution)/shard_map/psum | solution.py:131
  7.2 4.6 collective-permute-start.1
  9.8 6.4 collective-permute-start
  16.3 32.4 %copy-start.2 = (f32[6,8,32]{2,1,0:T(8,128)S(1)}, f32[6,8,32]{2,1,0:T(8,128)}, u32[]{:S(2)}) copy-start(f32[6,8,32]{2,1,0:T(8,128)} %param.7) | copy-start | bytes 18436
  16.8 30.1 %collective-permute-start.2 = (bf16[18,6,32,256]{3,2,1,0:T(8,128)(2,1)S(1)}, bf16[18,6,32,256]{3,2,1,0:T(8,128)(2,1)S(1)}, u32[]{:S(2)}, u32[]{:S(2)}) collective-permute-start(bf16[18,6,32,256]{3,2,1,0:T(8,128)(2,1)S(1)} %get-tuple-element.269), channel_id=1, source_target_pairs={{1,0},{3,2},{5,4},{7,6},{9,8},{11,10},{13,12},{15,14},{17,16},{19,... | collective-permute-start | bytes 5308424 | tf_op jit(solution)/shard_map/ppermute | solution.py:31
  18.1 30.6 %collective-permute-start.3 = (bf16[18,6,32,256]{3,2,1,0:T(8,128)(2,1)S(1)}, bf16[18,6,32,256]{3,2,1,0:T(8,128)(2,1)S(1)}, u32[]{:S(2)}, u32[]{:S(2)}) collective-permute-start(bf16[18,6,32,256]{3,2,1,0:T(8,128)(2,1)S(1)} %get-tuple-element.270), channel_id=1, source_target_pairs={{0,1},{2,3},{4,5},{6,7},{8,9},{10,11},{12,13},{14,15},{16,17},{18,... | collective-permute-start | bytes 5308424 | tf_op jit(solution)/shard_map/ppermute | solution.py:28
  54.5 17.0 %collective-permute-start.4 = (bf16[6,8,32,256]{3,2,1,0:T(8,128)(2,1)S(1)}, bf16[6,8,32,256]{3,2,1,0:T(8,128)(2,1)S(1)}, u32[]{:S(2)}, u32[]{:S(2)}) collective-permute-start(bf16[6,8,32,256]{3,2,1,0:T(8,128)(2,1)S(1)} %fusion.27), channel_id=1, source_target_pairs={{2,0},{4,2},{6,4},{8,6},{10,8},{12,10},{14,12},{16,14},{18,16},{20... | collective-permute-start | bytes 2359304 | tf_op jit(solution)/shard_map/ppermute | solution.py:31
  55.8 17.6 %collective-permute-start.5 = (bf16[6,8,32,256]{3,2,1,0:T(8,128)(2,1)S(1)}, bf16[6,8,32,256]{3,2,1,0:T(8,128)(2,1)S(1)}, u32[]{:S(2)}, u32[]{:S(2)}) collective-permute-start(bf16[6,8,32,256]{3,2,1,0:T(8,128)(2,1)S(1)} %fusion.27), channel_id=1, source_target_pairs={{0,2},{2,4},{4,6},{6,8},{8,10},{10,12},{12,14},{14,16},{16,18},{18... | collective-permute-start | bytes 2359304 | tf_op jit(solution)/shard_map/ppermute | solution.py:28
  74.2 24.4 %collective-permute-start.6 = (bf16[18,6,32,256]{3,2,1,0:T(8,128)(2,1)S(1)}, bf16[18,6,32,256]{3,2,1,0:T(8,128)(2,1)S(1)}, u32[]{:S(2)}, u32[]{:S(2)}) collective-permute-start(bf16[18,6,32,256]{3,2,1,0:T(8,128)(2,1)S(1)} %get-tuple-element.267), channel_id=1, source_target_pairs={{1,0},{3,2},{5,4},{7,6},{9,8},{11,10},{13,12},{15,14},{17,16},{19,... | collective-permute-start | bytes 5308424 | tf_op jit(solution)/shard_map/ppermute | solution.py:31
  75.5 24.7 %collective-permute-start.7 = (bf16[18,6,32,256]{3,2,1,0:T(8,128)(2,1)S(1)}, bf16[18,6,32,256]{3,2,1,0:T(8,128)(2,1)S(1)}, u32[]{:S(2)}, u32[]{:S(2)}) collective-permute-start(bf16[18,6,32,256]{3,2,1,0:T(8,128)(2,1)S(1)} %get-tuple-element.268), channel_id=1, source_target_pairs={{0,1},{2,3},{4,5},{6,7},{8,9},{10,11},{12,13},{14,15},{16,17},{18,... | collective-permute-start | bytes 5308424 | tf_op jit(solution)/shard_map/ppermute | solution.py:28
  107.2 23.0 %collective-permute-start.8 = (bf16[6,8,32,256]{3,2,1,0:T(8,128)(2,1)S(1)}, bf16[6,8,32,256]{3,2,1,0:T(8,128)(2,1)S(1)}, u32[]{:S(2)}, u32[]{:S(2)}) collective-permute-start(bf16[6,8,32,256]{3,2,1,0:T(8,128)(2,1)S(1)} %fusion.35), channel_id=1, source_target_pairs={{2,0},{4,2},{6,4},{8,6},{10,8},{12,10},{14,12},{16,14},{18,16},{20... | collective-permute-start | bytes 2359304 | tf_op jit(solution)/shard_map/ppermute | solution.py:31
  108.5 23.5 %collective-permute-start.9 = (bf16[6,8,32,256]{3,2,1,0:T(8,128)(2,1)S(1)}, bf16[6,8,32,256]{3,2,1,0:T(8,128)(2,1)S(1)}, u32[]{:S(2)}, u32[]{:S(2)}) collective-permute-start(bf16[6,8,32,256]{3,2,1,0:T(8,128)(2,1)S(1)} %fusion.35), channel_id=1, source_target_pairs={{0,2},{2,4},{4,6},{6,8},{8,10},{10,12},{12,14},{14,16},{16,18},{18... | collective-permute-start | bytes 2359304 | tf_op jit(solution)/shard_map/ppermute | solution.py:28
  132.8 24.4 %collective-permute-start.10 = (bf16[18,6,32,256]{3,2,1,0:T(8,128)(2,1)S(1)}, bf16[18,6,32,256]{3,2,1,0:T(8,128)(2,1)S(1)}, u32[]{:S(2)}, u32[]{:S(2)}) collective-permute-start(bf16[18,6,32,256]{3,2,1,0:T(8,128)(2,1)S(1)} %get-tuple-element.263), channel_id=1, source_target_pairs={{1,0},{3,2},{5,4},{7,6},{9,8},{11,10},{13,12},{15,14},{17,16},{19,... | collective-permute-start | bytes 5308424 | tf_op jit(solution)/shard_map/ppermute | solution.py:31
  134.1 24.7 %collective-permute-start.11 = (bf16[18,6,32,256]{3,2,1,0:T(8,128)(2,1)S(1)}, bf16[18,6,32,256]{3,2,1,0:T(8,128)(2,1)S(1)}, u32[]{:S(2)}, u32[]{:S(2)}) collective-permute-start(bf16[18,6,32,256]{3,2,1,0:T(8,128)(2,1)S(1)} %get-tuple-element.264), channel_id=1, source_target_pairs={{0,1},{2,3},{4,5},{6,7},{8,9},{10,11},{12,13},{14,15},{16,17},{18,... | collective-permute-start | bytes 5308424 | tf_op jit(solution)/shard_map/ppermute | solution.py:28
  1363.3 1.7 copy-start.1
Sparse Core Ops, SparseCore 0:
  167.2 169.6 all-reduce.4
where the time goes:
time: 1380 us; the launch traced here: 1370 us
  other arithmetic  524 us (38%)
  waiting for transfers between devices  244 us (18%)
  local copies, waits for them, and re-layouts  210 us (15%)
  loops' own time  200 us (14%)
  matrix products  117 us (8%)
  starting transfers between devices  62 us (4%)
  between operations  14.3 us (1%)
    another operation x1, loops' own time, column_cholesky(): lax.fori_loop(0, order, column_step, jnp.zeros((order, order), jnp.float32))  189 us
    div x256, other arithmetic, upper_step(): values = (unit - carried) / pivot  178 us
    reduce_sum x256, other arithmetic, column_step(): jnp.sum(jnp.where(index == column, residual, jnp.float32(0.0)))  170 us
    psum x1, waiting for transfers between devices, shards(): gram_matrix = lax.psum(local_gram, ('gx', 'gy'))  170 us
    dynamic_update_slice x256, local copies, waits for them, and re-layouts, column_step(): return lax.dynamic_update_slice_in_dim(lower, values[:, None], column, 1)  157 us
    reduce_sum x256, other arithmetic, upper_step(): pivot = jnp.sum(jnp.where(index == row, upper_row, jnp.float32(0.0)))  154 us
    dot_general x256, matrix products, column_step(): jnp.dot(lower, row_j, precision=lax.Precision.HIGHEST, preferred_element_...  67.9 us
    ppermute x6, waiting for transfers between devices, padded_2(): lax.ppermute(lax.slice_in_dim(block, 0, width, axis=dim), axis, backward)  64.7 us
  transfers between devices with their start and end apart: 13, of which 11 were waited for; matrix products, arithmetic and copies ran while one was open for 0% of the time, Pallas kernels for 0%

commit v1 on v0

v1 whole, which is shorter than its diff:
```python
import functools
import math

import jax
import jax.numpy as jnp
import ml_dtypes
import numpy as np
from jax import lax
from jax.experimental import pallas as pl
from jax.experimental.pallas import tpu as pltpu
from jax.sharding import PartitionSpec as P

DEG = 3


STENCIL_WEIGHTS = (
    -5369.0 / 1800.0,
    12.0 / 7.0,
    -15.0 / 56.0,
    10.0 / 189.0,
    -1.0 / 112.0,
    2.0 / 1925.0,
    -1.0 / 16632.0,
)
stencil_reach = 6
filter_center = 11.5
filter_half = 8.5
axes = ("gx", "gy")
vmem_limit = 48 * 1024 * 1024

center_shift = -1.5 * STENCIL_WEIGHTS[0] - filter_center
side_weights = tuple(-0.5 * weight / filter_half for weight in STENCIL_WEIGHTS)


def exact_parts(values):
    parts = []
    rest = np.asarray(values, np.float32)
    for _ in range(3):
        part = rest.astype(ml_dtypes.bfloat16)
        parts.append(part)
        rest = rest - part.astype(np.float32)
    return np.stack(parts)


def plane_weights(extent_y, extent_z):
    def band(extent, shift):
        matrix = np.zeros((extent, extent), np.float64)
        for source in range(extent):
            for target in range(extent):
                distance = abs(target - (source + shift))
                if 1 <= distance <= stencil_reach:
                    matrix[source, target] = side_weights[distance]
        return matrix

    eye_y, eye_z = np.eye(extent_y), np.eye(extent_z)
    own = np.kron(band(extent_y, 0), eye_z) + np.kron(eye_y, band(extent_z, 0))
    before = np.kron(band(extent_y, -extent_y), eye_z)
    after = np.kron(band(extent_y, extent_y), eye_z)
    return np.stack([exact_parts(part) for part in (own, before, after)])


def split_kernel(cells_ref, sent_ref):
    devices, rows, plane = sent_ref.shape
    layers = cells_ref.shape[0] // plane
    share = rows // layers
    for layer in range(0, layers, 2):
        pair = []
        for at in (layer, layer + 1):
            block = cells_ref[at * plane : (at + 1) * plane, :].astype(jnp.float32)
            pair.append(block.T.reshape(devices, share, plane))
        both = jnp.concatenate(pair, axis=1)
        sent_ref[:, layer * share : (layer + 2) * share, :] = both.astype(jnp.bfloat16)


def split_columns(cells, devices, plane):
    count, columns = cells.shape
    layers = count // plane
    share = columns // devices
    if share % 8 == 0 and layers % 2 == 0:
        return pl.pallas_call(
            split_kernel,
            out_shape=jax.ShapeDtypeStruct((devices, layers * share, plane), jnp.bfloat16),
            compiler_params=pltpu.CompilerParams(vmem_limit_bytes=vmem_limit),
        )(cells)
    spread = cells.reshape(layers, plane, devices, share).transpose(2, 0, 3, 1)
    return spread.reshape(devices, layers * share, plane)


def join_kernel(received_ref, cells_ref, gram_ref):
    devices, rows, plane = received_ref.shape
    layers = cells_ref.shape[0] // plane
    share = rows // layers
    columns = devices * share
    total = None
    for layer in range(0, layers, 2):
        both = received_ref[:, layer * share : (layer + 2) * share, :].astype(jnp.float32)
        for side in range(2):
            block = both[:, side * share : (side + 1) * share, :].reshape(columns, plane)
            at = (layer + side) * plane
            cells_ref[at : at + plane, :] = block.T.astype(jnp.bfloat16)
            narrow = block.astype(jnp.bfloat16)
            part = lax.dot_general(
                narrow, narrow, (((1,), (1,)), ((), ())), preferred_element_type=jnp.float32
            )
            total = part if total is None else total + part
    gram_ref[...] = total


def join_columns(received, layers):
    devices, rows, plane = received.shape
    share = rows // layers
    columns = devices * share
    if share % 8 == 0 and layers % 2 == 0:
        return pl.pallas_call(
            join_kernel,
            out_shape=(
                jax.ShapeDtypeStruct((layers * plane, columns), jnp.bfloat16),
                jax.ShapeDtypeStruct((columns, columns), jnp.float32),
            ),
            compiler_params=pltpu.CompilerParams(vmem_limit_bytes=vmem_limit),
        )(received)
    cells = received.reshape(devices, layers, share, plane).transpose(1, 3, 0, 2)
    cells = cells.reshape(layers * plane, columns)
    gram = lax.dot_general(cells, cells, (((0,), (0,)), ((), ())), preferred_element_type=jnp.float32)
    return cells, gram


def filter_kernel(
    bricks_x, bricks_y, received_ref, potential_ref, weights_ref, sent_ref,
    start_ref, first_ref, second_ref, plane_ref, center_ref,
):
    _, rows, plane = received_ref.shape
    layers = potential_ref.shape[1]
    share = rows // layers
    total = bricks_x * rows
    margin = stencil_reach * share
    for ref in (start_ref, first_ref, second_ref):
        ref[:margin, :] = jnp.zeros((margin, bricks_y * plane), jnp.float32)
        ref[margin + total :, :] = jnp.zeros((margin, bricks_y * plane), jnp.float32)
    for brick in range(bricks_x * bricks_y):
        at = margin + brick // bricks_y * rows
        lanes_at = brick % bricks_y * plane
        start_ref[at : at + rows, lanes_at : lanes_at + plane] = received_ref[brick].astype(jnp.float32)
        level = (potential_ref[brick] + center_shift) * (1.0 / filter_half)
        level = jnp.broadcast_to(level[:, None, :], (layers, share, plane)).reshape(rows, plane)
        center_ref[at - margin : at - margin + rows, lanes_at : lanes_at + plane] = level

    def apply(field_ref, write):
        narrow = [
            field_ref[margin : margin + total, b * plane : (b + 1) * plane].astype(jnp.bfloat16)
            for b in range(bricks_y)
        ]
        for b in range(bricks_y):
            fields, weights = [], []
            for kind, other in ((0, b), (1, b - 1), (2, b + 1)):
                if 0 <= other < bricks_y:
                    for part in range(weights_ref.shape[1]):
                        fields.append(narrow[other])
                        weights.append(weights_ref[kind, part])
            plane_ref[:, b * plane : (b + 1) * plane] = jnp.dot(
                jnp.concatenate(fields, axis=1),
                jnp.concatenate(weights, axis=0),
                preferred_element_type=jnp.float32,
            )

        def one_brick(brick, at):
            for b in range(bricks_y):
                here = slice(b * plane, (b + 1) * plane)
                window = field_ref[pl.ds(at, rows + 2 * margin), here]
                value = center_ref[pl.ds(at, rows), here] * window[margin : margin + rows]
                value = value + plane_ref[pl.ds(at, rows), here]
                for distance in range(1, stencil_reach + 1):
                    low = margin - distance * share
                    high = margin + distance * share
                    pair = window[low : low + rows] + window[high : high + rows]
                    value = value + side_weights[distance] * pair
                write(brick, b, at, here, value)

        if rows % 8 == 0:
            @pl.loop(0, bricks_x)
            def _(brick):
                one_brick(brick, pl.multiple_of(brick * rows, 8))
        else:
            for brick in range(bricks_x):
                one_brick(brick, brick * rows)

    def write_first(brick, b, at, here, value):
        first_ref[pl.ds(at + margin, rows), here] = value.astype(jnp.bfloat16).astype(jnp.float32)

    def write_second(brick, b, at, here, value):
        following = 2.0 * value - start_ref[pl.ds(at + margin, rows), here]
        second_ref[pl.ds(at + margin, rows), here] = following.astype(jnp.bfloat16).astype(jnp.float32)

    def write_third(brick, b, at, here, value):
        following = 2.0 * value - first_ref[pl.ds(at + margin, rows), here]
        sent_ref[brick * bricks_y + b] = following.astype(jnp.bfloat16)

    apply(start_ref, write_first)
    apply(first_ref, write_second)
    apply(second_ref, write_third)


def filter_columns(received, potential, weights, bricks_x, bricks_y):
    _, rows, plane = received.shape
    share = rows // potential.shape[1]
    total = bricks_x * rows
    padded = total + 2 * stencil_reach * share
    width = bricks_y * plane
    field = pltpu.VMEM((padded, width), jnp.float32)
    whole = pltpu.VMEM((total, width), jnp.float32)
    return pl.pallas_call(
        functools.partial(filter_kernel, bricks_x, bricks_y),
        out_shape=jax.ShapeDtypeStruct(received.shape, jnp.bfloat16),
        scratch_shapes=[field, field, field, whole, whole],
        compiler_params=pltpu.CompilerParams(vmem_limit_bytes=vmem_limit),
    )(received, potential, weights)


lanes = 128
panel_rows = 8
block_rows = 64


def row_splat(values, row):
    return jnp.broadcast_to(values[row : row + 1, :], values.shape)


def lane_splat(values, lane):
    return jnp.broadcast_to(values[:, lane : lane + 1], (panel_rows, lanes))


def panel_inverse(columns):
    row = lax.broadcasted_iota(jnp.int32, (panel_rows, lanes), 0)
    columns = list(columns)
    full = [jnp.where(row == k, 1.0, 0.0).astype(jnp.float32) for k in range(panel_rows)]
    forward = list(full)
    pivots = jnp.zeros((panel_rows, lanes), jnp.float32)
    for step in range(panel_rows):
        pivot = row_splat(columns[step], step)
        scale = 1.0 / pivot
        pivots = jnp.where(row == step, pivot, pivots)
        others = jnp.where(row == step, 0.0, columns[step])
        for k in range(step + 1, panel_rows):
            columns[k] = columns[k] - others * (row_splat(columns[k], step) * scale)
        for k in range(step):
            forward[k] = jnp.where(row == step, full[k], forward[k])
            full[k] = full[k] - others * (row_splat(full[k], step) * scale)
        full[step] = full[step] - others * scale
    inverse_pivots = 1.0 / pivots
    root = lax.rsqrt(pivots)
    full = [column * inverse_pivots for column in full]
    forward = [column * root for column in forward]
    return full, forward


def combine(columns, rows):
    width = rows.shape[1] // lanes
    parts = []
    for part in range(width):
        piece = rows[:, part * lanes : (part + 1) * lanes]
        total = None
        for k, column in enumerate(columns):
            term = column * row_splat(piece, k)
            total = term if total is None else total + term
        parts.append(total)
    return jnp.concatenate(parts, axis=1)


def factor_kernel(scale, gram_ref, rows_ref, rotated_ref, upper_ref, factor_ref, inverse_ref):
    order = gram_ref.shape[0]
    factor_ref[...] = jnp.zeros((order, order), jnp.float32)
    inverse_ref[...] = jnp.zeros((order, order), jnp.float32)
    for start in range(0, order, block_rows):
        left = start // lanes * lanes
        right = left + lanes
        local = start - left
        row = lax.broadcasted_iota(jnp.int32, (block_rows, right), 0)
        col = lax.broadcasted_iota(jnp.int32, (block_rows, right), 1)
        unit = jnp.where(col == row + start, 1.0, 0.0).astype(jnp.float32)
        block = jnp.concatenate([gram_ref[start : start + block_rows, left:order], unit], axis=1)
        if start > 0:
            done = jnp.concatenate(
                [factor_ref[:start, left:order], inverse_ref[:start, :right]], axis=1
            )
            update = lax.dot_general(
                factor_ref[:start, left : left + lanes],
                done,
                (((0,), (0,)), ((), ())),
                precision=lax.Precision.HIGHEST,
                preferred_element_type=jnp.float32,
            )
            block = block - update[local : local + block_rows]
        groups = [
            block[g : g + panel_rows] for g in range(0, block_rows, panel_rows)
        ]
        for index in range(len(groups)):
            lane = local + index * panel_rows
            rows = groups[index]
            full, forward = panel_inverse([lane_splat(rows, lane + k) for k in range(panel_rows)])
            step_rows = combine(full, rows)
            for other in range(index + 1, len(groups)):
                target = groups[other]
                columns = [lane_splat(target, lane + k) for k in range(panel_rows)]
                groups[other] = target - combine(columns, step_rows)
            finished = combine(forward, rows)
            at = start + index * panel_rows
            factor_ref[at : at + panel_rows, left:order] = finished[:, : order - left]
            inverse_ref[at : at + panel_rows, :right] = finished[:, order - left :]
    row = lax.broadcasted_iota(jnp.int32, (order, order), 0)
    col = lax.broadcasted_iota(jnp.int32, (order, order), 1)
    upper_ref[...] = jnp.where(col >= row, factor_ref[...] * (1.0 / scale), 0.0)
    inverse = jnp.where(col <= row, inverse_ref[...] * scale, 0.0)
    high = inverse.astype(jnp.bfloat16)
    rest = inverse - high.astype(jnp.float32)
    middle = rest.astype(jnp.bfloat16)
    low = (rest - middle.astype(jnp.float32)).astype(jnp.bfloat16)
    count = rows_ref.shape[0]
    chunk = math.gcd(count, 512)
    for at in range(0, count, chunk):
        piece = rows_ref[at : at + chunk, :]
        total = jnp.zeros((chunk, order), jnp.float32)
        for part in (low, middle, high):
            total = total + lax.dot_general(
                piece, part, (((1,), (1,)), ((), ())), preferred_element_type=jnp.float32
            )
        rotated_ref[at : at + chunk, :] = total.astype(jnp.bfloat16)


def factor_and_rotate(gram_matrix, rows, total_cells):
    order = gram_matrix.shape[0]
    count = rows.shape[0]
    return pl.pallas_call(
        functools.partial(factor_kernel, math.sqrt(total_cells)),
        out_shape=(
            jax.ShapeDtypeStruct((count, order), jnp.bfloat16),
            jax.ShapeDtypeStruct((order, order), jnp.float32),
        ),
        scratch_shapes=[
            pltpu.VMEM((order, order), jnp.float32),
            pltpu.VMEM((order, order), jnp.float32),
        ],
        compiler_params=pltpu.CompilerParams(vmem_limit_bytes=vmem_limit),
    )(gram_matrix, rows)


def sum_over_devices(values):
    count = lax.axis_size(axes)
    order = values.shape[0]
    if order % count:
        return lax.psum(values, axes)
    share = order // count
    parts = lax.all_to_all(values.reshape(count, share, order), axes, 0, 0)
    total = jnp.sum(parts, axis=0)
    spread = jnp.broadcast_to(total[None], (count, share, order))
    return lax.all_to_all(spread, axes, 0, 0).reshape(order, order)


def shards(trial_orbitals, potential):
    layers, extent_y, extent_z, columns = trial_orbitals.shape
    bricks_x, bricks_y = lax.axis_size("gx"), lax.axis_size("gy")
    devices = bricks_x * bricks_y
    plane = extent_y * extent_z
    total_cells = devices * layers * plane
    weights = jnp.asarray(plane_weights(extent_y, extent_z))

    sent = split_columns(trial_orbitals.reshape(layers * plane, columns), devices, plane)
    received = lax.all_to_all(sent, axes, 0, 0)
    levels = jnp.broadcast_to(potential.reshape(1, layers, plane), (devices, layers, plane))
    levels = lax.all_to_all(levels, axes, 0, 0)
    filtered = filter_columns(received, levels, weights, bricks_x, bricks_y)
    received = lax.all_to_all(filtered, axes, 0, 0)
    rows, local_gram = join_columns(received, layers)
    gram_matrix = sum_over_devices(local_gram)
    rotated, upper_factor = factor_and_rotate(gram_matrix, rows, total_cells)
    return (rotated.reshape(trial_orbitals.shape), upper_factor)


def solution(mesh):
    placed = (P("gx", "gy", None, None), P("gx", "gy", None))
    return jax.shard_map(
        shards,
        mesh=mesh,
        in_specs=placed,
        out_specs=(P("gx", "gy", None, None), P()),
        check_vma=False,
    )
```

time: 1380 us -> 114 us (0.08)
  other arithmetic: 524 us -> 0.04 us
  waiting for transfers between devices: 244 us -> 10.4 us
  local copies, waits for them, and re-layouts: 210 us -> 1.64 us
  loops' own time: 200 us -> 0 us
  matrix products: 117 us -> 0 us
  blocking collectives: 0 us -> 73.7 us
  starting transfers between devices: 62 us -> 7.3 us
  Pallas kernels: 0 us -> 19.9 us
    reduce_sum x512 -> x1, other arithmetic: 324 us -> 0.04 us  [sum_over_devices(): total = jnp.sum(parts, axis=0)]
    another operation x2 -> x0, loops' own time: 200 us -> none  [the longest x1 189 us: column_cholesky(): lax.fori_loop(0, order, column_step, jnp.zeros((order, order), jnp.float32))]
    div x257 -> x0, other arithmetic: 178 us -> none  [the longest x256 178 us: upper_step(): values = (unit - carried) / pivot]
    psum x1 -> x0, waiting for transfers between devices: 170 us -> none  [shards(): gram_matrix = lax.psum(local_gram, ('gx', 'gy'))]
    dynamic_update_slice x512 -> x0, local copies, waits for them, and re-layouts: 168 us -> none  [the longest x256 157 us: column_step(): return lax.dynamic_update_slice_in_dim(lower, values[:, None], column, 1)]
    dot_general x514 -> x0, matrix products: 117 us -> none  [the longest x256 67.9 us: column_step(): jnp.dot(lower, row_j, precision=lax.Precision.HIGHEST, preferred_element_...]
    ppermute x12 -> x0, waiting for transfers between devices: 74.1 us -> none  [the longest x6 64.7 us: padded_2(): lax.ppermute(lax.slice_in_dim(block, 0, width, axis=dim), axis, backward)]
    all_to_all x0 -> x4, blocking collectives: none -> 73.7 us  [the longest x1 24.1 us: shards(): received = lax.all_to_all(filtered, axes, 0, 0)]
  transfers between devices with their start and end apart: 13 -> 1, of which waited for: 11 -> 1; matrix products, arithmetic and copies ran while one was open for 0% -> 0% of each run, Pallas kernels for 0% -> 0%
where the time goes in v1:
time: 114 us
  blocking collectives  73.7 us (65%)
  Pallas kernels  19.9 us (17%)
  waiting for transfers between devices  10.4 us (9%)
  starting transfers between devices  7.3 us (6%)
  local copies, waits for them, and re-layouts  1.64 us (1%)
    all_to_all x1, blocking collectives, shards(): received = lax.all_to_all(filtered, axes, 0, 0)  24.1 us
    all_to_all x1, blocking collectives, shards(): received = lax.all_to_all(sent, axes, 0, 0)  22.7 us
    all_to_all x1, blocking collectives, sum_over_devices(): parts = lax.all_to_all(values.reshape(count, share, order), axes, 0, 0)  14.1 us
    all_to_all x1, blocking collectives, sum_over_devices(): return lax.all_to_all(spread, axes, 0, 0).reshape(order, order)  12.8 us
    pallas_call x1, Pallas kernels, factor_and_rotate(): pl.pallas_call(functools.partial(factor_kernel, math.sqrt(total_cells)),...  11 us
    all_to_all x1, waiting for transfers between devices, shards(): levels = lax.all_to_all(levels, axes, 0, 0)  10.4 us
    pallas_call x1, Pallas kernels, filter_columns(): pl.pallas_call(functools.partial(filter_kernel, bricks_x, bricks_y), out_...  8.22 us
    all_to_all x1, starting transfers between devices, shards(): levels = lax.all_to_all(levels, axes, 0, 0)  7.3 us
  transfers between devices with their start and end apart: 1, of which 1 were waited for; matrix products, arithmetic and copies ran while one was open for 0% of the time, Pallas kernels for 0%

profile of v1, /device:TPU:0, one launch (start us, length us, event | category | flops | bytes accessed | tf_op | source)
XLA Modules:
  0.0 113.7 jit_solution(17398026790354355166)
XLA Ops:
  0.6 0.0 copy-start.1
  0.6 0.9 broadcast_in_dim.6
  1.5 0.7 broadcast_in_dim.14
  2.2 7.3 %all-to-all-start.1 = ((f32[32,6,256]{2,1,0:T(8,128)}), f32[32,6,256]{2,1,0:T(8,128)S(1)}, u32[]{:S(2)}, u32[]{:S(2)}) async-start(f32[32,6,256]{2,1,0:T(8,128)} %broadcast_in_dim.14), calls=%async_computation.1 | async-start | bytes 524288 | tf_op jit(solution)/shard_map/all_to_all | solution.py:369
  9.6 0.0 copy-done.1
  9.6 0.0 copy-start
  9.6 0.3 shard_map.50
  9.8 10.4 %all-to-all-done.1.potential_ref = f32[32,6,256]{2,1,0:T(8,128)S(1)} async-done(((f32[32,6,256]{2,1,0:T(8,128)}), f32[32,6,256]{2,1,0:T(8,128)S(1)}, u32[]{:S(2)}, u32[]{:S(2)}) %all-to-all-start.1) | async-done | bytes 196640 | tf_op jit(solution)/shard_map/all_to_all | solution.py:369
  20.2 22.7 %all_to_all.25.received_ref = bf16[32,48,256]{2,1,0:T(8,128)(2,1)S(1)} all-to-all(bf16[32,48,256]{2,1,0:T(8,128)(2,1)S(1)} %shard_map.50), channel_id=1, replica_groups=mesh['gx'=16,'gy'=2] {'gx','gy'}, dimensions={0} | all-to-all | bytes 1572864 | tf_op jit(solution)/shard_map/all_to_all | solution.py:367
  43.0 0.0 copy-done
  43.0 8.2 %shard_map.51 = bf16[32,48,256]{2,1,0:T(8,128)(2,1)S(1)} custom-call(bf16[32,48,256]{2,1,0:T(8,128)(2,1)S(1)} %all_to_all.25.received_ref, f32[32,6,256]{2,1,0:T(8,128)S(1)} %all-to-all-done.1.potential_ref, bf16[3,3,256,256]{3,2,1,0:T(8,128)(2,1)S(1)} %copy-done), custom_call_target="tpu_custom_call" | custom-call | tf_op jit(solution)/shard_map/pallas_call | solution.py:211
  51.2 24.1 %all_to_all.26.received_ref = bf16[32,48,256]{2,1,0:T(8,128)(2,1)S(1)} all-to-all(bf16[32,48,256]{2,1,0:T(8,128)(2,1)S(1)} %shard_map.51), channel_id=1, replica_groups=mesh['gx'=16,'gy'=2] {'gx','gy'}, dimensions={0} | all-to-all | bytes 1572864 | tf_op jit(solution)/shard_map/all_to_all | solution.py:371
  75.3 0.4 shard_map.52
  75.7 14.1 %all_to_all.27 = f32[32,8,256]{2,1,0:T(8,128)S(1)} all-to-all(f32[32,8,256]{2,1,0:T(8,128)S(1)} %bitcast.6), channel_id=1, replica_groups=mesh['gx'=16,'gy'=2] {'gx','gy'}, dimensions={0} | all-to-all | bytes 524288 | tf_op jit(solution)/shard_map/all_to_all | solution.py:352
  89.9 12.8 %all_to_all.28 = f32[32,8,256]{2,1,0:T(8,128)S(1)} all-to-all(f32[32,8,256]{2,1,0:T(8,128)S(1)} %broadcast_in_dim.15), channel_id=1, replica_groups=mesh['gx'=16,'gy'=2] {'gx','gy'}, dimensions={0} | all-to-all | bytes 524288 | tf_op jit(solution)/shard_map/all_to_all | solution.py:355
  102.7 11.0 %shard_map.53 = (bf16[1536,256]{1,0:T(8,128)(2,1)}, f32[256,256]{1,0:T(8,128)}) custom-call(f32[256,256]{1,0:T(8,128)S(1)} %bitcast.4, bf16[1536,256]{1,0:T(8,128)(2,1)S(1)} %get-tuple-element.7.rows_ref), custom_call_target="tpu_custom_call" | custom-call | tf_op jit(solution)/shard_map/pallas_call | solution.py:332
  (2 shorter events, 0.1 us)
Async XLA Ops:
  0.6 8.9 %copy-start.1 = (bf16[6,8,32,256]{3,2,1,0:T(8,128)(2,1)S(1)}, bf16[6,8,32,256]{3,2,1,0:T(8,128)(2,1)}, u32[]{:S(2)}) copy-start(bf16[6,8,32,256]{3,2,1,0:T(8,128)(2,1)} %param.3) | copy-start | bytes 2359300
  2.2 18.0 %all-to-all-start.1 = ((f32[32,6,256]{2,1,0:T(8,128)}), f32[32,6,256]{2,1,0:T(8,128)S(1)}, u32[]{:S(2)}, u32[]{:S(2)}) async-start(f32[32,6,256]{2,1,0:T(8,128)} %broadcast_in_dim.14), calls=%async_computation.1 | async-start | bytes 524288 | tf_op jit(solution)/shard_map/all_to_all | solution.py:369
  9.6 33.4 %copy-start = (bf16[3,3,256,256]{3,2,1,0:T(8,128)(2,1)S(1)}, bf16[3,3,256,256]{3,2,1,0:T(8,128)(2,1)}, u32[]{:S(2)}) copy-start(bf16[3,3,256,256]{3,2,1,0:T(8,128)(2,1)} %constant.4.clone.weights_ref) | copy-start | bytes 3538948

commit v2 on v1

--- a/solution.py
+++ b/solution.py
@@ -8,7 +8,7 @@
 from jax import lax
 from jax.experimental import pallas as pl
 from jax.experimental.pallas import tpu as pltpu
-from jax.sharding import PartitionSpec as P
+from jax.sharding import Mesh, PartitionSpec as P
 
 DEG = 3
 
@@ -25,7 +25,7 @@
 stencil_reach = 6
 filter_center = 11.5
 filter_half = 8.5
-axes = ("gx", "gy")
+axes = ("far", "near", "gy")
 vmem_limit = 48 * 1024 * 1024
 
 center_shift = -1.5 * STENCIL_WEIGHTS[0] - filter_center
@@ -103,7 +103,10 @@
                 narrow, narrow, (((1,), (1,)), ((), ())), preferred_element_type=jnp.float32
             )
             total = part if total is None else total + part
-    gram_ref[...] = total
+    half, quarter = columns // 2, columns // 4
+    gram_ref[:half, :] = total[:half]
+    gram_ref[half:, :half] = total[half : half + quarter, half:]
+    gram_ref[half:, half:] = total[half + quarter :, half:]
 
 
 def join_columns(received, layers):
@@ -115,14 +118,16 @@
             join_kernel,
             out_shape=(
                 jax.ShapeDtypeStruct((layers * plane, columns), jnp.bfloat16),
-                jax.ShapeDtypeStruct((columns, columns), jnp.float32),
+                jax.ShapeDtypeStruct((columns // 4 * 3, columns), jnp.float32),
             ),
             compiler_params=pltpu.CompilerParams(vmem_limit_bytes=vmem_limit),
         )(received)
     cells = received.reshape(devices, layers, share, plane).transpose(1, 3, 0, 2)
     cells = cells.reshape(layers * plane, columns)
     gram = lax.dot_general(cells, cells, (((0,), (0,)), ((), ())), preferred_element_type=jnp.float32)
-    return cells, gram
+    half, quarter = columns // 2, columns // 4
+    rest = jnp.concatenate([gram[half : half + quarter, half:], gram[half + quarter :, half:]], axis=1)
+    return cells, jnp.concatenate([gram[:half], rest], axis=0)
 
 
 def filter_kernel(
@@ -267,7 +272,8 @@
 
 
 def factor_kernel(scale, gram_ref, rows_ref, rotated_ref, upper_ref, factor_ref, inverse_ref):
-    order = gram_ref.shape[0]
+    order = gram_ref.shape[1]
+    half, quarter = order // 2, order // 4
     factor_ref[...] = jnp.zeros((order, order), jnp.float32)
     inverse_ref[...] = jnp.zeros((order, order), jnp.float32)
     for start in range(0, order, block_rows):
@@ -277,7 +283,13 @@
         row = lax.broadcasted_iota(jnp.int32, (block_rows, right), 0)
         col = lax.broadcasted_iota(jnp.int32, (block_rows, right), 1)
         unit = jnp.where(col == row + start, 1.0, 0.0).astype(jnp.float32)
-        block = jnp.concatenate([gram_ref[start : start + block_rows, left:order], unit], axis=1)
+        if start < half:
+            own = gram_ref[start : start + block_rows, :]
+        else:
+            side = (start - half) // quarter * half
+            at = half + (start - half) % quarter
+            own = gram_ref[at : at + block_rows, side : side + half]
+        block = jnp.concatenate([own, unit], axis=1)
         if start > 0:
             done = jnp.concatenate(
                 [factor_ref[:start, left:order], inverse_ref[:start, :right]], axis=1
@@ -327,7 +339,7 @@
 
 
 def factor_and_rotate(gram_matrix, rows, total_cells):
-    order = gram_matrix.shape[0]
+    order = gram_matrix.shape[1]
     count = rows.shape[0]
     return pl.pallas_call(
         functools.partial(factor_kernel, math.sqrt(total_cells)),
@@ -344,20 +356,23 @@
 
 
 def sum_over_devices(values):
-    count = lax.axis_size(axes)
-    order = values.shape[0]
-    if order % count:
+    plane_axes = ("near", "gy")
+    plane, planes = lax.axis_size(plane_axes), lax.axis_size("far")
+    count, order = values.shape
+    if count % plane:
         return lax.psum(values, axes)
-    share = order // count
-    parts = lax.all_to_all(values.reshape(count, share, order), axes, 0, 0)
+    share = count // plane
+    parts = lax.all_to_all(values.reshape(plane, share, order), plane_axes, 0, 0)
     total = jnp.sum(parts, axis=0)
-    spread = jnp.broadcast_to(total[None], (count, share, order))
-    return lax.all_to_all(spread, axes, 0, 0).reshape(order, order)
+    spread = jnp.broadcast_to(total[None], (planes, share, order))
+    total = jnp.sum(lax.all_to_all(spread, "far", 0, 0), axis=0)
+    spread = jnp.broadcast_to(total[None], (plane, share, order))
+    return lax.all_to_all(spread, plane_axes, 0, 0).reshape(count, order)
 
 
 def shards(trial_orbitals, potential):
     layers, extent_y, extent_z, columns = trial_orbitals.shape
-    bricks_x, bricks_y = lax.axis_size("gx"), lax.axis_size("gy")
+    bricks_x, bricks_y = lax.axis_size(("far", "near")), lax.axis_size("gy")
     devices = bricks_x * bricks_y
     plane = extent_y * extent_z
     total_cells = devices * layers * plane
@@ -365,8 +380,7 @@
 
     sent = split_columns(trial_orbitals.reshape(layers * plane, columns), devices, plane)
     received = lax.all_to_all(sent, axes, 0, 0)
-    levels = jnp.broadcast_to(potential.reshape(1, layers, plane), (devices, layers, plane))
-    levels = lax.all_to_all(levels, axes, 0, 0)
+    levels = lax.all_gather(potential.reshape(layers, plane), axes)
     filtered = filter_columns(received, levels, weights, bricks_x, bricks_y)
     received = lax.all_to_all(filtered, axes, 0, 0)
     rows, local_gram = join_columns(received, layers)
@@ -376,11 +390,14 @@
 
 
 def solution(mesh):
-    placed = (P("gx", "gy", None, None), P("gx", "gy", None))
+    bricks_x, bricks_y = mesh.devices.shape
+    near = math.gcd(bricks_x, 4)
+    cut = Mesh(mesh.devices.reshape(bricks_x // near, near, bricks_y), axes)
+    cells = P(("far", "near"), "gy")
     return jax.shard_map(
         shards,
-        mesh=mesh,
-        in_specs=placed,
-        out_specs=(P("gx", "gy", None, None), P()),
+        mesh=cut,
+        in_specs=(cells, cells),
+        out_specs=(cells, P()),
         check_vma=False,
     )

time: 114 us -> 155 us (1.36)
  blocking collectives: 73.7 us -> 124 us
  waiting for transfers between devices: 10.4 us -> 0.01 us
    all_gather x0 -> x1, blocking collectives: none -> 76.3 us  [shards(): levels = lax.all_gather(potential.reshape(layers, plane), axes)]
    all_to_all x3, blocking collectives: 49.7 us -> 25 us  [the longest x1 8.8 us: sum_over_devices(): lax.all_to_all(values.reshape(plane, share, order), plane_axes, 0, 0)]
    all_to_all x1, waiting for transfers between devices: 10.4 us -> 0.01 us  [shards(): received = lax.all_to_all(sent, axes, 0, 0)]
    broadcast_in_dim x3 -> x2, local copies, waits for them, and re-layouts: 1.63 us -> 0.02 us  [the longest x1 0.01 us: sum_over_devices(): spread = jnp.broadcast_to(total[None], (plane, share, order))]
  transfers between devices with their start and end apart: 1 -> 1, of which waited for: 1 -> 0; matrix products, arithmetic and copies ran while one was open for 0% -> 0% of each run, Pallas kernels for 0% -> 0%
where the time goes in v2:
time: 155 us; the launch traced here: 154 us
  blocking collectives  124 us (80%)
  Pallas kernels  20.8 us (13%)
  starting transfers between devices  7.3 us (5%)
    all_gather x1, blocking collectives, shards(): levels = lax.all_gather(potential.reshape(layers, plane), axes)  76.3 us
    all_to_all x1, blocking collectives, shards(): received = lax.all_to_all(filtered, axes, 0, 0)  23 us
    pallas_call x1, Pallas kernels, factor_and_rotate(): pl.pallas_call(functools.partial(factor_kernel, math.sqrt(total_cells)),...  11 us
    all_to_all x1, blocking collectives, sum_over_devices(): lax.all_to_all(values.reshape(plane, share, order), plane_axes, 0, 0)  8.8 us
    all_to_all x1, blocking collectives, sum_over_devices(): total = jnp.sum(lax.all_to_all(spread, 'far', 0, 0), axis=0)  8.49 us
    pallas_call x1, Pallas kernels, filter_columns(): pl.pallas_call(functools.partial(filter_kernel, bricks_x, bricks_y), out_...  8.23 us
    all_to_all x1, blocking collectives, sum_over_devices(): return lax.all_to_all(spread, plane_axes, 0, 0).reshape(count, order)  7.73 us
    all_to_all x1, starting transfers between devices, shards(): received = lax.all_to_all(sent, axes, 0, 0)  7.3 us
  transfers between devices with their start and end apart: 1, of which 0 were waited for; matrix products, arithmetic and copies ran while one was open for 0% of the time, Pallas kernels for 0%

profile of v2, /device:TPU:0, one launch (start us, length us, event | category | flops | bytes accessed | tf_op | source)
XLA Modules:
  0.0 154.4 jit_solution(8058161951590550065)
XLA Ops:
  0.6 0.0 copy-start.1
  0.6 1.1 copy-done.1
  1.8 0.0 copy-start.2
  1.8 1.2 shard_map.50
  2.9 0.0 copy-start
  2.9 7.3 %all-to-all-start = ((bf16[32,48,256]{2,1,0:T(8,128)(2,1)}), bf16[32,48,256]{2,1,0:T(8,128)(2,1)S(1)}, u32[]{:S(2)}, u32[]{:S(2)}) async-start(bf16[32,48,256]{2,1,0:T(8,128)(2,1)} %shard_map.50), calls=%async_computation | async-start | bytes 1572864 | tf_op jit(solution)/shard_map/all_to_all | solution.py:382
  10.2 0.0 copy-done.2
  10.2 0.1 all_gather_reshape.3
  10.3 76.3 %all_gather.3.potential_ref = f32[32,6,256]{2,1,0:T(8,128)S(1)} all-gather(f32[1,6,256]{2,1,0:T(8,128)S(1)} %all_gather_reshape.3), channel_id=1, replica_groups=mesh['far'=4,'near'=4,'gy'=2] {'far','near','gy'}, dimensions={0}, use_global_device_ids=true | all-gather | bytes 202752 | tf_op jit(solution)/shard_map/all_gather | solution.py:383
  86.6 0.0 all-to-all-done.received_ref
  86.7 0.0 copy-done
  86.7 8.2 %shard_map.51 = bf16[32,48,256]{2,1,0:T(8,128)(2,1)S(1)} custom-call(bf16[32,48,256]{2,1,0:T(8,128)(2,1)S(1)} %all-to-all-done.received_ref, f32[32,6,256]{2,1,0:T(8,128)S(1)} %all_gather.3.potential_ref, bf16[3,3,256,256]{3,2,1,0:T(8,128)(2,1)S(1)} %copy-done), custom_call_target="tpu_custom_call" | custom-call | tf_op jit(solution)/shard_map/pallas_call | solution.py:216
  94.9 23.0 %all_to_all.25.received_ref = bf16[32,48,256]{2,1,0:T(8,128)(2,1)S(1)} all-to-all(bf16[32,48,256]{2,1,0:T(8,128)(2,1)S(1)} %shard_map.51), channel_id=1, replica_groups=mesh['far'=4,'near'=4,'gy'=2] {'far','near','gy'}, dimensions={0} | all-to-all | bytes 1572864 | tf_op jit(solution)/shard_map/all_to_all | solution.py:385
  117.9 0.4 shard_map.52
  118.3 8.8 %all_to_all.26 = f32[8,24,256]{2,1,0:T(8,128)S(1)} all-to-all(f32[8,24,256]{2,1,0:T(8,128)S(1)} %bitcast.6), channel_id=1, replica_groups=mesh['far'=4,'near'=4,'gy'=2] {'near','gy'}, dimensions={0} | all-to-all | bytes 393216 | tf_op jit(solution)/shard_map/all_to_all | solution.py:365
  127.1 8.5 %all_to_all.27 = f32[4,24,256]{2,1,0:T(8,128)S(1)} all-to-all(f32[4,24,256]{2,1,0:T(8,128)S(1)} %broadcast_in_dim.4), channel_id=1, replica_groups=mesh['far'=4,'near'=4,'gy'=2] {'far'}, dimensions={0} | all-to-all | bytes 196608 | tf_op jit(solution)/shard_map/all_to_all | solution.py:368
  135.7 7.7 %all_to_all.28 = f32[8,24,256]{2,1,0:T(8,128)S(1)} all-to-all(f32[8,24,256]{2,1,0:T(8,128)S(1)} %broadcast_in_dim.5), channel_id=1, replica_groups=mesh['far'=4,'near'=4,'gy'=2] {'near','gy'}, dimensions={0} | all-to-all | bytes 393216 | tf_op jit(solution)/shard_map/all_to_all | solution.py:370
  143.4 11.0 %shard_map.53 = (bf16[1536,256]{1,0:T(8,128)(2,1)}, f32[256,256]{1,0:T(8,128)}) custom-call(f32[192,256]{1,0:T(8,128)S(1)} %bitcast.5, bf16[1536,256]{1,0:T(8,128)(2,1)S(1)} %get-tuple-element.7.rows_ref), custom_call_target="tpu_custom_call" | custom-call | tf_op jit(solution)/shard_map/pallas_call | solution.py:344
  (4 shorter events, 0.0 us)
Async XLA Ops:
  0.6 1.1 copy-start.1
  1.8 8.5 %copy-start.2 = (f32[6,8,32]{2,1,0:T(8,128)S(1)}, f32[6,8,32]{2,1,0:T(8,128)}, u32[]{:S(2)}) copy-start(f32[6,8,32]{2,1,0:T(8,128)} %param.4) | copy-start | bytes 18436
  2.9 83.7 %copy-start = (bf16[3,3,256,256]{3,2,1,0:T(8,128)(2,1)S(1)}, bf16[3,3,256,256]{3,2,1,0:T(8,128)(2,1)}, u32[]{:S(2)}) copy-start(bf16[3,3,256,256]{3,2,1,0:T(8,128)(2,1)} %constant.4.clone.weights_ref) | copy-start | bytes 3538948
  2.9 83.7 %all-to-all-start = ((bf16[32,48,256]{2,1,0:T(8,128)(2,1)}), bf16[32,48,256]{2,1,0:T(8,128)(2,1)S(1)}, u32[]{:S(2)}, u32[]{:S(2)}) async-start(bf16[32,48,256]{2,1,0:T(8,128)(2,1)} %shard_map.50), calls=%async_computation | async-start | bytes 1572864 | tf_op jit(solution)/shard_map/all_to_all | solution.py:382

commit v3 on v1

v3 whole, which is shorter than its diff:
```python
import functools
import math

import jax
import jax.numpy as jnp
import ml_dtypes
import numpy as np
from jax import lax
from jax.experimental import pallas as pl
from jax.experimental.pallas import tpu as pltpu
from jax.sharding import Mesh, PartitionSpec as P

DEG = 3


STENCIL_WEIGHTS = (
    -5369.0 / 1800.0,
    12.0 / 7.0,
    -15.0 / 56.0,
    10.0 / 189.0,
    -1.0 / 112.0,
    2.0 / 1925.0,
    -1.0 / 16632.0,
)
stencil_reach = 6
filter_center = 11.5
filter_half = 8.5
axes = ("far", "mid", "core", "gy")
owned = 2
group = 16
vmem_limit = 48 * 1024 * 1024

center_shift = -1.5 * STENCIL_WEIGHTS[0] - filter_center
side_weights = tuple(-0.5 * weight / filter_half for weight in STENCIL_WEIGHTS)


def bfloat16_parts(values):
    parts = []
    rest = np.asarray(values, np.float32)
    for _ in range(3):
        part = rest.astype(ml_dtypes.bfloat16)
        parts.append(part)
        rest = rest - part.astype(np.float32)
    return np.stack(parts)


def plane_weights(extent_y, extent_z):
    def band(extent, shift):
        matrix = np.zeros((extent, extent), np.float64)
        for source in range(extent):
            for target in range(extent):
                distance = abs(target - (source + shift))
                if 1 <= distance <= stencil_reach:
                    matrix[source, target] = side_weights[distance]
        return matrix

    eye_y, eye_z = np.eye(extent_y), np.eye(extent_z)
    own = np.kron(band(extent_y, 0), eye_z) + np.kron(eye_y, band(extent_z, 0))
    before = np.kron(band(extent_y, -extent_y), eye_z)
    after = np.kron(band(extent_y, extent_y), eye_z)
    return np.stack([bfloat16_parts(part) for part in (own, before, after)])


def level_rows(potential, rows):
    rest = (potential + center_shift) * (1.0 / filter_half)
    parts = []
    for _ in range(3):
        part = rest.astype(jnp.bfloat16).astype(jnp.float32)
        parts.append(part)
        rest = rest - part
    unused = jnp.zeros((rows - 3 * rest.shape[0], rest.shape[1]), jnp.float32)
    return jnp.concatenate(parts + [unused], axis=0).astype(jnp.bfloat16)


def level_room(layers):
    return -(-3 * layers // 16) * 16


def offsets(bricks_y):
    return [(i, j) for i in range(owned) for j in range(bricks_y)]


def ahead(mid, y, step, bricks_y):
    return lax.rem(mid + step[0], owned), lax.rem(y + step[1], bricks_y)


def behind(mid, y, step, bricks_y):
    return lax.rem(mid + step[0], owned), lax.rem(y - step[1] + bricks_y, bricks_y)


def exchange(messages, bricks_y):
    result = [messages[0]]
    for step, message in list(zip(offsets(bricks_y), messages))[1:]:
        perm = []
        for mid in range(owned):
            for y in range(bricks_y):
                target = (mid + step[0]) % owned * bricks_y + (y + step[1]) % bricks_y
                perm.append((mid * bricks_y + y, target))
        result.append(lax.ppermute(message, ("mid", "gy"), perm))
    return result


def split_kernel(bricks_y, cells_ref, potential_ref, *refs):
    sent_refs, block_ref = refs[:-1], refs[-1]
    mid, y = lax.axis_index("mid"), lax.axis_index("gy")
    columns, plane = block_ref.shape
    share = columns // len(sent_refs)
    layers = cells_ref.shape[0] // plane
    potential = jnp.concatenate(
        [potential_ref[:, at, :] for at in range(potential_ref.shape[1])], axis=1
    )
    extra = level_rows(potential, sent_refs[0].shape[0] - layers * share)
    for sent_ref in sent_refs:
        sent_ref[layers * share :, :] = extra
    for layer in range(layers):
        block = cells_ref[layer * plane : (layer + 1) * plane, :].astype(jnp.float32)
        block_ref[...] = block.T
        for step, sent_ref in zip(offsets(bricks_y), sent_refs):
            to_mid, to_y = ahead(mid, y, step, bricks_y)
            first = pl.multiple_of((to_mid * bricks_y + to_y) * share, share)
            own = block_ref[pl.ds(first, share), :]
            sent_ref[layer * share : (layer + 1) * share, :] = own.astype(jnp.bfloat16)


def split_columns(cells, potential, bricks_y):
    count, columns = cells.shape
    layers = potential.shape[0]
    plane = count // layers
    parts = owned * bricks_y
    message = jax.ShapeDtypeStruct(
        (layers * (columns // parts) + level_room(layers), plane), jnp.bfloat16
    )
    return pl.pallas_call(
        functools.partial(split_kernel, bricks_y),
        out_shape=[message] * parts,
        scratch_shapes=[pltpu.VMEM((columns, plane), jnp.float32)],
        compiler_params=pltpu.CompilerParams(vmem_limit_bytes=vmem_limit),
    )(cells, potential)


def place_kernel(bricks_y, *refs):
    parts = owned * bricks_y
    received_refs, (own_ref, level_ref, edge_ref) = refs[:parts], refs[parts:]
    mid, y = lax.axis_index("mid"), lax.axis_index("gy")
    rows = own_ref.shape[2]
    layers = level_ref.shape[2]
    for step, received_ref in zip(offsets(bricks_y), received_refs):
        at, b = behind(mid, y, step, bricks_y)
        own_ref[at, b] = received_ref[:rows]
        extra = received_ref[rows:].astype(jnp.float32)
        level = extra[:layers] + extra[layers : 2 * layers] + extra[2 * layers : 3 * layers]
        level_ref[at, b] = level
    edge_ref[...] = own_ref[lax.axis_index("core")]


def place(received, layers, bricks_y):
    plane = received[0].shape[1]
    rows = received[0].shape[0] - level_room(layers)
    return pl.pallas_call(
        functools.partial(place_kernel, bricks_y),
        out_shape=(
            jax.ShapeDtypeStruct((owned, bricks_y, rows, plane), jnp.bfloat16),
            jax.ShapeDtypeStruct((owned, bricks_y, layers, plane), jnp.float32),
            jax.ShapeDtypeStruct((bricks_y, rows, plane), jnp.bfloat16),
        ),
        compiler_params=pltpu.CompilerParams(vmem_limit_bytes=vmem_limit),
    )(*received)


def plane_kernel(own_ref, level_ref, weights_ref, partial_ref):
    _, bricks_y, rows, plane = own_ref.shape
    layers = level_ref.shape[2]
    share = rows // layers
    for b in range(bricks_y):
        fields, weights = [], []
        for kind, other in ((0, b), (1, b - 1), (2, b + 1)):
            if 0 <= other < bricks_y:
                for part in range(weights_ref.shape[1]):
                    fields.append(own_ref[:, other].reshape(owned * rows, plane))
                    weights.append(weights_ref[kind, part])
        sides = jnp.dot(
            jnp.concatenate(fields, axis=1),
            jnp.concatenate(weights, axis=0),
            preferred_element_type=jnp.float32,
        )
        for a in range(owned):
            for layer in range(layers):
                here = slice(layer * share, (layer + 1) * share)
                center = own_ref[a, b, here].astype(jnp.float32)
                level = jnp.broadcast_to(level_ref[a, b, layer : layer + 1, :], (share, plane))
                side = sides[a * rows + layer * share : a * rows + (layer + 1) * share]
                partial_ref[a, b, here] = side + level * center


def plane_part(own, level, weights):
    _, bricks_y, rows, plane = own.shape
    flops = 2 * owned * bricks_y * bricks_y * 3 * rows * plane * plane
    return pl.pallas_call(
        plane_kernel,
        out_shape=jax.ShapeDtypeStruct(own.shape, jnp.float32),
        cost_estimate=pl.CostEstimate(flops=flops, bytes_accessed=own.size * 6, transcendentals=0),
        compiler_params=pltpu.CompilerParams(vmem_limit_bytes=vmem_limit),
    )(own, level, weights)


def layer_kernel(stage, layers, partial_ref, own_ref, swapped_ref, edge_ref, *refs):
    if stage == 0:
        before_ref, (next_ref, next_edge_ref) = None, refs
    else:
        before_ref, refs = refs[0], refs[1:]
        if stage == DEG - 1:
            sent_refs, next_ref = refs[:-1], refs[-1]
        else:
            next_ref, next_edge_ref = refs
    core, mid, y = lax.axis_index("core"), lax.axis_index("mid"), lax.axis_index("gy")
    _, bricks_y, rows, plane = own_ref.shape
    share = rows // layers
    width = min(plane, 128)

    def chosen(first, second):
        return jnp.where(core == 0, first.astype(jnp.float32), second.astype(jnp.float32))

    for a in range(owned):
        for b in range(bricks_y):
            for column in range(0, share, group):
                for left in range(0, plane, width):
                    lane = slice(left, left + width)

                    def rows_of(layer):
                        return slice(layer * share + column, layer * share + column + group)

                    low, own, high = [], [], []
                    for layer in range(layers):
                        here = rows_of(layer)
                        own.append(own_ref[a, b, here, lane].astype(jnp.float32))
                        near = swapped_ref[core, b, here, lane].astype(jnp.float32)
                        if a == 0:
                            low.append(chosen(edge_ref[b, here, lane], swapped_ref[0, b, here, lane]))
                            high.append(near)
                        else:
                            low.append(near)
                            high.append(chosen(swapped_ref[1, b, here, lane], edge_ref[b, here, lane]))
                    window = low + own + high
                    for layer in range(layers):
                        here = rows_of(layer)
                        value = partial_ref[a, b, here, lane]
                        for distance in range(1, stencil_reach + 1):
                            pair = window[layers + layer - distance] + window[layers + layer + distance]
                            value = value + side_weights[distance] * pair
                        if stage > 0:
                            value = 2.0 * value - before_ref[a, b, here, lane].astype(jnp.float32)
                        next_ref[a, b, here, lane] = value.astype(jnp.bfloat16)
    if stage < DEG - 1:
        next_edge_ref[...] = next_ref[core]
    else:
        for step, sent_ref in zip(offsets(bricks_y), sent_refs):
            to_mid, to_y = ahead(mid, y, step, bricks_y)
            sent_ref[...] = next_ref[to_mid, to_y]


def layer_part(stage, layers, partial, own, swapped, edge, before):
    _, bricks_y, rows, plane = own.shape
    whole = jax.ShapeDtypeStruct(own.shape, jnp.bfloat16)
    one = jax.ShapeDtypeStruct((rows, plane), jnp.bfloat16)
    last = stage == DEG - 1
    return pl.pallas_call(
        functools.partial(layer_kernel, stage, layers),
        out_shape=[one] * (owned * bricks_y) if last else [whole, jax.ShapeDtypeStruct(edge.shape, jnp.bfloat16)],
        scratch_shapes=[pltpu.VMEM(own.shape, jnp.bfloat16)] if last else [],
        compiler_params=pltpu.CompilerParams(vmem_limit_bytes=vmem_limit),
    )(partial, own, swapped, edge, *([] if stage == 0 else [before]))


def neighbour_bricks(own, edge):
    count = lax.axis_size(("far", "core"))
    pairs = [(at, at + 1) for at in range(1, count - 1, 2)]
    edge = lax.ppermute(edge, ("far", "core"), pairs + [(b, a) for a, b in pairs])
    return lax.ppermute(own, "core", [(0, 1), (1, 0)]), edge


def chebyshev(own, level, edge, weights):
    layers = level.shape[2]
    before = None
    for stage in range(DEG):
        swapped, arrived = neighbour_bricks(own, edge)
        partial = plane_part(own, level, weights)
        result = layer_part(stage, layers, partial, own, swapped, arrived, before)
        if stage < DEG - 1:
            before, (own, edge) = own, result
    return result


def join_kernel(bricks_y, *refs):
    parts = owned * bricks_y
    received_refs, (cells_ref, gram_ref, block_ref) = refs[:parts], refs[parts:]
    mid, y = lax.axis_index("mid"), lax.axis_index("gy")
    columns, plane = block_ref.shape
    share = columns // parts
    layers = cells_ref.shape[0] // plane
    total = None
    for layer in range(layers):
        for step, received_ref in zip(offsets(bricks_y), received_refs):
            from_mid, from_y = behind(mid, y, step, bricks_y)
            first = pl.multiple_of((from_mid * bricks_y + from_y) * share, share)
            own = received_ref[layer * share : (layer + 1) * share, :]
            block_ref[pl.ds(first, share), :] = own.astype(jnp.float32)
        block = block_ref[...]
        cells_ref[layer * plane : (layer + 1) * plane, :] = block.T.astype(jnp.bfloat16)
        narrow = block.astype(jnp.bfloat16)
        part = lax.dot_general(
            narrow, narrow, (((1,), (1,)), ((), ())), preferred_element_type=jnp.float32
        )
        total = part if total is None else total + part
    half = columns // 2
    packed = jnp.concatenate([total[:half], total[half:, half:]], axis=1)
    piece = gram_ref.shape[1]
    for device in range(gram_ref.shape[0]):
        gram_ref[device] = packed[device * piece : (device + 1) * piece]


def join_columns(received, layers, bricks_y):
    rows, plane = received[0].shape
    columns = rows // layers * owned * bricks_y
    half = columns // 2
    shares = math.gcd(lax.axis_size(axes), half)
    return pl.pallas_call(
        functools.partial(join_kernel, bricks_y),
        out_shape=(
            jax.ShapeDtypeStruct((layers * plane, columns), jnp.bfloat16),
            jax.ShapeDtypeStruct((shares, half // shares, 3 * half), jnp.float32),
        ),
        scratch_shapes=[pltpu.VMEM((columns, plane), jnp.float32)],
        compiler_params=pltpu.CompilerParams(vmem_limit_bytes=vmem_limit),
    )(*received)


lanes = 128
panel_rows = 8
block_rows = 64


def row_splat(values, row):
    return jnp.broadcast_to(values[row : row + 1, :], values.shape)


def lane_splat(values, lane):
    return jnp.broadcast_to(values[:, lane : lane + 1], (panel_rows, lanes))


def panel_inverse(columns):
    row = lax.broadcasted_iota(jnp.int32, (panel_rows, lanes), 0)
    columns = list(columns)
    full = [jnp.where(row == k, 1.0, 0.0).astype(jnp.float32) for k in range(panel_rows)]
    forward = list(full)
    pivots = jnp.zeros((panel_rows, lanes), jnp.float32)
    for step in range(panel_rows):
        pivot = row_splat(columns[step], step)
        scale = 1.0 / pivot
        pivots = jnp.where(row == step, pivot, pivots)
        others = jnp.where(row == step, 0.0, columns[step])
        for k in range(step + 1, panel_rows):
            columns[k] = columns[k] - others * (row_splat(columns[k], step) * scale)
        for k in range(step):
            forward[k] = jnp.where(row == step, full[k], forward[k])
            full[k] = full[k] - others * (row_splat(full[k], step) * scale)
        full[step] = full[step] - others * scale
    inverse_pivots = 1.0 / pivots
    root = lax.rsqrt(pivots)
    full = [column * inverse_pivots for column in full]
    forward = [column * root for column in forward]
    return full, forward


def combine(columns, rows):
    width = rows.shape[1] // lanes
    parts = []
    for part in range(width):
        piece = rows[:, part * lanes : (part + 1) * lanes]
        total = None
        for k, column in enumerate(columns):
            term = column * row_splat(piece, k)
            total = term if total is None else total + term
        parts.append(total)
    return jnp.concatenate(parts, axis=1)


def factor_kernel(scale, gram_ref, rows_ref, rotated_ref, upper_ref, packed_ref, factor_ref, inverse_ref):
    shares, piece, width = gram_ref.shape
    half = shares * piece
    order = 2 * half
    for share in range(shares):
        packed_ref[share * piece : (share + 1) * piece, :] = gram_ref[share]
    factor_ref[...] = jnp.zeros((order, order), jnp.float32)
    inverse_ref[...] = jnp.zeros((order, order), jnp.float32)
    for start in range(0, order, block_rows):
        left = start // lanes * lanes
        right = left + lanes
        local = start - left
        row = lax.broadcasted_iota(jnp.int32, (block_rows, right), 0)
        col = lax.broadcasted_iota(jnp.int32, (block_rows, right), 1)
        unit = jnp.where(col == row + start, 1.0, 0.0).astype(jnp.float32)
        at, side = (start, 0) if start < half else (start - half, order)
        own = packed_ref[at : at + block_rows, side : side + order - left]
        block = jnp.concatenate([own, unit], axis=1)
        if start > 0:
            done = jnp.concatenate(
                [factor_ref[:start, left:order], inverse_ref[:start, :right]], axis=1
            )
            update = lax.dot_general(
                factor_ref[:start, left : left + lanes],
                done,
                (((0,), (0,)), ((), ())),
                precision=lax.Precision.HIGHEST,
                preferred_element_type=jnp.float32,
            )
            block = block - update[local : local + block_rows]
        groups = [
            block[g : g + panel_rows] for g in range(0, block_rows, panel_rows)
        ]
        for index in range(len(groups)):
            lane = local + index * panel_rows
            rows = groups[index]
            full, forward = panel_inverse([lane_splat(rows, lane + k) for k in range(panel_rows)])
            step_rows = combine(full, rows)
            for other in range(index + 1, len(groups)):
                target = groups[other]
                columns = [lane_splat(target, lane + k) for k in range(panel_rows)]
                groups[other] = target - combine(columns, step_rows)
            finished = combine(forward, rows)
            at = start + index * panel_rows
            factor_ref[at : at + panel_rows, left:order] = finished[:, : order - left]
            inverse_ref[at : at + panel_rows, :right] = finished[:, order - left :]
    row = lax.broadcasted_iota(jnp.int32, (order, order), 0)
    col = lax.broadcasted_iota(jnp.int32, (order, order), 1)
    upper_ref[...] = jnp.where(col >= row, factor_ref[...] * (1.0 / scale), 0.0)
    inverse = jnp.where(col <= row, inverse_ref[...] * scale, 0.0)
    high = inverse.astype(jnp.bfloat16)
    rest = inverse - high.astype(jnp.float32)
    middle = rest.astype(jnp.bfloat16)
    low = (rest - middle.astype(jnp.float32)).astype(jnp.bfloat16)
    count = rows_ref.shape[0]
    chunk = math.gcd(count, 512)
    for at in range(0, count, chunk):
        piece = rows_ref[at : at + chunk, :]
        total = jnp.zeros((chunk, order), jnp.float32)
        for part in (low, middle, high):
            total = total + lax.dot_general(
                piece, part, (((1,), (1,)), ((), ())), preferred_element_type=jnp.float32
            )
        rotated_ref[at : at + chunk, :] = total.astype(jnp.bfloat16)


def factor_and_rotate(gram_matrix, rows, total_cells):
    order = rows.shape[1]
    count = rows.shape[0]
    return pl.pallas_call(
        functools.partial(factor_kernel, math.sqrt(total_cells)),
        out_shape=(
            jax.ShapeDtypeStruct((count, order), jnp.bfloat16),
            jax.ShapeDtypeStruct((order, order), jnp.float32),
        ),
        scratch_shapes=[
            pltpu.VMEM((order // 2, order // 2 * 3), jnp.float32),
            pltpu.VMEM((order, order), jnp.float32),
            pltpu.VMEM((order, order), jnp.float32),
        ],
        compiler_params=pltpu.CompilerParams(vmem_limit_bytes=vmem_limit),
    )(gram_matrix, rows)


def sum_over_devices(values):
    if lax.axis_size(axes) != values.shape[0]:
        return lax.psum(values, axes)
    total = jnp.sum(lax.all_to_all(values, axes, 0, 0), axis=0)
    return lax.all_to_all(jnp.broadcast_to(total[None], values.shape), axes, 0, 0)


def shards(trial_orbitals, potential):
    layers, extent_y, extent_z, columns = trial_orbitals.shape
    bricks_y = lax.axis_size("gy")
    total_cells = lax.axis_size(axes) * layers * extent_y * extent_z
    weights = jnp.asarray(plane_weights(extent_y, extent_z))

    cells = trial_orbitals.reshape(layers * extent_y * extent_z, columns)
    sent = split_columns(cells, potential, bricks_y)
    own, level, edge = place(exchange(sent, bricks_y), layers, bricks_y)
    sent = chebyshev(own, level, edge, weights)
    rows, local_gram = join_columns(exchange(sent, bricks_y), layers, bricks_y)
    gram_matrix = sum_over_devices(local_gram)
    rotated, upper_factor = factor_and_rotate(gram_matrix, rows, total_cells)
    return (rotated.reshape(trial_orbitals.shape), upper_factor)


def solution(mesh):
    bricks_x, bricks_y = mesh.devices.shape
    cut = Mesh(mesh.devices.reshape(bricks_x // 4, owned, 2, bricks_y), axes)
    cells = P(("far", "mid", "core"), "gy")
    return jax.shard_map(
        shards,
        mesh=cut,
        in_specs=(cells, cells),
        out_specs=(cells, P()),
        check_vma=False,
    )
```

time: 114 us -> 99.9 us (0.88)
  blocking collectives: 73.7 us -> 35.8 us
  starting transfers between devices: 7.3 us -> 24.8 us
  waiting for transfers between devices: 10.4 us -> 15.9 us
    all_to_all x4 -> x2, blocking collectives: 73.7 us -> 35.8 us  [the longest x1 24.4 us: sum_over_devices(): total = jnp.sum(lax.all_to_all(values, axes, 0, 0), axis=0)]
    ppermute x0 -> x12, starting transfers between devices: none -> 24.8 us  [the longest x3 14.6 us: neighbour_bricks(): return (lax.ppermute(own, 'core', [(0, 1), (1, 0)]), edge)]
    ppermute x0 -> x12, waiting for transfers between devices: none -> 15.9 us  [the longest x6 15.7 us: exchange(): result.append(lax.ppermute(message, ('mid', 'gy'), perm))]
    all_to_all x1 -> x0, waiting for transfers between devices: 10.4 us -> none  [shards(): levels = lax.all_to_all(levels, axes, 0, 0)]
    all_to_all x1 -> x0, starting transfers between devices: 7.3 us -> none  [shards(): levels = lax.all_to_all(levels, axes, 0, 0)]
    unnamed x4 -> x6, local copies, waits for them, and re-layouts: 0.01 us -> 1.87 us
    broadcast_in_dim x3 -> x1, local copies, waits for them, and re-layouts: 1.63 us -> 0.03 us  [sum_over_devices(): jnp.broadcast_to(total[None], values.shape)]
    pallas_call x3 -> x9, Pallas kernels: 8.9 us -> 9.44 us  [the longest x3 4.13 us: plane_part(): pl.pallas_call(plane_kernel, out_shape=jax.ShapeDtypeStruct(own.shape, jn...]
  transfers between devices with their start and end apart: 1 -> 12, of which waited for: 1 -> 7; matrix products, arithmetic and copies ran while one was open for 0% -> 0% of each run, Pallas kernels for 0% -> 4%
where the time goes in v3:
time: 99.9 us; the launch traced here: 99.7 us
  blocking collectives  35.8 us (36%)
  starting transfers between devices  24.8 us (25%)
  Pallas kernels  20.4 us (20%)
  waiting for transfers between devices  15.9 us (16%)
  local copies, waits for them, and re-layouts  1.9 us (2%)
    all_to_all x1, blocking collectives, sum_over_devices(): total = jnp.sum(lax.all_to_all(values, axes, 0, 0), axis=0)  24.4 us
    ppermute x6, waiting for transfers between devices, exchange(): result.append(lax.ppermute(message, ('mid', 'gy'), perm))  15.7 us
    ppermute x3, starting transfers between devices, neighbour_bricks(): return (lax.ppermute(own, 'core', [(0, 1), (1, 0)]), edge)  14.6 us
    all_to_all x1, blocking collectives, sum_over_devices(): lax.all_to_all(jnp.broadcast_to(total[None], values.shape), axes, 0, 0)  11.4 us
    pallas_call x1, Pallas kernels, factor_and_rotate(): pl.pallas_call(functools.partial(factor_kernel, math.sqrt(total_cells)),...  11 us
    ppermute x6, starting transfers between devices, exchange(): result.append(lax.ppermute(message, ('mid', 'gy'), perm))  8.13 us
    pallas_call x3, Pallas kernels, plane_part(): pl.pallas_call(plane_kernel, out_shape=jax.ShapeDtypeStruct(own.shape, jn...  4.13 us
    pallas_call x3, Pallas kernels, layer_part(): pl.pallas_call(functools.partial(layer_kernel, stage, layers), out_shape=...  4.07 us
  transfers between devices with their start and end apart: 12, of which 7 were waited for; matrix products, arithmetic and copies ran while one was open for 0% of the time, Pallas kernels for 4%

profile of v3, /device:TPU:0, one launch (start us, length us, event | category | flops | bytes accessed | tf_op | source)
XLA Modules:
  0.0 99.7 jit_solution(2450298924441649652)
XLA Ops:
  0.6 0.0 copy-start
  0.6 1.1 %copy-done = bf16[6,8,32,256]{3,2,1,0:T(8,128)(2,1)S(1)} copy-done((bf16[6,8,32,256]{3,2,1,0:T(8,128)(2,1)S(1)}, bf16[6,8,32,256]{3,2,1,0:T(8,128)(2,1)}, u32[]{:S(2)}) %copy-start) | copy-done | bytes 786456
  1.8 0.0 copy-start.1
  1.8 0.7 copy-done.1
  2.5 0.0 copy-start.2
  2.5 0.5 shard_map.50
  3.0 3.0 %collective-permute-start = (bf16[416,256]{1,0:T(8,128)(2,1)S(1)}, bf16[416,256]{1,0:T(8,128)(2,1)S(1)}, u32[]{:S(2)}, u32[]{:S(2)}) collective-permute-start(bf16[416,256]{1,0:T(8,128)(2,1)S(1)} %get-tuple-element.22), channel_id=1, source_target_pairs={{0,1},{1,0},{4,5},{5,4},{2,3},{3,2},{6,7},{7,6},{8,9},{9,8},{12,13... | collective-permute-start | bytes 638984 | tf_op jit(solution)/shard_map/ppermute | solution.py:99
  6.1 1.5 %collective-permute-start.1 = (bf16[416,256]{1,0:T(8,128)(2,1)S(1)}, bf16[416,256]{1,0:T(8,128)(2,1)S(1)}, u32[]{:S(2)}, u32[]{:S(2)}) collective-permute-start(bf16[416,256]{1,0:T(8,128)(2,1)S(1)} %get-tuple-element.23), channel_id=1, source_target_pairs={{0,4},{1,5},{4,0},{5,1},{2,6},{3,7},{6,2},{7,3},{8,12},{9,13},{12,... | collective-permute-start | bytes 638984 | tf_op jit(solution)/shard_map/ppermute | solution.py:99
  7.5 0.0 collective-permute-start.2
  7.6 3.7 %collective-permute-done.refs_1_ = bf16[416,256]{1,0:T(8,128)(2,1)S(1)} collective-permute-done((bf16[416,256]{1,0:T(8,128)(2,1)S(1)}, bf16[416,256]{1,0:T(8,128)(2,1)S(1)}, u32[]{:S(2)}, u32[]{:S(2)}) %collective-permute-start) | collective-permute-done | bytes 213024 | tf_op jit(solution)/shard_map/ppermute | solution.py:99
  11.3 2.9 %collective-permute-done.1.refs_2_ = bf16[416,256]{1,0:T(8,128)(2,1)S(1)} collective-permute-done((bf16[416,256]{1,0:T(8,128)(2,1)S(1)}, bf16[416,256]{1,0:T(8,128)(2,1)S(1)}, u32[]{:S(2)}, u32[]{:S(2)}) %collective-permute-start.1) | collective-permute-done | bytes 213024 | tf_op jit(solution)/shard_map/ppermute | solution.py:99
  14.2 2.9 %collective-permute-done.2.refs_3_ = bf16[416,256]{1,0:T(8,128)(2,1)S(1)} collective-permute-done((bf16[416,256]{1,0:T(8,128)(2,1)S(1)}, bf16[416,256]{1,0:T(8,128)(2,1)S(1)}, u32[]{:S(2)}, u32[]{:S(2)}) %collective-permute-start.2) | collective-permute-done | bytes 213024 | tf_op jit(solution)/shard_map/ppermute | solution.py:99
  17.1 0.1 shard_map.51
  17.2 0.1 collective-permute-start.3
  17.3 0.7 collective-permute-start.4
  18.0 0.0 copy-done.2
  18.0 1.4 %shard_map.52.partial_ref = f32[2,2,384,256]{3,2,1,0:T(8,128)S(1)} custom-call(bf16[2,2,384,256]{3,2,1,0:T(8,128)(2,1)S(1)} %get-tuple-element.25.own_ref.refs_0_, f32[2,2,6,256]{3,2,1,0:T(8,128)S(1)} %get-tuple-element.26.level_ref, bf16[3,3,256,256]{3,2,1,0:T(8,128)(2,1)S(1)} %copy-done.2), custom_call_target="tpu_custom_call" | custom-call | flops 1207959552 | bytes 2359296 | tf_op jit(solution)/shard_map/pallas_call | solution.py:198
  19.4 0.0 collective-permute-done.4.edge_ref
  19.4 0.2 collective-permute-done.3.swapped_ref
  19.6 1.2 %shard_map.53 = (bf16[2,2,384,256]{3,2,1,0:T(8,128)(2,1)S(1)}, bf16[2,384,256]{2,1,0:T(8,128)(2,1)S(1)}) custom-call(f32[2,2,384,256]{3,2,1,0:T(8,128)S(1)} %shard_map.52.partial_ref, bf16[2,2,384,256]{3,2,1,0:T(8,128)(2,1)S(1)} %get-tuple-element.25.own_ref.refs_0_, bf16[2,2,384,256]{3,2,1,0:T(8,128)(2,1)S(1)} %collective-permute-done.3.swapped_ref, ...), custom_call_target="tpu_custom_call" | custom-call | tf_op jit(solution)/shard_map/pallas_call | solution.py:266
  20.8 7.4 %collective-permute-start.5 = (bf16[2,2,384,256]{3,2,1,0:T(8,128)(2,1)S(1)}, bf16[2,2,384,256]{3,2,1,0:T(8,128)(2,1)S(1)}, u32[]{:S(2)}, u32[]{:S(2)}) collective-permute-start(bf16[2,2,384,256]{3,2,1,0:T(8,128)(2,1)S(1)} %get-tuple-element.28.own_ref.refs_0_), channel_id=1, source_target_pairs={{0,2},{2,0},{1,3},{3,1},{4,6},{6,4},{5,7},{7,5},{8,10},{10,8},{9,1... | collective-permute-start | bytes 2359304 | tf_op jit(solution)/shard_map/ppermute | solution.py:278
  28.2 0.7 collective-permute-start.6
  28.9 1.4 %shard_map.54.partial_ref = f32[2,2,384,256]{3,2,1,0:T(8,128)S(1)} custom-call(bf16[2,2,384,256]{3,2,1,0:T(8,128)(2,1)S(1)} %get-tuple-element.28.own_ref.refs_0_, f32[2,2,6,256]{3,2,1,0:T(8,128)S(1)} %get-tuple-element.26.level_ref, bf16[3,3,256,256]{3,2,1,0:T(8,128)(2,1)S(1)} %copy-done.2), custom_call_target="tpu_custom_call" | custom-call | flops 1207959552 | bytes 2359296 | tf_op jit(solution)/shard_map/pallas_call | solution.py:198
  30.3 0.0 collective-permute-done.6.edge_ref
  30.3 0.0 collective-permute-done.5.swapped_ref
  30.3 1.4 %shard_map.55 = (bf16[2,2,384,256]{3,2,1,0:T(8,128)(2,1)S(1)}, bf16[2,384,256]{2,1,0:T(8,128)(2,1)S(1)}) custom-call(f32[2,2,384,256]{3,2,1,0:T(8,128)S(1)} %shard_map.54.partial_ref, bf16[2,2,384,256]{3,2,1,0:T(8,128)(2,1)S(1)} %get-tuple-element.28.own_ref.refs_0_, bf16[2,2,384,256]{3,2,1,0:T(8,128)(2,1)S(1)} %collective-permute-done.5.swapped_ref, ...), custom_call_target="tpu_custom_call" | custom-call | tf_op jit(solution)/shard_map/pallas_call | solution.py:266
  31.7 7.2 %collective-permute-start.7 = (bf16[2,2,384,256]{3,2,1,0:T(8,128)(2,1)S(1)}, bf16[2,2,384,256]{3,2,1,0:T(8,128)(2,1)S(1)}, u32[]{:S(2)}, u32[]{:S(2)}) collective-permute-start(bf16[2,2,384,256]{3,2,1,0:T(8,128)(2,1)S(1)} %get-tuple-element.30.own_ref), channel_id=1, source_target_pairs={{0,2},{2,0},{1,3},{3,1},{4,6},{6,4},{5,7},{7,5},{8,10},{10,8},{9,1... | collective-permute-start | bytes 2359304 | tf_op jit(solution)/shard_map/ppermute | solution.py:278
  38.9 0.7 collective-permute-start.8
  39.6 1.4 %shard_map.56.partial_ref = f32[2,2,384,256]{3,2,1,0:T(8,128)S(1)} custom-call(bf16[2,2,384,256]{3,2,1,0:T(8,128)(2,1)S(1)} %get-tuple-element.30.own_ref, f32[2,2,6,256]{3,2,1,0:T(8,128)S(1)} %get-tuple-element.26.level_ref, bf16[3,3,256,256]{3,2,1,0:T(8,128)(2,1)S(1)} %copy-done.2), custom_call_target="tpu_custom_call" | custom-call | flops 1207959552 | bytes 2359296 | tf_op jit(solution)/shard_map/pallas_call | solution.py:198
  40.9 0.0 collective-permute-done.8.edge_ref
  41.0 0.0 collective-permute-done.7.swapped_ref
  41.0 1.4 %shard_map.57 = (bf16[384,256]{1,0:T(8,128)(2,1)S(1)}, bf16[384,256]{1,0:T(8,128)(2,1)S(1)}, bf16[384,256]{1,0:T(8,128)(2,1)S(1)}, bf16[384,256]{1,0:T(8,128)(2,1)S(1)}) custom-call(f32[2,2,384,256]{3,2,1,0:T(8,128)S(1)} %shard_map.56.partial_ref, bf16[2,2,384,256]{3,2,1,0:T(8,128)(2,1)S(1)} %get-tuple-element.30.own_ref, ...), custom_call_target="tpu_custom_call" | custom-call | tf_op jit(solution)/shard_map/pallas_call | solution.py:266
  42.4 1.7 %collective-permute-start.9 = (bf16[384,256]{1,0:T(8,128)(2,1)S(1)}, bf16[384,256]{1,0:T(8,128)(2,1)S(1)}, u32[]{:S(2)}, u32[]{:S(2)}) collective-permute-start(bf16[384,256]{1,0:T(8,128)(2,1)S(1)} %get-tuple-element.33), channel_id=1, source_target_pairs={{0,1},{1,0},{4,5},{5,4},{2,3},{3,2},{6,7},{7,6},{8,9},{9,8},{12,13... | collective-permute-start | bytes 589832 | tf_op jit(solution)/shard_map/ppermute | solution.py:99
  44.0 1.5 %collective-permute-start.10 = (bf16[384,256]{1,0:T(8,128)(2,1)S(1)}, bf16[384,256]{1,0:T(8,128)(2,1)S(1)}, u32[]{:S(2)}, u32[]{:S(2)}) collective-permute-start(bf16[384,256]{1,0:T(8,128)(2,1)S(1)} %get-tuple-element.34), channel_id=1, source_target_pairs={{0,4},{1,5},{4,0},{5,1},{2,6},{3,7},{6,2},{7,3},{8,12},{9,13},{12,... | collective-permute-start | bytes 589832 | tf_op jit(solution)/shard_map/ppermute | solution.py:99
  45.5 0.4 collective-permute-start.11
  45.9 2.2 %collective-permute-done.9.refs_1_ = bf16[384,256]{1,0:T(8,128)(2,1)S(1)} collective-permute-done((bf16[384,256]{1,0:T(8,128)(2,1)S(1)}, bf16[384,256]{1,0:T(8,128)(2,1)S(1)}, u32[]{:S(2)}, u32[]{:S(2)}) %collective-permute-start.9) | collective-permute-done | bytes 196640 | tf_op jit(solution)/shard_map/ppermute | solution.py:99
  48.1 1.6 %collective-permute-done.10.refs_2_ = bf16[384,256]{1,0:T(8,128)(2,1)S(1)} collective-permute-done((bf16[384,256]{1,0:T(8,128)(2,1)S(1)}, bf16[384,256]{1,0:T(8,128)(2,1)S(1)}, u32[]{:S(2)}, u32[]{:S(2)}) %collective-permute-start.10) | collective-permute-done | bytes 196640 | tf_op jit(solution)/shard_map/ppermute | solution.py:99
  49.7 2.4 %collective-permute-done.11.refs_3_ = bf16[384,256]{1,0:T(8,128)(2,1)S(1)} collective-permute-done((bf16[384,256]{1,0:T(8,128)(2,1)S(1)}, bf16[384,256]{1,0:T(8,128)(2,1)S(1)}, u32[]{:S(2)}, u32[]{:S(2)}) %collective-permute-start.11) | collective-permute-done | bytes 196640 | tf_op jit(solution)/shard_map/ppermute | solution.py:99
  52.1 0.6 shard_map.58
  52.7 24.4 %all_to_all.10 = f32[32,4,384]{2,1,0:T(4,128)S(1)} all-to-all(f32[32,4,384]{2,1,0:T(4,128)S(1)} %get-tuple-element.36), channel_id=1, replica_groups=mesh['far'=4,'mid'=2,'core'=2,'gy'=2] {'far','mid','core','gy'}, dimensions={0} | all-to-all | bytes 393216 | tf_op jit(solution)/shard_map/all_to_all | solution.py:474
  77.2 0.1 reduce_sum.9
  77.2 11.4 %all_to_all.11.gram_ref = f32[32,4,384]{2,1,0:T(4,128)S(1)} all-to-all(f32[32,4,384]{2,1,0:T(4,128)S(1)} %broadcast_in_dim.2), channel_id=1, replica_groups=mesh['far'=4,'mid'=2,'core'=2,'gy'=2] {'far','mid','core','gy'}, dimensions={0} | all-to-all | bytes 393216 | tf_op jit(solution)/shard_map/all_to_all | solution.py:475
  88.7 11.0 %shard_map.59 = (bf16[1536,256]{1,0:T(8,128)(2,1)}, f32[256,256]{1,0:T(8,128)}) custom-call(f32[32,4,384]{2,1,0:T(4,128)S(1)} %all_to_all.11.gram_ref, bf16[1536,256]{1,0:T(8,128)(2,1)S(1)} %get-tuple-element.37.rows_ref), custom_call_target="tpu_custom_call" | custom-call | tf_op jit(solution)/shard_map/pallas_call | solution.py:456
  (1 shorter events, 0.0 us)
Async XLA Ops:
  0.6 1.1 %copy-start = (bf16[6,8,32,256]{3,2,1,0:T(8,128)(2,1)S(1)}, bf16[6,8,32,256]{3,2,1,0:T(8,128)(2,1)}, u32[]{:S(2)}) copy-start(bf16[6,8,32,256]{3,2,1,0:T(8,128)(2,1)} %param.3) | copy-start | bytes 2359300
  1.8 0.7 copy-start.1
  2.5 15.5 %copy-start.2 = (bf16[3,3,256,256]{3,2,1,0:T(8,128)(2,1)S(1)}, bf16[3,3,256,256]{3,2,1,0:T(8,128)(2,1)}, u32[]{:S(2)}) copy-start(bf16[3,3,256,256]{3,2,1,0:T(8,128)(2,1)} %constant.4.clone.weights_ref) | copy-start | bytes 3538948
  3.0 8.3 %collective-permute-start = (bf16[416,256]{1,0:T(8,128)(2,1)S(1)}, bf16[416,256]{1,0:T(8,128)(2,1)S(1)}, u32[]{:S(2)}, u32[]{:S(2)}) collective-permute-start(bf16[416,256]{1,0:T(8,128)(2,1)S(1)} %get-tuple-element.22), channel_id=1, source_target_pairs={{0,1},{1,0},{4,5},{5,4},{2,3},{3,2},{6,7},{7,6},{8,9},{9,8},{12,13... | collective-permute-start | bytes 638984 | tf_op jit(solution)/shard_map/ppermute | solution.py:99
  6.1 8.2 %collective-permute-start.1 = (bf16[416,256]{1,0:T(8,128)(2,1)S(1)}, bf16[416,256]{1,0:T(8,128)(2,1)S(1)}, u32[]{:S(2)}, u32[]{:S(2)}) collective-permute-start(bf16[416,256]{1,0:T(8,128)(2,1)S(1)} %get-tuple-element.23), channel_id=1, source_target_pairs={{0,4},{1,5},{4,0},{5,1},{2,6},{3,7},{6,2},{7,3},{8,12},{9,13},{12,... | collective-permute-start | bytes 638984 | tf_op jit(solution)/shard_map/ppermute | solution.py:99
  7.5 9.6 %collective-permute-start.2 = (bf16[416,256]{1,0:T(8,128)(2,1)S(1)}, bf16[416,256]{1,0:T(8,128)(2,1)S(1)}, u32[]{:S(2)}, u32[]{:S(2)}) collective-permute-start(bf16[416,256]{1,0:T(8,128)(2,1)S(1)} %get-tuple-element.24), channel_id=1, source_target_pairs={{0,5},{1,4},{4,1},{5,0},{2,7},{3,6},{6,3},{7,2},{8,13},{9,12},{12,... | collective-permute-start | bytes 638984 | tf_op jit(solution)/shard_map/ppermute | solution.py:99
  17.2 2.4 %collective-permute-start.3 = (bf16[2,2,384,256]{3,2,1,0:T(8,128)(2,1)S(1)}, bf16[2,2,384,256]{3,2,1,0:T(8,128)(2,1)S(1)}, u32[]{:S(2)}, u32[]{:S(2)}) collective-permute-start(bf16[2,2,384,256]{3,2,1,0:T(8,128)(2,1)S(1)} %get-tuple-element.25.own_ref.refs_0_), channel_id=1, source_target_pairs={{0,2},{2,0},{1,3},{3,1},{4,6},{6,4},{5,7},{7,5},{8,10},{10,8},{9,1... | collective-permute-start | bytes 2359304 | tf_op jit(solution)/shard_map/ppermute | solution.py:278
  17.3 2.1 %collective-permute-start.4 = (bf16[2,384,256]{2,1,0:T(8,128)(2,1)S(1)}, bf16[2,384,256]{2,1,0:T(8,128)(2,1)S(1)}, u32[]{:S(2)}, u32[]{:S(2)}) collective-permute-start(bf16[2,384,256]{2,1,0:T(8,128)(2,1)S(1)} %get-tuple-element.27), channel_id=1, source_target_pairs={{2,8},{10,16},{18,24},{8,2},{16,10},{24,18},{3,9},{11,17},{19,25},... | collective-permute-start | bytes 1179656 | tf_op jit(solution)/shard_map/ppermute | solution.py:277
  20.8 9.5 %collective-permute-start.5 = (bf16[2,2,384,256]{3,2,1,0:T(8,128)(2,1)S(1)}, bf16[2,2,384,256]{3,2,1,0:T(8,128)(2,1)S(1)}, u32[]{:S(2)}, u32[]{:S(2)}) collective-permute-start(bf16[2,2,384,256]{3,2,1,0:T(8,128)(2,1)S(1)} %get-tuple-element.28.own_ref.refs_0_), channel_id=1, source_target_pairs={{0,2},{2,0},{1,3},{3,1},{4,6},{6,4},{5,7},{7,5},{8,10},{10,8},{9,1... | collective-permute-start | bytes 2359304 | tf_op jit(solution)/shard_map/ppermute | solution.py:278
  28.2 2.1 %collective-permute-start.6 = (bf16[2,384,256]{2,1,0:T(8,128)(2,1)S(1)}, bf16[2,384,256]{2,1,0:T(8,128)(2,1)S(1)}, u32[]{:S(2)}, u32[]{:S(2)}) collective-permute-start(bf16[2,384,256]{2,1,0:T(8,128)(2,1)S(1)} %get-tuple-element.29), channel_id=1, source_target_pairs={{2,8},{10,16},{18,24},{8,2},{16,10},{24,18},{3,9},{11,17},{19,25},... | collective-permute-start | bytes 1179656 | tf_op jit(solution)/shard_map/ppermute | solution.py:277
  31.7 9.3 %collective-permute-start.7 = (bf16[2,2,384,256]{3,2,1,0:T(8,128)(2,1)S(1)}, bf16[2,2,384,256]{3,2,1,0:T(8,128)(2,1)S(1)}, u32[]{:S(2)}, u32[]{:S(2)}) collective-permute-start(bf16[2,2,384,256]{3,2,1,0:T(8,128)(2,1)S(1)} %get-tuple-element.30.own_ref), channel_id=1, source_target_pairs={{0,2},{2,0},{1,3},{3,1},{4,6},{6,4},{5,7},{7,5},{8,10},{10,8},{9,1... | collective-permute-start | bytes 2359304 | tf_op jit(solution)/shard_map/ppermute | solution.py:278
  38.9 2.1 %collective-permute-start.8 = (bf16[2,384,256]{2,1,0:T(8,128)(2,1)S(1)}, bf16[2,384,256]{2,1,0:T(8,128)(2,1)S(1)}, u32[]{:S(2)}, u32[]{:S(2)}) collective-permute-start(bf16[2,384,256]{2,1,0:T(8,128)(2,1)S(1)} %get-tuple-element.31), channel_id=1, source_target_pairs={{2,8},{10,16},{18,24},{8,2},{16,10},{24,18},{3,9},{11,17},{19,25},... | collective-permute-start | bytes 1179656 | tf_op jit(solution)/shard_map/ppermute | solution.py:277
  42.4 5.7 %collective-permute-start.9 = (bf16[384,256]{1,0:T(8,128)(2,1)S(1)}, bf16[384,256]{1,0:T(8,128)(2,1)S(1)}, u32[]{:S(2)}, u32[]{:S(2)}) collective-permute-start(bf16[384,256]{1,0:T(8,128)(2,1)S(1)} %get-tuple-element.33), channel_id=1, source_target_pairs={{0,1},{1,0},{4,5},{5,4},{2,3},{3,2},{6,7},{7,6},{8,9},{9,8},{12,13... | collective-permute-start | bytes 589832 | tf_op jit(solution)/shard_map/ppermute | solution.py:99
  44.0 5.7 %collective-permute-start.10 = (bf16[384,256]{1,0:T(8,128)(2,1)S(1)}, bf16[384,256]{1,0:T(8,128)(2,1)S(1)}, u32[]{:S(2)}, u32[]{:S(2)}) collective-permute-start(bf16[384,256]{1,0:T(8,128)(2,1)S(1)} %get-tuple-element.34), channel_id=1, source_target_pairs={{0,4},{1,5},{4,0},{5,1},{2,6},{3,7},{6,2},{7,3},{8,12},{9,13},{12,... | collective-permute-start | bytes 589832 | tf_op jit(solution)/shard_map/ppermute | solution.py:99
  45.5 6.6 %collective-permute-start.11 = (bf16[384,256]{1,0:T(8,128)(2,1)S(1)}, bf16[384,256]{1,0:T(8,128)(2,1)S(1)}, u32[]{:S(2)}, u32[]{:S(2)}) collective-permute-start(bf16[384,256]{1,0:T(8,128)(2,1)S(1)} %get-tuple-element.35), channel_id=1, source_target_pairs={{0,5},{1,4},{4,1},{5,0},{2,7},{3,6},{6,3},{7,2},{8,13},{9,12},{12,... | collective-permute-start | bytes 589832 | tf_op jit(solution)/shard_map/ppermute | solution.py:99

commit v4 on v3

--- a/solution.py
+++ b/solution.py
@@ -29,6 +29,7 @@
 owned = 2
 group = 16
 vmem_limit = 48 * 1024 * 1024
+fetching_limit = 63 * 1024 * 1024
 
 center_shift = -1.5 * STENCIL_WEIGHTS[0] - filter_center
 side_weights = tuple(-0.5 * weight / filter_half for weight in STENCIL_WEIGHTS)
@@ -101,19 +102,29 @@
 
 
 def split_kernel(bricks_y, cells_ref, potential_ref, *refs):
-    sent_refs, block_ref = refs[:-1], refs[-1]
+    sent_refs, (block_ref, fetched_ref, level_ref, arrived) = refs[:-4], refs[-4:]
     mid, y = lax.axis_index("mid"), lax.axis_index("gy")
     columns, plane = block_ref.shape
     share = columns // len(sent_refs)
     layers = cells_ref.shape[0] // plane
+    fetches = [pltpu.make_async_copy(potential_ref, level_ref, arrived.at[layers])]
+    for layer in range(layers):
+        part = pl.ds(layer * plane, plane)
+        fetches.append(
+            pltpu.make_async_copy(cells_ref.at[part], fetched_ref.at[part], arrived.at[layer])
+        )
+    for fetch in fetches:
+        fetch.start()
+    fetches[0].wait()
     potential = jnp.concatenate(
-        [potential_ref[:, at, :] for at in range(potential_ref.shape[1])], axis=1
+        [level_ref[:, at, :] for at in range(level_ref.shape[1])], axis=1
     )
     extra = level_rows(potential, sent_refs[0].shape[0] - layers * share)
     for sent_ref in sent_refs:
         sent_ref[layers * share :, :] = extra
     for layer in range(layers):
-        block = cells_ref[layer * plane : (layer + 1) * plane, :].astype(jnp.float32)
+        fetches[layer + 1].wait()
+        block = fetched_ref[layer * plane : (layer + 1) * plane, :].astype(jnp.float32)
         block_ref[...] = block.T
         for step, sent_ref in zip(offsets(bricks_y), sent_refs):
             to_mid, to_y = ahead(mid, y, step, bricks_y)
@@ -132,16 +143,23 @@
     )
     return pl.pallas_call(
         functools.partial(split_kernel, bricks_y),
+        in_specs=[pl.BlockSpec(memory_space=pltpu.HBM)] * 2,
         out_shape=[message] * parts,
-        scratch_shapes=[pltpu.VMEM((columns, plane), jnp.float32)],
-        compiler_params=pltpu.CompilerParams(vmem_limit_bytes=vmem_limit),
+        scratch_shapes=[
+            pltpu.VMEM((columns, plane), jnp.float32),
+            pltpu.VMEM((count, columns), jnp.bfloat16),
+            pltpu.VMEM(potential.shape, jnp.float32),
+            pltpu.SemaphoreType.DMA((layers + 1,)),
+        ],
+        compiler_params=pltpu.CompilerParams(vmem_limit_bytes=fetching_limit),
     )(cells, potential)
 
 
 def place_kernel(bricks_y, *refs):
     parts = owned * bricks_y
-    received_refs, (own_ref, level_ref, edge_ref) = refs[:parts], refs[parts:]
-    mid, y = lax.axis_index("mid"), lax.axis_index("gy")
+    received_refs, results = refs[:parts], refs[parts:]
+    edge_ref, inner_ref, edge_level_ref, inner_level_ref, own_ref, level_ref = results
+    mid, y, core = lax.axis_index("mid"), lax.axis_index("gy"), lax.axis_index("core")
     rows = own_ref.shape[2]
     layers = level_ref.shape[2]
     for step, received_ref in zip(offsets(bricks_y), received_refs):
@@ -150,51 +168,54 @@
         extra = received_ref[rows:].astype(jnp.float32)
         level = extra[:layers] + extra[layers : 2 * layers] + extra[2 * layers : 3 * layers]
         level_ref[at, b] = level
-    edge_ref[...] = own_ref[lax.axis_index("core")]
+    edge_ref[...] = own_ref[core]
+    inner_ref[...] = own_ref[1 - core]
+    edge_level_ref[...] = level_ref[core]
+    inner_level_ref[...] = level_ref[1 - core]
 
 
 def place(received, layers, bricks_y):
     plane = received[0].shape[1]
     rows = received[0].shape[0] - level_room(layers)
+    field = (bricks_y, rows, plane)
+    level = (bricks_y, layers, plane)
     return pl.pallas_call(
         functools.partial(place_kernel, bricks_y),
-        out_shape=(
-            jax.ShapeDtypeStruct((owned, bricks_y, rows, plane), jnp.bfloat16),
-            jax.ShapeDtypeStruct((owned, bricks_y, layers, plane), jnp.float32),
-            jax.ShapeDtypeStruct((bricks_y, rows, plane), jnp.bfloat16),
-        ),
+        out_shape=[jax.ShapeDtypeStruct(field, jnp.bfloat16)] * 2
+        + [jax.ShapeDtypeStruct(level, jnp.float32)] * 2,
+        scratch_shapes=[
+            pltpu.VMEM((owned,) + field, jnp.bfloat16),
+            pltpu.VMEM((owned,) + level, jnp.float32),
+        ],
         compiler_params=pltpu.CompilerParams(vmem_limit_bytes=vmem_limit),
     )(*received)
 
 
 def plane_kernel(own_ref, level_ref, weights_ref, partial_ref):
-    _, bricks_y, rows, plane = own_ref.shape
-    layers = level_ref.shape[2]
+    bricks_y, rows, plane = own_ref.shape
+    layers = level_ref.shape[1]
     share = rows // layers
     for b in range(bricks_y):
         fields, weights = [], []
         for kind, other in ((0, b), (1, b - 1), (2, b + 1)):
             if 0 <= other < bricks_y:
                 for part in range(weights_ref.shape[1]):
-                    fields.append(own_ref[:, other].reshape(owned * rows, plane))
+                    fields.append(own_ref[other])
                     weights.append(weights_ref[kind, part])
         sides = jnp.dot(
             jnp.concatenate(fields, axis=1),
             jnp.concatenate(weights, axis=0),
             preferred_element_type=jnp.float32,
         )
-        for a in range(owned):
-            for layer in range(layers):
-                here = slice(layer * share, (layer + 1) * share)
-                center = own_ref[a, b, here].astype(jnp.float32)
-                level = jnp.broadcast_to(level_ref[a, b, layer : layer + 1, :], (share, plane))
-                side = sides[a * rows + layer * share : a * rows + (layer + 1) * share]
-                partial_ref[a, b, here] = side + level * center
+        for layer in range(layers):
+            here = slice(layer * share, (layer + 1) * share)
+            level = jnp.broadcast_to(level_ref[b, layer : layer + 1, :], (share, plane))
+            partial_ref[b, here] = sides[here] + level * own_ref[b, here].astype(jnp.float32)
 
 
 def plane_part(own, level, weights):
-    _, bricks_y, rows, plane = own.shape
-    flops = 2 * owned * bricks_y * bricks_y * 3 * rows * plane * plane
+    bricks_y, rows, plane = own.shape
+    flops = 2 * bricks_y * bricks_y * 3 * rows * plane * plane
     return pl.pallas_call(
         plane_kernel,
         out_shape=jax.ShapeDtypeStruct(own.shape, jnp.float32),
@@ -203,91 +224,103 @@
     )(own, level, weights)
 
 
-def layer_kernel(stage, layers, partial_ref, own_ref, swapped_ref, edge_ref, *refs):
-    if stage == 0:
-        before_ref, (next_ref, next_edge_ref) = None, refs
-    else:
-        before_ref, refs = refs[0], refs[1:]
-        if stage == DEG - 1:
-            sent_refs, next_ref = refs[:-1], refs[-1]
-        else:
-            next_ref, next_edge_ref = refs
+def layer_kernel(first, layers, pack, partial_ref, own_ref, outer_ref, other_ref, *refs):
+    refs = list(refs)
+    before_ref = None if first else refs.pop(0)
+    inner_ref = refs.pop(0) if pack else None
+    next_ref = refs.pop()
     core, mid, y = lax.axis_index("core"), lax.axis_index("mid"), lax.axis_index("gy")
-    _, bricks_y, rows, plane = own_ref.shape
+    bricks_y, rows, plane = own_ref.shape
     share = rows // layers
     width = min(plane, 128)
 
-    def chosen(first, second):
-        return jnp.where(core == 0, first.astype(jnp.float32), second.astype(jnp.float32))
-
-    for a in range(owned):
+    def step(low_ref, high_ref):
         for b in range(bricks_y):
             for column in range(0, share, group):
                 for left in range(0, plane, width):
                     lane = slice(left, left + width)
-
-                    def rows_of(layer):
-                        return slice(layer * share + column, layer * share + column + group)
-
-                    low, own, high = [], [], []
-                    for layer in range(layers):
-                        here = rows_of(layer)
-                        own.append(own_ref[a, b, here, lane].astype(jnp.float32))
-                        near = swapped_ref[core, b, here, lane].astype(jnp.float32)
-                        if a == 0:
-                            low.append(chosen(edge_ref[b, here, lane], swapped_ref[0, b, here, lane]))
-                            high.append(near)
-                        else:
-                            low.append(near)
-                            high.append(chosen(swapped_ref[1, b, here, lane], edge_ref[b, here, lane]))
-                    window = low + own + high
-                    for layer in range(layers):
-                        here = rows_of(layer)
-                        value = partial_ref[a, b, here, lane]
+                    places = [
+                        slice(layer * share + column, layer * share + column + group)
+                        for layer in range(layers)
+                    ]
+                    window = [
+                        ref[b, here, lane].astype(jnp.float32)
+                        for ref in (low_ref, own_ref, high_ref)
+                        for here in places
+                    ]
+                    for layer, here in enumerate(places):
+                        value = partial_ref[b, here, lane]
                         for distance in range(1, stencil_reach + 1):
                             pair = window[layers + layer - distance] + window[layers + layer + distance]
                             value = value + side_weights[distance] * pair
-                        if stage > 0:
-                            value = 2.0 * value - before_ref[a, b, here, lane].astype(jnp.float32)
-                        next_ref[a, b, here, lane] = value.astype(jnp.bfloat16)
-    if stage < DEG - 1:
-        next_edge_ref[...] = next_ref[core]
-    else:
-        for step, sent_ref in zip(offsets(bricks_y), sent_refs):
-            to_mid, to_y = ahead(mid, y, step, bricks_y)
-            sent_ref[...] = next_ref[to_mid, to_y]
-
-
-def layer_part(stage, layers, partial, own, swapped, edge, before):
-    _, bricks_y, rows, plane = own.shape
-    whole = jax.ShapeDtypeStruct(own.shape, jnp.bfloat16)
+                        if before_ref is not None:
+                            value = 2.0 * value - before_ref[b, here, lane].astype(jnp.float32)
+                        next_ref[b, here, lane] = value.astype(jnp.bfloat16)
+
+    @pl.when(core == 0)
+    def _():
+        step(outer_ref, other_ref)
+
+    @pl.when(core != 0)
+    def _():
+        step(other_ref, outer_ref)
+
+    if pack:
+        for offset, sent_ref in zip(offsets(bricks_y), refs):
+            to_mid, to_y = ahead(mid, y, offset, bricks_y)
+
+            @pl.when(to_mid == core)
+            def _():
+                sent_ref[...] = next_ref[to_y]
+
+            @pl.when(to_mid != core)
+            def _():
+                sent_ref[...] = inner_ref[to_y]
+
+
+def layer_part(layers, partial, own, outer, other, before, inner=None):
+    bricks_y, rows, plane = own.shape
+    pack = inner is not None
+    operands = [partial, own, outer, other]
+    operands += [] if before is None else [before]
+    operands += [inner] if pack else []
     one = jax.ShapeDtypeStruct((rows, plane), jnp.bfloat16)
-    last = stage == DEG - 1
     return pl.pallas_call(
-        functools.partial(layer_kernel, stage, layers),
-        out_shape=[one] * (owned * bricks_y) if last else [whole, jax.ShapeDtypeStruct(edge.shape, jnp.bfloat16)],
-        scratch_shapes=[pltpu.VMEM(own.shape, jnp.bfloat16)] if last else [],
+        functools.partial(layer_kernel, before is None, layers, pack),
+        out_shape=[one] * (owned * bricks_y) if pack else jax.ShapeDtypeStruct(own.shape, jnp.bfloat16),
+        scratch_shapes=[pltpu.VMEM(own.shape, jnp.bfloat16)] if pack else [],
+        cost_estimate=pl.CostEstimate(
+            flops=24 * own.size, bytes_accessed=own.size * 14, transcendentals=0
+        ),
         compiler_params=pltpu.CompilerParams(vmem_limit_bytes=vmem_limit),
-    )(partial, own, swapped, edge, *([] if stage == 0 else [before]))
-
-
-def neighbour_bricks(own, edge):
+    )(*operands)
+
+
+def from_other_core(own):
+    return lax.ppermute(own, "core", [(0, 1), (1, 0)])
+
+
+def from_next_chip(edge):
     count = lax.axis_size(("far", "core"))
     pairs = [(at, at + 1) for at in range(1, count - 1, 2)]
-    edge = lax.ppermute(edge, ("far", "core"), pairs + [(b, a) for a, b in pairs])
-    return lax.ppermute(own, "core", [(0, 1), (1, 0)]), edge
-
-
-def chebyshev(own, level, edge, weights):
-    layers = level.shape[2]
-    before = None
+    return lax.ppermute(edge, ("far", "core"), pairs + [(b, a) for a, b in pairs])
+
+
+def chebyshev(edge, inner, edge_level, inner_level, weights):
+    layers = edge_level.shape[1]
+    edge_before = inner_before = None
     for stage in range(DEG):
-        swapped, arrived = neighbour_bricks(own, edge)
-        partial = plane_part(own, level, weights)
-        result = layer_part(stage, layers, partial, own, swapped, arrived, before)
-        if stage < DEG - 1:
-            before, (own, edge) = own, result
-    return result
+        outer = from_next_chip(edge)
+        other_inner = from_other_core(inner)
+        other_edge = from_other_core(edge)
+        edge_partial = plane_part(edge, edge_level, weights)
+        inner_partial = plane_part(inner, inner_level, weights)
+        inner_next = layer_part(layers, inner_partial, inner, other_inner, other_edge, inner_before)
+        last = inner_next if stage == DEG - 1 else None
+        edge_next = layer_part(layers, edge_partial, edge, outer, other_inner, edge_before, last)
+        edge_before, edge = edge, edge_next
+        inner_before, inner = inner, inner_next
+    return edge
 
 
 def join_kernel(bricks_y, *refs):
@@ -483,8 +516,8 @@
 
     cells = trial_orbitals.reshape(layers * extent_y * extent_z, columns)
     sent = split_columns(cells, potential, bricks_y)
-    own, level, edge = place(exchange(sent, bricks_y), layers, bricks_y)
-    sent = chebyshev(own, level, edge, weights)
+    placed = place(exchange(sent, bricks_y), layers, bricks_y)
+    sent = chebyshev(*placed, weights)
     rows, local_gram = join_columns(exchange(sent, bricks_y), layers, bricks_y)
     gram_matrix = sum_over_devices(local_gram)
     rotated, upper_factor = factor_and_rotate(gram_matrix, rows, total_cells)

time: 99.9 us -> 99.4 us (level)
  Pallas kernels: 20.4 us -> 23.2 us
  starting transfers between devices: 24.8 us -> 22.2 us
  blocking collectives: 35.8 us -> 34.8 us
    ppermute x6 -> x9, starting transfers between devices: 16.7 us -> 14 us  [the longest x6 12 us: from_other_core(): return lax.ppermute(own, 'core', [(0, 1), (1, 0)])]
    pallas_call x5 -> x8, Pallas kernels: 4.67 us -> 6.88 us  [the longest x6 4.02 us: layer_part(): pl.pallas_call(functools.partial(layer_kernel, before is None, layers, pa...]
    all_to_all x1, blocking collectives: 24.4 us -> 23.4 us  [sum_over_devices(): total = jnp.sum(lax.all_to_all(values, axes, 0, 0), axis=0)]
    pallas_call x3 -> x6, Pallas kernels: 4.13 us -> 4.63 us  [plane_part(): pl.pallas_call(plane_kernel, out_shape=jax.ShapeDtypeStruct(own.shape, jn...]
  transfers between devices with their start and end apart: 12 -> 15, of which waited for: 7 -> 6; matrix products, arithmetic and copies ran while one was open for 0% -> 0% of each run, Pallas kernels for 4% -> 8%
where the time goes in v4:
time: 99.4 us; the launch traced here: 99.1 us
  blocking collectives  34.8 us (35%)
  Pallas kernels  23.2 us (23%)
  starting transfers between devices  22.2 us (22%)
  waiting for transfers between devices  15.9 us (16%)
  local copies, waits for them, and re-layouts  2.24 us (2%)
    all_to_all x1, blocking collectives, sum_over_devices(): total = jnp.sum(lax.all_to_all(values, axes, 0, 0), axis=0)  23.4 us
    ppermute x6, waiting for transfers between devices, exchange(): result.append(lax.ppermute(message, ('mid', 'gy'), perm))  15.9 us
    ppermute x6, starting transfers between devices, from_other_core(): return lax.ppermute(own, 'core', [(0, 1), (1, 0)])  12 us
    all_to_all x1, blocking collectives, sum_over_devices(): lax.all_to_all(jnp.broadcast_to(total[None], values.shape), axes, 0, 0)  11.4 us
    pallas_call x1, Pallas kernels, factor_and_rotate(): pl.pallas_call(functools.partial(factor_kernel, math.sqrt(total_cells)),...  11 us
    ppermute x6, starting transfers between devices, exchange(): result.append(lax.ppermute(message, ('mid', 'gy'), perm))  8.13 us
    pallas_call x6, Pallas kernels, plane_part(): pl.pallas_call(plane_kernel, out_shape=jax.ShapeDtypeStruct(own.shape, jn...  4.63 us
    pallas_call x6, Pallas kernels, layer_part(): pl.pallas_call(functools.partial(layer_kernel, before is None, layers, pa...  4.02 us
  transfers between devices with their start and end apart: 15, of which 6 were waited for; matrix products, arithmetic and copies ran while one was open for 0% of the time, Pallas kernels for 8%

profile of v4, /device:TPU:0, one launch (start us, length us, event | category | flops | bytes accessed | tf_op | source)
XLA Modules:
  0.0 99.1 jit_solution(5577601375474174041)
XLA Ops:
  0.6 2.7 %shard_map.50 = (bf16[416,256]{1,0:T(8,128)(2,1)}, bf16[416,256]{1,0:T(8,128)(2,1)}, bf16[416,256]{1,0:T(8,128)(2,1)}, bf16[416,256]{1,0:T(8,128)(2,1)}) custom-call(bf16[1536,256]{1,0:T(8,128)(2,1)} %bitcast.2, f32[6,8,32]{2,1,0:T(8,128)} %potential_ref.1), custom_call_target="tpu_custom_call" | custom-call | tf_op jit(solution)/shard_map/pallas_call | solution.py:144
  3.4 3.0 %collective-permute-start = (bf16[416,256]{1,0:T(8,128)(2,1)}, bf16[416,256]{1,0:T(8,128)(2,1)S(1)}, u32[]{:S(2)}, u32[]{:S(2)}) collective-permute-start(bf16[416,256]{1,0:T(8,128)(2,1)} %get-tuple-element.19), channel_id=1, source_target_pairs={{0,1},{1,0},{4,5},{5,4},{2,3},{3,2},{6,7},{7,6},{8,9},{9,8},{12,13... | collective-permute-start | bytes 638984 | tf_op jit(solution)/shard_map/ppermute | solution.py:100
  6.4 1.5 %collective-permute-start.1 = (bf16[416,256]{1,0:T(8,128)(2,1)}, bf16[416,256]{1,0:T(8,128)(2,1)S(1)}, u32[]{:S(2)}, u32[]{:S(2)}) collective-permute-start(bf16[416,256]{1,0:T(8,128)(2,1)} %get-tuple-element.20), channel_id=1, source_target_pairs={{0,4},{1,5},{4,0},{5,1},{2,6},{3,7},{6,2},{7,3},{8,12},{9,13},{12,... | collective-permute-start | bytes 638984 | tf_op jit(solution)/shard_map/ppermute | solution.py:100
  7.9 0.1 collective-permute-start.2
  7.9 3.9 %collective-permute-done.refs_1_ = bf16[416,256]{1,0:T(8,128)(2,1)S(1)} collective-permute-done((bf16[416,256]{1,0:T(8,128)(2,1)}, bf16[416,256]{1,0:T(8,128)(2,1)S(1)}, u32[]{:S(2)}, u32[]{:S(2)}) %collective-permute-start) | collective-permute-done | bytes 213024 | tf_op jit(solution)/shard_map/ppermute | solution.py:100
  11.9 2.9 %collective-permute-done.1.refs_2_ = bf16[416,256]{1,0:T(8,128)(2,1)S(1)} collective-permute-done((bf16[416,256]{1,0:T(8,128)(2,1)}, bf16[416,256]{1,0:T(8,128)(2,1)S(1)}, u32[]{:S(2)}, u32[]{:S(2)}) %collective-permute-start.1) | collective-permute-done | bytes 213024 | tf_op jit(solution)/shard_map/ppermute | solution.py:100
  14.8 2.9 %collective-permute-done.2.refs_3_ = bf16[416,256]{1,0:T(8,128)(2,1)S(1)} collective-permute-done((bf16[416,256]{1,0:T(8,128)(2,1)}, bf16[416,256]{1,0:T(8,128)(2,1)S(1)}, u32[]{:S(2)}, u32[]{:S(2)}) %collective-permute-start.2) | collective-permute-done | bytes 213024 | tf_op jit(solution)/shard_map/ppermute | solution.py:100
  17.7 0.9 copy-done.2
  18.6 0.1 shard_map.51
  18.7 0.1 collective-permute-start.4
  18.8 0.5 collective-permute-start.6
  19.3 0.7 collective-permute-start.3
  20.0 0.0 copy-start
  20.0 1.3 %copy-done = bf16[3,3,256,256]{3,2,1,0:T(8,128)(2,1)S(1)} copy-done((bf16[3,3,256,256]{3,2,1,0:T(8,128)(2,1)S(1)}, bf16[3,3,256,256]{3,2,1,0:T(8,128)(2,1)}, u32[]{:S(2)}) %copy-start) | copy-done | bytes 1179672
  21.3 0.8 shard_map.55.partial_ref
  22.1 0.8 shard_map.52.partial_ref
  22.8 0.0 collective-permute-done.4.other_ref.outer_ref
  22.9 0.6 shard_map.56.own_ref.refs_0_
  23.4 0.0 copy-start.1
  23.5 3.1 %collective-permute-start.7 = (bf16[2,384,256]{2,1,0:T(8,128)(2,1)S(1)}, bf16[2,384,256]{2,1,0:T(8,128)(2,1)S(1)}, u32[]{:S(2)}, u32[]{:S(2)}) collective-permute-start(bf16[2,384,256]{2,1,0:T(8,128)(2,1)S(1)} %shard_map.56.own_ref.refs_0_), channel_id=1, source_target_pairs={{0,2},{2,0},{1,3},{3,1},{4,6},{6,4},{5,7},{7,5},{8,10},{10,8},{9,1... | collective-permute-start | bytes 1179656 | tf_op jit(solution)/shard_map/ppermute | solution.py:300
  26.6 0.0 collective-permute-done.3.outer_ref
  26.6 0.6 shard_map.53.own_ref.refs_0_
  27.2 2.0 %collective-permute-start.9 = (bf16[2,384,256]{2,1,0:T(8,128)(2,1)S(1)}, bf16[2,384,256]{2,1,0:T(8,128)(2,1)S(1)}, u32[]{:S(2)}, u32[]{:S(2)}) collective-permute-start(bf16[2,384,256]{2,1,0:T(8,128)(2,1)S(1)} %shard_map.53.own_ref.refs_0_), channel_id=1, source_target_pairs={{0,2},{2,0},{1,3},{3,1},{4,6},{6,4},{5,7},{7,5},{8,10},{10,8},{9,1... | collective-permute-start | bytes 1179656 | tf_op jit(solution)/shard_map/ppermute | solution.py:300
  29.1 0.7 collective-permute-start.5
  29.8 0.8 shard_map.59.partial_ref
  30.6 0.8 shard_map.54.partial_ref
  31.4 0.0 collective-permute-done.7.other_ref.outer_ref
  31.4 0.7 shard_map.60.own_ref
  32.1 3.1 %collective-permute-start.10 = (bf16[2,384,256]{2,1,0:T(8,128)(2,1)S(1)}, bf16[2,384,256]{2,1,0:T(8,128)(2,1)S(1)}, u32[]{:S(2)}, u32[]{:S(2)}) collective-permute-start(bf16[2,384,256]{2,1,0:T(8,128)(2,1)S(1)} %shard_map.60.own_ref), channel_id=1, source_target_pairs={{0,2},{2,0},{1,3},{3,1},{4,6},{6,4},{5,7},{7,5},{8,10},{10,8},{9,1... | collective-permute-start | bytes 1179656 | tf_op jit(solution)/shard_map/ppermute | solution.py:300
  35.2 0.6 shard_map.57.own_ref
  35.9 3.2 %collective-permute-start.11 = (bf16[2,384,256]{2,1,0:T(8,128)(2,1)S(1)}, bf16[2,384,256]{2,1,0:T(8,128)(2,1)S(1)}, u32[]{:S(2)}, u32[]{:S(2)}) collective-permute-start(bf16[2,384,256]{2,1,0:T(8,128)(2,1)S(1)} %shard_map.57.own_ref), channel_id=1, source_target_pairs={{0,2},{2,0},{1,3},{3,1},{4,6},{6,4},{5,7},{7,5},{8,10},{10,8},{9,1... | collective-permute-start | bytes 1179656 | tf_op jit(solution)/shard_map/ppermute | solution.py:300
  39.1 0.7 collective-permute-start.8
  39.7 0.8 shard_map.61.partial_ref
  40.5 0.8 shard_map.58.partial_ref
  41.3 0.7 shard_map.62.refs_1_
  42.0 0.0 collective-permute-done.8.outer_ref
  42.0 0.9 shard_map.63
  42.9 1.6 %collective-permute-start.12 = (bf16[384,256]{1,0:T(8,128)(2,1)S(1)}, bf16[384,256]{1,0:T(8,128)(2,1)S(1)}, u32[]{:S(2)}, u32[]{:S(2)}) collective-permute-start(bf16[384,256]{1,0:T(8,128)(2,1)S(1)} %get-tuple-element.27), channel_id=1, source_target_pairs={{0,1},{1,0},{4,5},{5,4},{2,3},{3,2},{6,7},{7,6},{8,9},{9,8},{12,13... | collective-permute-start | bytes 589832 | tf_op jit(solution)/shard_map/ppermute | solution.py:100
  44.5 1.5 %collective-permute-start.13 = (bf16[384,256]{1,0:T(8,128)(2,1)S(1)}, bf16[384,256]{1,0:T(8,128)(2,1)S(1)}, u32[]{:S(2)}, u32[]{:S(2)}) collective-permute-start(bf16[384,256]{1,0:T(8,128)(2,1)S(1)} %get-tuple-element.28), channel_id=1, source_target_pairs={{0,4},{1,5},{4,0},{5,1},{2,6},{3,7},{6,2},{7,3},{8,12},{9,13},{12,... | collective-permute-start | bytes 589832 | tf_op jit(solution)/shard_map/ppermute | solution.py:100
  46.0 0.5 collective-permute-start.14
  46.5 2.2 %collective-permute-done.12.refs_1_ = bf16[384,256]{1,0:T(8,128)(2,1)S(1)} collective-permute-done((bf16[384,256]{1,0:T(8,128)(2,1)S(1)}, bf16[384,256]{1,0:T(8,128)(2,1)S(1)}, u32[]{:S(2)}, u32[]{:S(2)}) %collective-permute-start.12) | collective-permute-done | bytes 196640 | tf_op jit(solution)/shard_map/ppermute | solution.py:100
  48.7 1.5 %collective-permute-done.13.refs_2_ = bf16[384,256]{1,0:T(8,128)(2,1)S(1)} collective-permute-done((bf16[384,256]{1,0:T(8,128)(2,1)S(1)}, bf16[384,256]{1,0:T(8,128)(2,1)S(1)}, u32[]{:S(2)}, u32[]{:S(2)}) %collective-permute-start.13) | collective-permute-done | bytes 196640 | tf_op jit(solution)/shard_map/ppermute | solution.py:100
  50.2 2.4 %collective-permute-done.14.refs_3_ = bf16[384,256]{1,0:T(8,128)(2,1)S(1)} collective-permute-done((bf16[384,256]{1,0:T(8,128)(2,1)S(1)}, bf16[384,256]{1,0:T(8,128)(2,1)S(1)}, u32[]{:S(2)}, u32[]{:S(2)}) %collective-permute-start.14) | collective-permute-done | bytes 196640 | tf_op jit(solution)/shard_map/ppermute | solution.py:100
  52.6 0.6 shard_map.64
  53.3 23.4 %all_to_all.10 = f32[32,4,384]{2,1,0:T(4,128)S(1)} all-to-all(f32[32,4,384]{2,1,0:T(4,128)S(1)} %get-tuple-element.30), channel_id=1, replica_groups=mesh['far'=4,'mid'=2,'core'=2,'gy'=2] {'far','mid','core','gy'}, dimensions={0} | all-to-all | bytes 393216 | tf_op jit(solution)/shard_map/all_to_all | solution.py:507
  76.6 0.1 reduce_sum.9
  76.7 11.4 %all_to_all.11.gram_ref = f32[32,4,384]{2,1,0:T(4,128)S(1)} all-to-all(f32[32,4,384]{2,1,0:T(4,128)S(1)} %broadcast_in_dim.2), channel_id=1, replica_groups=mesh['far'=4,'mid'=2,'core'=2,'gy'=2] {'far','mid','core','gy'}, dimensions={0} | all-to-all | bytes 393216 | tf_op jit(solution)/shard_map/all_to_all | solution.py:508
  88.1 11.0 %shard_map.65 = (bf16[1536,256]{1,0:T(8,128)(2,1)}, f32[256,256]{1,0:T(8,128)}) custom-call(f32[32,4,384]{2,1,0:T(4,128)S(1)} %all_to_all.11.gram_ref, bf16[1536,256]{1,0:T(8,128)(2,1)S(1)} %get-tuple-element.31.rows_ref), custom_call_target="tpu_custom_call" | custom-call | tf_op jit(solution)/shard_map/pallas_call | solution.py:489
  (8 shorter events, 0.0 us)
Async XLA Ops:
  3.4 8.5 %collective-permute-start = (bf16[416,256]{1,0:T(8,128)(2,1)}, bf16[416,256]{1,0:T(8,128)(2,1)S(1)}, u32[]{:S(2)}, u32[]{:S(2)}) collective-permute-start(bf16[416,256]{1,0:T(8,128)(2,1)} %get-tuple-element.19), channel_id=1, source_target_pairs={{0,1},{1,0},{4,5},{5,4},{2,3},{3,2},{6,7},{7,6},{8,9},{9,8},{12,13... | collective-permute-start | bytes 638984 | tf_op jit(solution)/shard_map/ppermute | solution.py:100
  6.4 8.4 %collective-permute-start.1 = (bf16[416,256]{1,0:T(8,128)(2,1)}, bf16[416,256]{1,0:T(8,128)(2,1)S(1)}, u32[]{:S(2)}, u32[]{:S(2)}) collective-permute-start(bf16[416,256]{1,0:T(8,128)(2,1)} %get-tuple-element.20), channel_id=1, source_target_pairs={{0,4},{1,5},{4,0},{5,1},{2,6},{3,7},{6,2},{7,3},{8,12},{9,13},{12,... | collective-permute-start | bytes 638984 | tf_op jit(solution)/shard_map/ppermute | solution.py:100
  7.9 9.8 %collective-permute-start.2 = (bf16[416,256]{1,0:T(8,128)(2,1)}, bf16[416,256]{1,0:T(8,128)(2,1)S(1)}, u32[]{:S(2)}, u32[]{:S(2)}) collective-permute-start(bf16[416,256]{1,0:T(8,128)(2,1)} %get-tuple-element.21), channel_id=1, source_target_pairs={{0,5},{1,4},{4,1},{5,0},{2,7},{3,6},{6,3},{7,2},{8,13},{9,12},{12,... | collective-permute-start | bytes 638984 | tf_op jit(solution)/shard_map/ppermute | solution.py:100
  17.7 0.9 copy-start.2
  18.7 4.1 %collective-permute-start.4 = (bf16[2,384,256]{2,1,0:T(8,128)(2,1)S(1)}, bf16[2,384,256]{2,1,0:T(8,128)(2,1)S(1)}, u32[]{:S(2)}, u32[]{:S(2)}) collective-permute-start(bf16[2,384,256]{2,1,0:T(8,128)(2,1)S(1)} %get-tuple-element.24.own_ref.refs_0_), channel_id=1, source_target_pairs={{0,2},{2,0},{1,3},{3,1},{4,6},{6,4},{5,7},{7,5},{8,10},{10,8},{9,1... | collective-permute-start | bytes 1179656 | tf_op jit(solution)/shard_map/ppermute | solution.py:300
  18.8 4.0 %collective-permute-start.6 = (bf16[2,384,256]{2,1,0:T(8,128)(2,1)S(1)}, bf16[2,384,256]{2,1,0:T(8,128)(2,1)S(1)}, u32[]{:S(2)}, u32[]{:S(2)}) collective-permute-start(bf16[2,384,256]{2,1,0:T(8,128)(2,1)S(1)} %get-tuple-element.22.own_ref.refs_0_), channel_id=1, source_target_pairs={{0,2},{2,0},{1,3},{3,1},{4,6},{6,4},{5,7},{7,5},{8,10},{10,8},{9,1... | collective-permute-start | bytes 1179656 | tf_op jit(solution)/shard_map/ppermute | solution.py:300
  19.3 7.3 %collective-permute-start.3 = (bf16[2,384,256]{2,1,0:T(8,128)(2,1)S(1)}, bf16[2,384,256]{2,1,0:T(8,128)(2,1)S(1)}, u32[]{:S(2)}, u32[]{:S(2)}) collective-permute-start(bf16[2,384,256]{2,1,0:T(8,128)(2,1)S(1)} %get-tuple-element.22.own_ref.refs_0_), channel_id=1, source_target_pairs={{2,8},{10,16},{18,24},{8,2},{16,10},{24,18},{3,9},{11,17},{19,25},... | collective-permute-start | bytes 1179656 | tf_op jit(solution)/shard_map/ppermute | solution.py:306
  20.0 1.3 %copy-start = (bf16[3,3,256,256]{3,2,1,0:T(8,128)(2,1)S(1)}, bf16[3,3,256,256]{3,2,1,0:T(8,128)(2,1)}, u32[]{:S(2)}) copy-start(bf16[3,3,256,256]{3,2,1,0:T(8,128)(2,1)} %constant.4.clone.weights_ref) | copy-start | bytes 3538948
  23.4 6.4 %copy-start.1 = (bf16[3,3,256,256]{3,2,1,0:T(8,128)(2,1)S(1)}, bf16[3,3,256,256]{3,2,1,0:T(8,128)(2,1)}, u32[]{:S(2)}) copy-start(bf16[3,3,256,256]{3,2,1,0:T(8,128)(2,1)} %constant.4.clone.weights_ref) | copy-start | bytes 3538948
  23.5 7.9 %collective-permute-start.7 = (bf16[2,384,256]{2,1,0:T(8,128)(2,1)S(1)}, bf16[2,384,256]{2,1,0:T(8,128)(2,1)S(1)}, u32[]{:S(2)}, u32[]{:S(2)}) collective-permute-start(bf16[2,384,256]{2,1,0:T(8,128)(2,1)S(1)} %shard_map.56.own_ref.refs_0_), channel_id=1, source_target_pairs={{0,2},{2,0},{1,3},{3,1},{4,6},{6,4},{5,7},{7,5},{8,10},{10,8},{9,1... | collective-permute-start | bytes 1179656 | tf_op jit(solution)/shard_map/ppermute | solution.py:300
  27.2 4.2 %collective-permute-start.9 = (bf16[2,384,256]{2,1,0:T(8,128)(2,1)S(1)}, bf16[2,384,256]{2,1,0:T(8,128)(2,1)S(1)}, u32[]{:S(2)}, u32[]{:S(2)}) collective-permute-start(bf16[2,384,256]{2,1,0:T(8,128)(2,1)S(1)} %shard_map.53.own_ref.refs_0_), channel_id=1, source_target_pairs={{0,2},{2,0},{1,3},{3,1},{4,6},{6,4},{5,7},{7,5},{8,10},{10,8},{9,1... | collective-permute-start | bytes 1179656 | tf_op jit(solution)/shard_map/ppermute | solution.py:300
  29.1 6.1 %collective-permute-start.5 = (bf16[2,384,256]{2,1,0:T(8,128)(2,1)S(1)}, bf16[2,384,256]{2,1,0:T(8,128)(2,1)S(1)}, u32[]{:S(2)}, u32[]{:S(2)}) collective-permute-start(bf16[2,384,256]{2,1,0:T(8,128)(2,1)S(1)} %shard_map.53.own_ref.refs_0_), channel_id=1, source_target_pairs={{2,8},{10,16},{18,24},{8,2},{16,10},{24,18},{3,9},{11,17},{19,25},... | collective-permute-start | bytes 1179656 | tf_op jit(solution)/shard_map/ppermute | solution.py:306
  32.1 9.2 %collective-permute-start.10 = (bf16[2,384,256]{2,1,0:T(8,128)(2,1)S(1)}, bf16[2,384,256]{2,1,0:T(8,128)(2,1)S(1)}, u32[]{:S(2)}, u32[]{:S(2)}) collective-permute-start(bf16[2,384,256]{2,1,0:T(8,128)(2,1)S(1)} %shard_map.60.own_ref), channel_id=1, source_target_pairs={{0,2},{2,0},{1,3},{3,1},{4,6},{6,4},{5,7},{7,5},{8,10},{10,8},{9,1... | collective-permute-start | bytes 1179656 | tf_op jit(solution)/shard_map/ppermute | solution.py:300
  35.9 5.4 %collective-permute-start.11 = (bf16[2,384,256]{2,1,0:T(8,128)(2,1)S(1)}, bf16[2,384,256]{2,1,0:T(8,128)(2,1)S(1)}, u32[]{:S(2)}, u32[]{:S(2)}) collective-permute-start(bf16[2,384,256]{2,1,0:T(8,128)(2,1)S(1)} %shard_map.57.own_ref), channel_id=1, source_target_pairs={{0,2},{2,0},{1,3},{3,1},{4,6},{6,4},{5,7},{7,5},{8,10},{10,8},{9,1... | collective-permute-start | bytes 1179656 | tf_op jit(solution)/shard_map/ppermute | solution.py:300
  39.1 2.9 %collective-permute-start.8 = (bf16[2,384,256]{2,1,0:T(8,128)(2,1)S(1)}, bf16[2,384,256]{2,1,0:T(8,128)(2,1)S(1)}, u32[]{:S(2)}, u32[]{:S(2)}) collective-permute-start(bf16[2,384,256]{2,1,0:T(8,128)(2,1)S(1)} %shard_map.57.own_ref), channel_id=1, source_target_pairs={{2,8},{10,16},{18,24},{8,2},{16,10},{24,18},{3,9},{11,17},{19,25},... | collective-permute-start | bytes 1179656 | tf_op jit(solution)/shard_map/ppermute | solution.py:306
  42.9 5.7 %collective-permute-start.12 = (bf16[384,256]{1,0:T(8,128)(2,1)S(1)}, bf16[384,256]{1,0:T(8,128)(2,1)S(1)}, u32[]{:S(2)}, u32[]{:S(2)}) collective-permute-start(bf16[384,256]{1,0:T(8,128)(2,1)S(1)} %get-tuple-element.27), channel_id=1, source_target_pairs={{0,1},{1,0},{4,5},{5,4},{2,3},{3,2},{6,7},{7,6},{8,9},{9,8},{12,13... | collective-permute-start | bytes 589832 | tf_op jit(solution)/shard_map/ppermute | solution.py:100
  44.5 5.7 %collective-permute-start.13 = (bf16[384,256]{1,0:T(8,128)(2,1)S(1)}, bf16[384,256]{1,0:T(8,128)(2,1)S(1)}, u32[]{:S(2)}, u32[]{:S(2)}) collective-permute-start(bf16[384,256]{1,0:T(8,128)(2,1)S(1)} %get-tuple-element.28), channel_id=1, source_target_pairs={{0,4},{1,5},{4,0},{5,1},{2,6},{3,7},{6,2},{7,3},{8,12},{9,13},{12,... | collective-permute-start | bytes 589832 | tf_op jit(solution)/shard_map/ppermute | solution.py:100
  46.0 6.6 %collective-permute-start.14 = (bf16[384,256]{1,0:T(8,128)(2,1)S(1)}, bf16[384,256]{1,0:T(8,128)(2,1)S(1)}, u32[]{:S(2)}, u32[]{:S(2)}) collective-permute-start(bf16[384,256]{1,0:T(8,128)(2,1)S(1)} %get-tuple-element.29), channel_id=1, source_target_pairs={{0,5},{1,4},{4,1},{5,0},{2,7},{3,6},{6,3},{7,2},{8,13},{9,12},{12,... | collective-permute-start | bytes 589832 | tf_op jit(solution)/shard_map/ppermute | solution.py:100

commit v5 on v4

--- a/solution.py
+++ b/solution.py
@@ -29,7 +29,6 @@
 owned = 2
 group = 16
 vmem_limit = 48 * 1024 * 1024
-fetching_limit = 63 * 1024 * 1024
 
 center_shift = -1.5 * STENCIL_WEIGHTS[0] - filter_center
 side_weights = tuple(-0.5 * weight / filter_half for weight in STENCIL_WEIGHTS)
@@ -102,29 +101,19 @@
 
 
 def split_kernel(bricks_y, cells_ref, potential_ref, *refs):
-    sent_refs, (block_ref, fetched_ref, level_ref, arrived) = refs[:-4], refs[-4:]
+    sent_refs, block_ref = refs[:-1], refs[-1]
     mid, y = lax.axis_index("mid"), lax.axis_index("gy")
     columns, plane = block_ref.shape
     share = columns // len(sent_refs)
     layers = cells_ref.shape[0] // plane
-    fetches = [pltpu.make_async_copy(potential_ref, level_ref, arrived.at[layers])]
-    for layer in range(layers):
-        part = pl.ds(layer * plane, plane)
-        fetches.append(
-            pltpu.make_async_copy(cells_ref.at[part], fetched_ref.at[part], arrived.at[layer])
-        )
-    for fetch in fetches:
-        fetch.start()
-    fetches[0].wait()
     potential = jnp.concatenate(
-        [level_ref[:, at, :] for at in range(level_ref.shape[1])], axis=1
+        [potential_ref[:, at, :] for at in range(potential_ref.shape[1])], axis=1
     )
     extra = level_rows(potential, sent_refs[0].shape[0] - layers * share)
     for sent_ref in sent_refs:
         sent_ref[layers * share :, :] = extra
     for layer in range(layers):
-        fetches[layer + 1].wait()
-        block = fetched_ref[layer * plane : (layer + 1) * plane, :].astype(jnp.float32)
+        block = cells_ref[layer * plane : (layer + 1) * plane, :].astype(jnp.float32)
         block_ref[...] = block.T
         for step, sent_ref in zip(offsets(bricks_y), sent_refs):
             to_mid, to_y = ahead(mid, y, step, bricks_y)
@@ -143,22 +132,22 @@
     )
     return pl.pallas_call(
         functools.partial(split_kernel, bricks_y),
-        in_specs=[pl.BlockSpec(memory_space=pltpu.HBM)] * 2,
         out_shape=[message] * parts,
-        scratch_shapes=[
-            pltpu.VMEM((columns, plane), jnp.float32),
-            pltpu.VMEM((count, columns), jnp.bfloat16),
-            pltpu.VMEM(potential.shape, jnp.float32),
-            pltpu.SemaphoreType.DMA((layers + 1,)),
-        ],
-        compiler_params=pltpu.CompilerParams(vmem_limit_bytes=fetching_limit),
+        scratch_shapes=[pltpu.VMEM((columns, plane), jnp.float32)],
+        compiler_params=pltpu.CompilerParams(vmem_limit_bytes=vmem_limit),
     )(cells, potential)
 
 
+def taker(refs, bricks_y):
+    rest = iter(refs)
+    return lambda count=bricks_y: [next(rest) for _ in range(count)]
+
+
 def place_kernel(bricks_y, *refs):
-    parts = owned * bricks_y
-    received_refs, results = refs[:parts], refs[parts:]
-    edge_ref, inner_ref, edge_level_ref, inner_level_ref, own_ref, level_ref = results
+    take = taker(refs, bricks_y)
+    received_refs = take(owned * bricks_y)
+    edge_refs, inner_refs = take(), take()
+    edge_level_ref, inner_level_ref, own_ref, level_ref = take(4)
     mid, y, core = lax.axis_index("mid"), lax.axis_index("gy"), lax.axis_index("core")
     rows = own_ref.shape[2]
     layers = level_ref.shape[2]
@@ -168,8 +157,9 @@
         extra = received_ref[rows:].astype(jnp.float32)
         level = extra[:layers] + extra[layers : 2 * layers] + extra[2 * layers : 3 * layers]
         level_ref[at, b] = level
-    edge_ref[...] = own_ref[core]
-    inner_ref[...] = own_ref[1 - core]
+    for b in range(bricks_y):
+        edge_refs[b][...] = own_ref[core, b]
+        inner_refs[b][...] = own_ref[1 - core, b]
     edge_level_ref[...] = level_ref[core]
     inner_level_ref[...] = level_ref[1 - core]
 
@@ -177,22 +167,25 @@
 def place(received, layers, bricks_y):
     plane = received[0].shape[1]
     rows = received[0].shape[0] - level_room(layers)
-    field = (bricks_y, rows, plane)
+    field = (rows, plane)
     level = (bricks_y, layers, plane)
-    return pl.pallas_call(
+    results = pl.pallas_call(
         functools.partial(place_kernel, bricks_y),
-        out_shape=[jax.ShapeDtypeStruct(field, jnp.bfloat16)] * 2
+        out_shape=[jax.ShapeDtypeStruct(field, jnp.bfloat16)] * (2 * bricks_y)
         + [jax.ShapeDtypeStruct(level, jnp.float32)] * 2,
         scratch_shapes=[
-            pltpu.VMEM((owned,) + field, jnp.bfloat16),
+            pltpu.VMEM((owned, bricks_y) + field, jnp.bfloat16),
             pltpu.VMEM((owned,) + level, jnp.float32),
         ],
         compiler_params=pltpu.CompilerParams(vmem_limit_bytes=vmem_limit),
     )(*received)
-
-
-def plane_kernel(own_ref, level_ref, weights_ref, partial_ref):
-    bricks_y, rows, plane = own_ref.shape
+    return results[:bricks_y], results[bricks_y : 2 * bricks_y], results[-2], results[-1]
+
+
+def plane_kernel(bricks_y, *refs):
+    take = taker(refs, bricks_y)
+    own_refs, (level_ref, weights_ref), partial_refs = take(), take(2), take()
+    rows, plane = own_refs[0].shape
     layers = level_ref.shape[1]
     share = rows // layers
     for b in range(bricks_y):
@@ -200,7 +193,7 @@
         for kind, other in ((0, b), (1, b - 1), (2, b + 1)):
             if 0 <= other < bricks_y:
                 for part in range(weights_ref.shape[1]):
-                    fields.append(own_ref[other])
+                    fields.append(own_refs[other][...])
                     weights.append(weights_ref[kind, part])
         sides = jnp.dot(
             jnp.concatenate(fields, axis=1),
@@ -210,31 +203,36 @@
         for layer in range(layers):
             here = slice(layer * share, (layer + 1) * share)
             level = jnp.broadcast_to(level_ref[b, layer : layer + 1, :], (share, plane))
-            partial_ref[b, here] = sides[here] + level * own_ref[b, here].astype(jnp.float32)
+            partial_refs[b][here] = sides[here] + level * own_refs[b][here].astype(jnp.float32)
 
 
 def plane_part(own, level, weights):
-    bricks_y, rows, plane = own.shape
+    bricks_y = len(own)
+    rows, plane = own[0].shape
     flops = 2 * bricks_y * bricks_y * 3 * rows * plane * plane
     return pl.pallas_call(
-        plane_kernel,
-        out_shape=jax.ShapeDtypeStruct(own.shape, jnp.float32),
-        cost_estimate=pl.CostEstimate(flops=flops, bytes_accessed=own.size * 6, transcendentals=0),
+        functools.partial(plane_kernel, bricks_y),
+        out_shape=[jax.ShapeDtypeStruct((rows, plane), jnp.float32)] * bricks_y,
+        cost_estimate=pl.CostEstimate(
+            flops=flops, bytes_accessed=6 * bricks_y * rows * plane, transcendentals=0
+        ),
         compiler_params=pltpu.CompilerParams(vmem_limit_bytes=vmem_limit),
-    )(own, level, weights)
-
-
-def layer_kernel(first, layers, pack, partial_ref, own_ref, outer_ref, other_ref, *refs):
-    refs = list(refs)
-    before_ref = None if first else refs.pop(0)
-    inner_ref = refs.pop(0) if pack else None
-    next_ref = refs.pop()
+    )(*own, level, weights)
+
+
+def layer_kernel(first, layers, bricks_y, pack, *refs):
+    take = taker(refs, bricks_y)
+    partial_refs, own_refs, outer_refs, other_refs = take(), take(), take(), take()
+    before_refs = None if first else take()
+    inner_refs = take() if pack else None
+    sent_refs = take(owned * bricks_y) if pack else None
+    next_refs = take()
     core, mid, y = lax.axis_index("core"), lax.axis_index("mid"), lax.axis_index("gy")
-    bricks_y, rows, plane = own_ref.shape
+    rows, plane = own_refs[0].shape
     share = rows // layers
     width = min(plane, 128)
 
-    def step(low_ref, high_ref):
+    def step(low_refs, high_refs):
         for b in range(bricks_y):
             for column in range(0, share, group):
                 for left in range(0, plane, width):
@@ -244,66 +242,66 @@
                         for layer in range(layers)
                     ]
                     window = [
-                        ref[b, here, lane].astype(jnp.float32)
-                        for ref in (low_ref, own_ref, high_ref)
+                        ref[here, lane].astype(jnp.float32)
+                        for ref in (low_refs[b], own_refs[b], high_refs[b])
                         for here in places
                     ]
                     for layer, here in enumerate(places):
-                        value = partial_ref[b, here, lane]
+                        value = partial_refs[b][here, lane]
                         for distance in range(1, stencil_reach + 1):
                             pair = window[layers + layer - distance] + window[layers + layer + distance]
                             value = value + side_weights[distance] * pair
-                        if before_ref is not None:
-                            value = 2.0 * value - before_ref[b, here, lane].astype(jnp.float32)
-                        next_ref[b, here, lane] = value.astype(jnp.bfloat16)
+                        if before_refs is not None:
+                            value = 2.0 * value - before_refs[b][here, lane].astype(jnp.float32)
+                        next_refs[b][here, lane] = value.astype(jnp.bfloat16)
 
     @pl.when(core == 0)
     def _():
-        step(outer_ref, other_ref)
+        step(outer_refs, other_refs)
 
     @pl.when(core != 0)
     def _():
-        step(other_ref, outer_ref)
+        step(other_refs, outer_refs)
 
     if pack:
-        for offset, sent_ref in zip(offsets(bricks_y), refs):
+        for offset, sent_ref in zip(offsets(bricks_y), sent_refs):
             to_mid, to_y = ahead(mid, y, offset, bricks_y)
-
-            @pl.when(to_mid == core)
-            def _():
-                sent_ref[...] = next_ref[to_y]
-
-            @pl.when(to_mid != core)
-            def _():
-                sent_ref[...] = inner_ref[to_y]
+            for b in range(bricks_y):
+
+                @pl.when((to_mid == core) & (to_y == b))
+                def _():
+                    sent_ref[...] = next_refs[b][...]
+
+                @pl.when((to_mid != core) & (to_y == b))
+                def _():
+                    sent_ref[...] = inner_refs[b][...]
 
 
 def layer_part(layers, partial, own, outer, other, before, inner=None):
-    bricks_y, rows, plane = own.shape
+    bricks_y = len(own)
+    rows, plane = own[0].shape
     pack = inner is not None
-    operands = [partial, own, outer, other]
-    operands += [] if before is None else [before]
-    operands += [inner] if pack else []
+    operands = [*partial, *own, *outer, *other, *(before or []), *(inner or [])]
+    size = bricks_y * rows * plane
     one = jax.ShapeDtypeStruct((rows, plane), jnp.bfloat16)
     return pl.pallas_call(
-        functools.partial(layer_kernel, before is None, layers, pack),
-        out_shape=[one] * (owned * bricks_y) if pack else jax.ShapeDtypeStruct(own.shape, jnp.bfloat16),
-        scratch_shapes=[pltpu.VMEM(own.shape, jnp.bfloat16)] if pack else [],
-        cost_estimate=pl.CostEstimate(
-            flops=24 * own.size, bytes_accessed=own.size * 14, transcendentals=0
-        ),
+        functools.partial(layer_kernel, before is None, layers, bricks_y, pack),
+        out_shape=[one] * (owned * bricks_y if pack else bricks_y),
+        scratch_shapes=[pltpu.VMEM((rows, plane), jnp.bfloat16)] * bricks_y if pack else [],
+        cost_estimate=pl.CostEstimate(flops=24 * size, bytes_accessed=14 * size, transcendentals=0),
         compiler_params=pltpu.CompilerParams(vmem_limit_bytes=vmem_limit),
     )(*operands)
 
 
 def from_other_core(own):
-    return lax.ppermute(own, "core", [(0, 1), (1, 0)])
+    return [lax.ppermute(brick, "core", [(0, 1), (1, 0)]) for brick in own]
 
 
 def from_next_chip(edge):
     count = lax.axis_size(("far", "core"))
     pairs = [(at, at + 1) for at in range(1, count - 1, 2)]
-    return lax.ppermute(edge, ("far", "core"), pairs + [(b, a) for a, b in pairs])
+    both = pairs + [(b, a) for a, b in pairs]
+    return [lax.ppermute(brick, ("far", "core"), both) for brick in edge]
 
 
 def chebyshev(edge, inner, edge_level, inner_level, weights):
@@ -385,11 +383,10 @@
     columns = list(columns)
     full = [jnp.where(row == k, 1.0, 0.0).astype(jnp.float32) for k in range(panel_rows)]
     forward = list(full)
-    pivots = jnp.zeros((panel_rows, lanes), jnp.float32)
+    scales = jnp.zeros((panel_rows, lanes), jnp.float32)
     for step in range(panel_rows):
-        pivot = row_splat(columns[step], step)
-        scale = 1.0 / pivot
-        pivots = jnp.where(row == step, pivot, pivots)
+        scale = 1.0 / row_splat(columns[step], step)
+        scales = jnp.where(row == step, scale, scales)
         others = jnp.where(row == step, 0.0, columns[step])
         for k in range(step + 1, panel_rows):
             columns[k] = columns[k] - others * (row_splat(columns[k], step) * scale)
@@ -397,23 +394,20 @@
             forward[k] = jnp.where(row == step, full[k], forward[k])
             full[k] = full[k] - others * (row_splat(full[k], step) * scale)
         full[step] = full[step] - others * scale
-    inverse_pivots = 1.0 / pivots
-    root = lax.rsqrt(pivots)
-    full = [column * inverse_pivots for column in full]
+    root = jnp.sqrt(scales)
+    full = [column * scales for column in full]
     forward = [column * root for column in forward]
     return full, forward
 
 
 def combine(columns, rows):
-    width = rows.shape[1] // lanes
     parts = []
-    for part in range(width):
-        piece = rows[:, part * lanes : (part + 1) * lanes]
-        total = None
-        for k, column in enumerate(columns):
-            term = column * row_splat(piece, k)
-            total = term if total is None else total + term
-        parts.append(total)
+    for left in range(0, rows.shape[1], lanes):
+        piece = rows[:, left : left + lanes]
+        terms = [column * row_splat(piece, k) for k, column in enumerate(columns)]
+        while len(terms) > 1:
+            terms = [a + b for a, b in zip(terms[::2], terms[1::2])]
+        parts.append(terms[0])
     return jnp.concatenate(parts, axis=1)
 
 

time: 99.4 us -> 102 us (1.026)
  starting transfers between devices: 22.2 us -> 27.6 us
  Pallas kernels: 23.2 us -> 21 us
    ppermute x9 -> x18, starting transfers between devices: 14 us -> 19.5 us  [the longest x12 15.5 us: from_other_core(): return [lax.ppermute(brick, 'core', [(0, 1), (1, 0)]) for brick in own]]
    pallas_call x13, Pallas kernels: 11.4 us -> 9.24 us  [the longest x6 4.63 us: plane_part(): pl.pallas_call(functools.partial(plane_kernel, bricks_y), out_shape=[jax....]
  transfers between devices with their start and end apart: 15 -> 24, of which waited for: 6 -> 6; matrix products, arithmetic and copies ran while one was open for 0% -> 0% of each run, Pallas kernels for 8% -> 8%
where the time goes in v5:
time: 102 us; the launch traced here: 101 us
  blocking collectives  34.3 us (34%)
  starting transfers between devices  27.6 us (27%)
  Pallas kernels  21 us (21%)
  waiting for transfers between devices  15.7 us (15%)
  local copies, waits for them, and re-layouts  1.9 us (2%)
    all_to_all x1, blocking collectives, sum_over_devices(): total = jnp.sum(lax.all_to_all(values, axes, 0, 0), axis=0)  22.9 us
    ppermute x6, waiting for transfers between devices, exchange(): result.append(lax.ppermute(message, ('mid', 'gy'), perm))  15.6 us
    ppermute x12, starting transfers between devices, from_other_core(): return [lax.ppermute(brick, 'core', [(0, 1), (1, 0)]) for brick in own]  15.5 us
    all_to_all x1, blocking collectives, sum_over_devices(): lax.all_to_all(jnp.broadcast_to(total[None], values.shape), axes, 0, 0)  11.4 us
    pallas_call x1, Pallas kernels, factor_and_rotate(): pl.pallas_call(functools.partial(factor_kernel, math.sqrt(total_cells)),...  11 us
    ppermute x6, starting transfers between devices, exchange(): result.append(lax.ppermute(message, ('mid', 'gy'), perm))  8.13 us
    pallas_call x6, Pallas kernels, plane_part(): pl.pallas_call(functools.partial(plane_kernel, bricks_y), out_shape=[jax....  4.63 us
    pallas_call x6, Pallas kernels, layer_part(): pl.pallas_call(functools.partial(layer_kernel, before is None, layers, br...  4.11 us
  transfers between devices with their start and end apart: 24, of which 6 were waited for; matrix products, arithmetic and copies ran while one was open for 0% of the time, Pallas kernels for 8%

profile of v5, /device:TPU:0, one launch (start us, length us, event | category | flops | bytes accessed | tf_op | source)
XLA Modules:
  0.0 101.5 jit_solution(7064878579353048217)
XLA Ops:
  0.6 1.1 %copy-done = bf16[6,8,32,256]{3,2,1,0:T(8,128)(2,1)S(1)} copy-done((bf16[6,8,32,256]{3,2,1,0:T(8,128)(2,1)S(1)}, bf16[6,8,32,256]{3,2,1,0:T(8,128)(2,1)}, u32[]{:S(2)}) %copy-start) | copy-done | bytes 786456
  1.8 0.7 copy-done.1
  2.5 0.5 shard_map.50
  3.0 3.0 %collective-permute-start = (bf16[416,256]{1,0:T(8,128)(2,1)S(1)}, bf16[416,256]{1,0:T(8,128)(2,1)S(1)}, u32[]{:S(2)}, u32[]{:S(2)}) collective-permute-start(bf16[416,256]{1,0:T(8,128)(2,1)S(1)} %get-tuple-element.43), channel_id=1, source_target_pairs={{0,1},{1,0},{4,5},{5,4},{2,3},{3,2},{6,7},{7,6},{8,9},{9,8},{12,13... | collective-permute-start | bytes 638984 | tf_op jit(solution)/shard_map/ppermute | solution.py:99
  6.1 1.5 %collective-permute-start.1 = (bf16[416,256]{1,0:T(8,128)(2,1)S(1)}, bf16[416,256]{1,0:T(8,128)(2,1)S(1)}, u32[]{:S(2)}, u32[]{:S(2)}) collective-permute-start(bf16[416,256]{1,0:T(8,128)(2,1)S(1)} %get-tuple-element.44), channel_id=1, source_target_pairs={{0,4},{1,5},{4,0},{5,1},{2,6},{3,7},{6,2},{7,3},{8,12},{9,13},{12,... | collective-permute-start | bytes 638984 | tf_op jit(solution)/shard_map/ppermute | solution.py:99
  7.6 3.7 %collective-permute-done.refs_1_ = bf16[416,256]{1,0:T(8,128)(2,1)S(1)} collective-permute-done((bf16[416,256]{1,0:T(8,128)(2,1)S(1)}, bf16[416,256]{1,0:T(8,128)(2,1)S(1)}, u32[]{:S(2)}, u32[]{:S(2)}) %collective-permute-start) | collective-permute-done | bytes 213024 | tf_op jit(solution)/shard_map/ppermute | solution.py:99
  11.3 2.9 %collective-permute-done.1.refs_2_ = bf16[416,256]{1,0:T(8,128)(2,1)S(1)} collective-permute-done((bf16[416,256]{1,0:T(8,128)(2,1)S(1)}, bf16[416,256]{1,0:T(8,128)(2,1)S(1)}, u32[]{:S(2)}, u32[]{:S(2)}) %collective-permute-start.1) | collective-permute-done | bytes 213024 | tf_op jit(solution)/shard_map/ppermute | solution.py:99
  14.2 2.9 %collective-permute-done.2.refs_3_ = bf16[416,256]{1,0:T(8,128)(2,1)S(1)} collective-permute-done((bf16[416,256]{1,0:T(8,128)(2,1)S(1)}, bf16[416,256]{1,0:T(8,128)(2,1)S(1)}, u32[]{:S(2)}, u32[]{:S(2)}) %collective-permute-start.2) | collective-permute-done | bytes 213024 | tf_op jit(solution)/shard_map/ppermute | solution.py:99
  17.1 0.1 shard_map.51
  17.3 0.5 collective-permute-start.5
  17.8 0.1 collective-permute-start.6
  17.9 0.4 collective-permute-start.9
  18.3 0.7 collective-permute-start.3
  19.0 0.7 collective-permute-start.4
  19.7 0.8 shard_map.55
  20.5 0.6 shard_map.56
  21.1 4.4 %collective-permute-start.11 = (bf16[384,256]{1,0:T(8,128)(2,1)S(1)}, bf16[384,256]{1,0:T(8,128)(2,1)S(1)}, u32[]{:S(2)}, u32[]{:S(2)}) collective-permute-start(bf16[384,256]{1,0:T(8,128)(2,1)S(1)} %get-tuple-element.60.refs_0_.refs_2_.refs_8_), channel_id=1, source_target_pairs={{0,2},{2,0},{1,3},{3,1},{4,6},{6,4},{5,7},{7,5},{8,10},{10,8},{9,1... | collective-permute-start | bytes 589832 | tf_op jit(solution)/shard_map/ppermute | solution.py:297
  25.5 0.8 shard_map.52
  26.3 0.1 collective-permute-start.12
  26.4 0.6 shard_map.53
  27.0 2.8 %collective-permute-start.15 = (bf16[384,256]{1,0:T(8,128)(2,1)S(1)}, bf16[384,256]{1,0:T(8,128)(2,1)S(1)}, u32[]{:S(2)}, u32[]{:S(2)}) collective-permute-start(bf16[384,256]{1,0:T(8,128)(2,1)S(1)} %get-tuple-element.53.refs_0_.refs_2_.refs_8_), channel_id=1, source_target_pairs={{0,2},{2,0},{1,3},{3,1},{4,6},{6,4},{5,7},{7,5},{8,10},{10,8},{9,1... | collective-permute-start | bytes 589832 | tf_op jit(solution)/shard_map/ppermute | solution.py:297
  29.7 0.1 collective-permute-start.16
  29.8 0.7 collective-permute-start.7
  30.5 0.7 collective-permute-start.8
  31.2 0.8 shard_map.59
  32.0 0.7 shard_map.60
  32.6 4.7 %collective-permute-start.17 = (bf16[384,256]{1,0:T(8,128)(2,1)S(1)}, bf16[384,256]{1,0:T(8,128)(2,1)S(1)}, u32[]{:S(2)}, u32[]{:S(2)}) collective-permute-start(bf16[384,256]{1,0:T(8,128)(2,1)S(1)} %get-tuple-element.68.refs_0_.refs_2_), channel_id=1, source_target_pairs={{0,2},{2,0},{1,3},{3,1},{4,6},{6,4},{5,7},{7,5},{8,10},{10,8},{9,1... | collective-permute-start | bytes 589832 | tf_op jit(solution)/shard_map/ppermute | solution.py:297
  37.3 0.8 shard_map.54
  38.1 0.1 collective-permute-start.18
  38.2 0.7 shard_map.57
  38.9 2.2 %collective-permute-start.19 = (bf16[384,256]{1,0:T(8,128)(2,1)S(1)}, bf16[384,256]{1,0:T(8,128)(2,1)S(1)}, u32[]{:S(2)}, u32[]{:S(2)}) collective-permute-start(bf16[384,256]{1,0:T(8,128)(2,1)S(1)} %get-tuple-element.62.refs_0_.refs_2_), channel_id=1, source_target_pairs={{0,2},{2,0},{1,3},{3,1},{4,6},{6,4},{5,7},{7,5},{8,10},{10,8},{9,1... | collective-permute-start | bytes 589832 | tf_op jit(solution)/shard_map/ppermute | solution.py:297
  41.1 0.1 collective-permute-start.20
  41.2 0.7 collective-permute-start.13
  41.9 0.7 collective-permute-start.14
  42.5 0.8 shard_map.61
  43.3 0.8 shard_map.58
  44.1 0.7 shard_map.62
  44.8 1.0 shard_map.63
  45.8 1.6 %collective-permute-start.21 = (bf16[384,256]{1,0:T(8,128)(2,1)S(1)}, bf16[384,256]{1,0:T(8,128)(2,1)S(1)}, u32[]{:S(2)}, u32[]{:S(2)}) collective-permute-start(bf16[384,256]{1,0:T(8,128)(2,1)S(1)} %get-tuple-element.75), channel_id=1, source_target_pairs={{0,1},{1,0},{4,5},{5,4},{2,3},{3,2},{6,7},{7,6},{8,9},{9,8},{12,13... | collective-permute-start | bytes 589832 | tf_op jit(solution)/shard_map/ppermute | solution.py:99
  47.4 1.5 %collective-permute-start.22 = (bf16[384,256]{1,0:T(8,128)(2,1)S(1)}, bf16[384,256]{1,0:T(8,128)(2,1)S(1)}, u32[]{:S(2)}, u32[]{:S(2)}) collective-permute-start(bf16[384,256]{1,0:T(8,128)(2,1)S(1)} %get-tuple-element.76), channel_id=1, source_target_pairs={{0,4},{1,5},{4,0},{5,1},{2,6},{3,7},{6,2},{7,3},{8,12},{9,13},{12,... | collective-permute-start | bytes 589832 | tf_op jit(solution)/shard_map/ppermute | solution.py:99
  48.9 0.5 collective-permute-start.23
  49.3 2.2 %collective-permute-done.21.refs_1_ = bf16[384,256]{1,0:T(8,128)(2,1)S(1)} collective-permute-done((bf16[384,256]{1,0:T(8,128)(2,1)S(1)}, bf16[384,256]{1,0:T(8,128)(2,1)S(1)}, u32[]{:S(2)}, u32[]{:S(2)}) %collective-permute-start.21) | collective-permute-done | bytes 196640 | tf_op jit(solution)/shard_map/ppermute | solution.py:99
  51.5 1.5 %collective-permute-done.22.refs_2_ = bf16[384,256]{1,0:T(8,128)(2,1)S(1)} collective-permute-done((bf16[384,256]{1,0:T(8,128)(2,1)S(1)}, bf16[384,256]{1,0:T(8,128)(2,1)S(1)}, u32[]{:S(2)}, u32[]{:S(2)}) %collective-permute-start.22) | collective-permute-done | bytes 196640 | tf_op jit(solution)/shard_map/ppermute | solution.py:99
  53.1 2.4 %collective-permute-done.23.refs_3_ = bf16[384,256]{1,0:T(8,128)(2,1)S(1)} collective-permute-done((bf16[384,256]{1,0:T(8,128)(2,1)S(1)}, bf16[384,256]{1,0:T(8,128)(2,1)S(1)}, u32[]{:S(2)}, u32[]{:S(2)}) %collective-permute-start.23) | collective-permute-done | bytes 196640 | tf_op jit(solution)/shard_map/ppermute | solution.py:99
  55.4 0.6 shard_map.64
  56.1 22.9 %all_to_all.10 = f32[32,4,384]{2,1,0:T(4,128)S(1)} all-to-all(f32[32,4,384]{2,1,0:T(4,128)S(1)} %get-tuple-element.78), channel_id=1, replica_groups=mesh['far'=4,'mid'=2,'core'=2,'gy'=2] {'far','mid','core','gy'}, dimensions={0} | all-to-all | bytes 393216 | tf_op jit(solution)/shard_map/all_to_all | solution.py:501
  79.1 11.4 %all_to_all.11.gram_ref = f32[32,4,384]{2,1,0:T(4,128)S(1)} all-to-all(f32[32,4,384]{2,1,0:T(4,128)S(1)} %broadcast_in_dim.2), channel_id=1, replica_groups=mesh['far'=4,'mid'=2,'core'=2,'gy'=2] {'far','mid','core','gy'}, dimensions={0} | all-to-all | bytes 393216 | tf_op jit(solution)/shard_map/all_to_all | solution.py:502
  90.5 11.0 %shard_map.65 = (bf16[1536,256]{1,0:T(8,128)(2,1)}, f32[256,256]{1,0:T(8,128)}) custom-call(f32[32,4,384]{2,1,0:T(4,128)S(1)} %all_to_all.11.gram_ref, bf16[1536,256]{1,0:T(8,128)(2,1)S(1)} %get-tuple-element.79.rows_ref), custom_call_target="tpu_custom_call" | custom-call | tf_op jit(solution)/shard_map/pallas_call | solution.py:483
  (26 shorter events, 0.3 us)
Async XLA Ops:
  0.6 1.1 %copy-start = (bf16[6,8,32,256]{3,2,1,0:T(8,128)(2,1)S(1)}, bf16[6,8,32,256]{3,2,1,0:T(8,128)(2,1)}, u32[]{:S(2)}) copy-start(bf16[6,8,32,256]{3,2,1,0:T(8,128)(2,1)} %param.3) | copy-start | bytes 2359300
  1.8 0.7 copy-start.1
  2.5 17.2 %copy-start.2 = (bf16[3,3,256,256]{3,2,1,0:T(8,128)(2,1)S(1)}, bf16[3,3,256,256]{3,2,1,0:T(8,128)(2,1)}, u32[]{:S(2)}) copy-start(bf16[3,3,256,256]{3,2,1,0:T(8,128)(2,1)} %constant.4.clone.refs_3_) | copy-start | bytes 3538948
  3.0 8.3 %collective-permute-start = (bf16[416,256]{1,0:T(8,128)(2,1)S(1)}, bf16[416,256]{1,0:T(8,128)(2,1)S(1)}, u32[]{:S(2)}, u32[]{:S(2)}) collective-permute-start(bf16[416,256]{1,0:T(8,128)(2,1)S(1)} %get-tuple-element.43), channel_id=1, source_target_pairs={{0,1},{1,0},{4,5},{5,4},{2,3},{3,2},{6,7},{7,6},{8,9},{9,8},{12,13... | collective-permute-start | bytes 638984 | tf_op jit(solution)/shard_map/ppermute | solution.py:99
  6.1 8.2 %collective-permute-start.1 = (bf16[416,256]{1,0:T(8,128)(2,1)S(1)}, bf16[416,256]{1,0:T(8,128)(2,1)S(1)}, u32[]{:S(2)}, u32[]{:S(2)}) collective-permute-start(bf16[416,256]{1,0:T(8,128)(2,1)S(1)} %get-tuple-element.44), channel_id=1, source_target_pairs={{0,4},{1,5},{4,0},{5,1},{2,6},{3,7},{6,2},{7,3},{8,12},{9,13},{12,... | collective-permute-start | bytes 638984 | tf_op jit(solution)/shard_map/ppermute | solution.py:99
  7.5 9.6 %collective-permute-start.2 = (bf16[416,256]{1,0:T(8,128)(2,1)S(1)}, bf16[416,256]{1,0:T(8,128)(2,1)S(1)}, u32[]{:S(2)}, u32[]{:S(2)}) collective-permute-start(bf16[416,256]{1,0:T(8,128)(2,1)S(1)} %get-tuple-element.45), channel_id=1, source_target_pairs={{0,5},{1,4},{4,1},{5,0},{2,7},{3,6},{6,3},{7,2},{8,13},{9,12},{12,... | collective-permute-start | bytes 638984 | tf_op jit(solution)/shard_map/ppermute | solution.py:99
  17.3 1.8 %collective-permute-start.10 = (bf16[384,256]{1,0:T(8,128)(2,1)S(1)}, bf16[384,256]{1,0:T(8,128)(2,1)S(1)}, u32[]{:S(2)}, u32[]{:S(2)}) collective-permute-start(bf16[384,256]{1,0:T(8,128)(2,1)S(1)} %get-tuple-element.47.refs_1_.refs_3_.refs_9_), channel_id=1, source_target_pairs={{0,2},{2,0},{1,3},{3,1},{4,6},{6,4},{5,7},{7,5},{8,10},{10,8},{9,1... | collective-permute-start | bytes 589832 | tf_op jit(solution)/shard_map/ppermute | solution.py:297
  17.3 3.2 %collective-permute-start.5 = (bf16[384,256]{1,0:T(8,128)(2,1)S(1)}, bf16[384,256]{1,0:T(8,128)(2,1)S(1)}, u32[]{:S(2)}, u32[]{:S(2)}) collective-permute-start(bf16[384,256]{1,0:T(8,128)(2,1)S(1)} %get-tuple-element.51.refs_0_.refs_2_.refs_8_), channel_id=1, source_target_pairs={{0,2},{2,0},{1,3},{3,1},{4,6},{6,4},{5,7},{7,5},{8,10},{10,8},{9,1... | collective-permute-start | bytes 589832 | tf_op jit(solution)/shard_map/ppermute | solution.py:297
  17.8 2.7 %collective-permute-start.6 = (bf16[384,256]{1,0:T(8,128)(2,1)S(1)}, bf16[384,256]{1,0:T(8,128)(2,1)S(1)}, u32[]{:S(2)}, u32[]{:S(2)}) collective-permute-start(bf16[384,256]{1,0:T(8,128)(2,1)S(1)} %get-tuple-element.52.refs_1_.refs_3_.refs_9_), channel_id=1, source_target_pairs={{0,2},{2,0},{1,3},{3,1},{4,6},{6,4},{5,7},{7,5},{8,10},{10,8},{9,1... | collective-permute-start | bytes 589832 | tf_op jit(solution)/shard_map/ppermute | solution.py:297
  17.9 2.6 %collective-permute-start.9 = (bf16[384,256]{1,0:T(8,128)(2,1)S(1)}, bf16[384,256]{1,0:T(8,128)(2,1)S(1)}, u32[]{:S(2)}, u32[]{:S(2)}) collective-permute-start(bf16[384,256]{1,0:T(8,128)(2,1)S(1)} %get-tuple-element.46.refs_0_.refs_2_.refs_8_), channel_id=1, source_target_pairs={{0,2},{2,0},{1,3},{3,1},{4,6},{6,4},{5,7},{7,5},{8,10},{10,8},{9,1... | collective-permute-start | bytes 589832 | tf_op jit(solution)/shard_map/ppermute | solution.py:297
  18.3 8.0 %collective-permute-start.3 = (bf16[384,256]{1,0:T(8,128)(2,1)S(1)}, bf16[384,256]{1,0:T(8,128)(2,1)S(1)}, u32[]{:S(2)}, u32[]{:S(2)}) collective-permute-start(bf16[384,256]{1,0:T(8,128)(2,1)S(1)} %get-tuple-element.46.refs_0_.refs_2_.refs_8_), channel_id=1, source_target_pairs={{2,8},{10,16},{18,24},{8,2},{16,10},{24,18},{3,9},{11,17},{19,25},... | collective-permute-start | bytes 589832 | tf_op jit(solution)/shard_map/ppermute | solution.py:304
  19.0 7.3 %collective-permute-start.4 = (bf16[384,256]{1,0:T(8,128)(2,1)S(1)}, bf16[384,256]{1,0:T(8,128)(2,1)S(1)}, u32[]{:S(2)}, u32[]{:S(2)}) collective-permute-start(bf16[384,256]{1,0:T(8,128)(2,1)S(1)} %get-tuple-element.47.refs_1_.refs_3_.refs_9_), channel_id=1, source_target_pairs={{2,8},{10,16},{18,24},{8,2},{16,10},{24,18},{3,9},{11,17},{19,25},... | collective-permute-start | bytes 589832 | tf_op jit(solution)/shard_map/ppermute | solution.py:304
  21.1 9.4 %collective-permute-start.11 = (bf16[384,256]{1,0:T(8,128)(2,1)S(1)}, bf16[384,256]{1,0:T(8,128)(2,1)S(1)}, u32[]{:S(2)}, u32[]{:S(2)}) collective-permute-start(bf16[384,256]{1,0:T(8,128)(2,1)S(1)} %get-tuple-element.60.refs_0_.refs_2_.refs_8_), channel_id=1, source_target_pairs={{0,2},{2,0},{1,3},{3,1},{4,6},{6,4},{5,7},{7,5},{8,10},{10,8},{9,1... | collective-permute-start | bytes 589832 | tf_op jit(solution)/shard_map/ppermute | solution.py:297
  26.3 5.7 %collective-permute-start.12 = (bf16[384,256]{1,0:T(8,128)(2,1)S(1)}, bf16[384,256]{1,0:T(8,128)(2,1)S(1)}, u32[]{:S(2)}, u32[]{:S(2)}) collective-permute-start(bf16[384,256]{1,0:T(8,128)(2,1)S(1)} %get-tuple-element.61.refs_1_.refs_3_.refs_9_), channel_id=1, source_target_pairs={{0,2},{2,0},{1,3},{3,1},{4,6},{6,4},{5,7},{7,5},{8,10},{10,8},{9,1... | collective-permute-start | bytes 589832 | tf_op jit(solution)/shard_map/ppermute | solution.py:297
  27.0 5.0 %collective-permute-start.15 = (bf16[384,256]{1,0:T(8,128)(2,1)S(1)}, bf16[384,256]{1,0:T(8,128)(2,1)S(1)}, u32[]{:S(2)}, u32[]{:S(2)}) collective-permute-start(bf16[384,256]{1,0:T(8,128)(2,1)S(1)} %get-tuple-element.53.refs_0_.refs_2_.refs_8_), channel_id=1, source_target_pairs={{0,2},{2,0},{1,3},{3,1},{4,6},{6,4},{5,7},{7,5},{8,10},{10,8},{9,1... | collective-permute-start | bytes 589832 | tf_op jit(solution)/shard_map/ppermute | solution.py:297
  29.7 2.2 %collective-permute-start.16 = (bf16[384,256]{1,0:T(8,128)(2,1)S(1)}, bf16[384,256]{1,0:T(8,128)(2,1)S(1)}, u32[]{:S(2)}, u32[]{:S(2)}) collective-permute-start(bf16[384,256]{1,0:T(8,128)(2,1)S(1)} %get-tuple-element.54.refs_1_.refs_3_.refs_9_), channel_id=1, source_target_pairs={{0,2},{2,0},{1,3},{3,1},{4,6},{6,4},{5,7},{7,5},{8,10},{10,8},{9,1... | collective-permute-start | bytes 589832 | tf_op jit(solution)/shard_map/ppermute | solution.py:297
  29.8 8.4 %collective-permute-start.7 = (bf16[384,256]{1,0:T(8,128)(2,1)S(1)}, bf16[384,256]{1,0:T(8,128)(2,1)S(1)}, u32[]{:S(2)}, u32[]{:S(2)}) collective-permute-start(bf16[384,256]{1,0:T(8,128)(2,1)S(1)} %get-tuple-element.53.refs_0_.refs_2_.refs_8_), channel_id=1, source_target_pairs={{2,8},{10,16},{18,24},{8,2},{16,10},{24,18},{3,9},{11,17},{19,25},... | collective-permute-start | bytes 589832 | tf_op jit(solution)/shard_map/ppermute | solution.py:304
  30.5 7.7 %collective-permute-start.8 = (bf16[384,256]{1,0:T(8,128)(2,1)S(1)}, bf16[384,256]{1,0:T(8,128)(2,1)S(1)}, u32[]{:S(2)}, u32[]{:S(2)}) collective-permute-start(bf16[384,256]{1,0:T(8,128)(2,1)S(1)} %get-tuple-element.54.refs_1_.refs_3_.refs_9_), channel_id=1, source_target_pairs={{2,8},{10,16},{18,24},{8,2},{16,10},{24,18},{3,9},{11,17},{19,25},... | collective-permute-start | bytes 589832 | tf_op jit(solution)/shard_map/ppermute | solution.py:304
  32.6 9.2 %collective-permute-start.17 = (bf16[384,256]{1,0:T(8,128)(2,1)S(1)}, bf16[384,256]{1,0:T(8,128)(2,1)S(1)}, u32[]{:S(2)}, u32[]{:S(2)}) collective-permute-start(bf16[384,256]{1,0:T(8,128)(2,1)S(1)} %get-tuple-element.68.refs_0_.refs_2_), channel_id=1, source_target_pairs={{0,2},{2,0},{1,3},{3,1},{4,6},{6,4},{5,7},{7,5},{8,10},{10,8},{9,1... | collective-permute-start | bytes 589832 | tf_op jit(solution)/shard_map/ppermute | solution.py:297
  38.1 6.0 %collective-permute-start.18 = (bf16[384,256]{1,0:T(8,128)(2,1)S(1)}, bf16[384,256]{1,0:T(8,128)(2,1)S(1)}, u32[]{:S(2)}, u32[]{:S(2)}) collective-permute-start(bf16[384,256]{1,0:T(8,128)(2,1)S(1)} %get-tuple-element.69.refs_1_.refs_3_), channel_id=1, source_target_pairs={{0,2},{2,0},{1,3},{3,1},{4,6},{6,4},{5,7},{7,5},{8,10},{10,8},{9,1... | collective-permute-start | bytes 589832 | tf_op jit(solution)/shard_map/ppermute | solution.py:297
  38.9 5.2 %collective-permute-start.19 = (bf16[384,256]{1,0:T(8,128)(2,1)S(1)}, bf16[384,256]{1,0:T(8,128)(2,1)S(1)}, u32[]{:S(2)}, u32[]{:S(2)}) collective-permute-start(bf16[384,256]{1,0:T(8,128)(2,1)S(1)} %get-tuple-element.62.refs_0_.refs_2_), channel_id=1, source_target_pairs={{0,2},{2,0},{1,3},{3,1},{4,6},{6,4},{5,7},{7,5},{8,10},{10,8},{9,1... | collective-permute-start | bytes 589832 | tf_op jit(solution)/shard_map/ppermute | solution.py:297
  41.1 3.0 %collective-permute-start.20 = (bf16[384,256]{1,0:T(8,128)(2,1)S(1)}, bf16[384,256]{1,0:T(8,128)(2,1)S(1)}, u32[]{:S(2)}, u32[]{:S(2)}) collective-permute-start(bf16[384,256]{1,0:T(8,128)(2,1)S(1)} %get-tuple-element.63.refs_1_.refs_3_), channel_id=1, source_target_pairs={{0,2},{2,0},{1,3},{3,1},{4,6},{6,4},{5,7},{7,5},{8,10},{10,8},{9,1... | collective-permute-start | bytes 589832 | tf_op jit(solution)/shard_map/ppermute | solution.py:297
  41.2 3.6 %collective-permute-start.13 = (bf16[384,256]{1,0:T(8,128)(2,1)S(1)}, bf16[384,256]{1,0:T(8,128)(2,1)S(1)}, u32[]{:S(2)}, u32[]{:S(2)}) collective-permute-start(bf16[384,256]{1,0:T(8,128)(2,1)S(1)} %get-tuple-element.62.refs_0_.refs_2_), channel_id=1, source_target_pairs={{2,8},{10,16},{18,24},{8,2},{16,10},{24,18},{3,9},{11,17},{19,25},... | collective-permute-start | bytes 589832 | tf_op jit(solution)/shard_map/ppermute | solution.py:304
  41.9 3.0 %collective-permute-start.14 = (bf16[384,256]{1,0:T(8,128)(2,1)S(1)}, bf16[384,256]{1,0:T(8,128)(2,1)S(1)}, u32[]{:S(2)}, u32[]{:S(2)}) collective-permute-start(bf16[384,256]{1,0:T(8,128)(2,1)S(1)} %get-tuple-element.63.refs_1_.refs_3_), channel_id=1, source_target_pairs={{2,8},{10,16},{18,24},{8,2},{16,10},{24,18},{3,9},{11,17},{19,25},... | collective-permute-start | bytes 589832 | tf_op jit(solution)/shard_map/ppermute | solution.py:304
  45.8 5.7 %collective-permute-start.21 = (bf16[384,256]{1,0:T(8,128)(2,1)S(1)}, bf16[384,256]{1,0:T(8,128)(2,1)S(1)}, u32[]{:S(2)}, u32[]{:S(2)}) collective-permute-start(bf16[384,256]{1,0:T(8,128)(2,1)S(1)} %get-tuple-element.75), channel_id=1, source_target_pairs={{0,1},{1,0},{4,5},{5,4},{2,3},{3,2},{6,7},{7,6},{8,9},{9,8},{12,13... | collective-permute-start | bytes 589832 | tf_op jit(solution)/shard_map/ppermute | solution.py:99
  47.4 5.7 %collective-permute-start.22 = (bf16[384,256]{1,0:T(8,128)(2,1)S(1)}, bf16[384,256]{1,0:T(8,128)(2,1)S(1)}, u32[]{:S(2)}, u32[]{:S(2)}) collective-permute-start(bf16[384,256]{1,0:T(8,128)(2,1)S(1)} %get-tuple-element.76), channel_id=1, source_target_pairs={{0,4},{1,5},{4,0},{5,1},{2,6},{3,7},{6,2},{7,3},{8,12},{9,13},{12,... | collective-permute-start | bytes 589832 | tf_op jit(solution)/shard_map/ppermute | solution.py:99
  48.9 6.6 %collective-permute-start.23 = (bf16[384,256]{1,0:T(8,128)(2,1)S(1)}, bf16[384,256]{1,0:T(8,128)(2,1)S(1)}, u32[]{:S(2)}, u32[]{:S(2)}) collective-permute-start(bf16[384,256]{1,0:T(8,128)(2,1)S(1)} %get-tuple-element.77), channel_id=1, source_target_pairs={{0,5},{1,4},{4,1},{5,0},{2,7},{3,6},{6,3},{7,2},{8,13},{9,12},{12,... | collective-permute-start | bytes 589832 | tf_op jit(solution)/shard_map/ppermute | solution.py:99

commit v6 on v4

--- a/solution.py
+++ b/solution.py
@@ -29,7 +29,6 @@
 owned = 2
 group = 16
 vmem_limit = 48 * 1024 * 1024
-fetching_limit = 63 * 1024 * 1024
 
 center_shift = -1.5 * STENCIL_WEIGHTS[0] - filter_center
 side_weights = tuple(-0.5 * weight / filter_half for weight in STENCIL_WEIGHTS)
@@ -102,29 +101,19 @@
 
 
 def split_kernel(bricks_y, cells_ref, potential_ref, *refs):
-    sent_refs, (block_ref, fetched_ref, level_ref, arrived) = refs[:-4], refs[-4:]
+    sent_refs, block_ref = refs[:-1], refs[-1]
     mid, y = lax.axis_index("mid"), lax.axis_index("gy")
     columns, plane = block_ref.shape
     share = columns // len(sent_refs)
     layers = cells_ref.shape[0] // plane
-    fetches = [pltpu.make_async_copy(potential_ref, level_ref, arrived.at[layers])]
-    for layer in range(layers):
-        part = pl.ds(layer * plane, plane)
-        fetches.append(
-            pltpu.make_async_copy(cells_ref.at[part], fetched_ref.at[part], arrived.at[layer])
-        )
-    for fetch in fetches:
-        fetch.start()
-    fetches[0].wait()
     potential = jnp.concatenate(
-        [level_ref[:, at, :] for at in range(level_ref.shape[1])], axis=1
+        [potential_ref[:, at, :] for at in range(potential_ref.shape[1])], axis=1
     )
     extra = level_rows(potential, sent_refs[0].shape[0] - layers * share)
     for sent_ref in sent_refs:
         sent_ref[layers * share :, :] = extra
     for layer in range(layers):
-        fetches[layer + 1].wait()
-        block = fetched_ref[layer * plane : (layer + 1) * plane, :].astype(jnp.float32)
+        block = cells_ref[layer * plane : (layer + 1) * plane, :].astype(jnp.float32)
         block_ref[...] = block.T
         for step, sent_ref in zip(offsets(bricks_y), sent_refs):
             to_mid, to_y = ahead(mid, y, step, bricks_y)
@@ -143,15 +132,9 @@
     )
     return pl.pallas_call(
         functools.partial(split_kernel, bricks_y),
-        in_specs=[pl.BlockSpec(memory_space=pltpu.HBM)] * 2,
         out_shape=[message] * parts,
-        scratch_shapes=[
-            pltpu.VMEM((columns, plane), jnp.float32),
-            pltpu.VMEM((count, columns), jnp.bfloat16),
-            pltpu.VMEM(potential.shape, jnp.float32),
-            pltpu.SemaphoreType.DMA((layers + 1,)),
-        ],
-        compiler_params=pltpu.CompilerParams(vmem_limit_bytes=fetching_limit),
+        scratch_shapes=[pltpu.VMEM((columns, plane), jnp.float32)],
+        compiler_params=pltpu.CompilerParams(vmem_limit_bytes=vmem_limit),
     )(cells, potential)
 
 
@@ -385,11 +368,10 @@
     columns = list(columns)
     full = [jnp.where(row == k, 1.0, 0.0).astype(jnp.float32) for k in range(panel_rows)]
     forward = list(full)
-    pivots = jnp.zeros((panel_rows, lanes), jnp.float32)
+    scales = jnp.zeros((panel_rows, lanes), jnp.float32)
     for step in range(panel_rows):
-        pivot = row_splat(columns[step], step)
-        scale = 1.0 / pivot
-        pivots = jnp.where(row == step, pivot, pivots)
+        scale = 1.0 / row_splat(columns[step], step)
+        scales = jnp.where(row == step, scale, scales)
         others = jnp.where(row == step, 0.0, columns[step])
         for k in range(step + 1, panel_rows):
             columns[k] = columns[k] - others * (row_splat(columns[k], step) * scale)
@@ -397,23 +379,20 @@
             forward[k] = jnp.where(row == step, full[k], forward[k])
             full[k] = full[k] - others * (row_splat(full[k], step) * scale)
         full[step] = full[step] - others * scale
-    inverse_pivots = 1.0 / pivots
-    root = lax.rsqrt(pivots)
-    full = [column * inverse_pivots for column in full]
+    root = jnp.sqrt(scales)
+    full = [column * scales for column in full]
     forward = [column * root for column in forward]
     return full, forward
 
 
 def combine(columns, rows):
-    width = rows.shape[1] // lanes
     parts = []
-    for part in range(width):
-        piece = rows[:, part * lanes : (part + 1) * lanes]
-        total = None
-        for k, column in enumerate(columns):
-            term = column * row_splat(piece, k)
-            total = term if total is None else total + term
-        parts.append(total)
+    for left in range(0, rows.shape[1], lanes):
+        piece = rows[:, left : left + lanes]
+        terms = [column * row_splat(piece, k) for k, column in enumerate(columns)]
+        while len(terms) > 1:
+            terms = [a + b for a, b in zip(terms[::2], terms[1::2])]
+        parts.append(terms[0])
     return jnp.concatenate(parts, axis=1)
 
 

time: 99.4 us -> 98 us (0.986)
  Pallas kernels: 23.2 us -> 20.9 us
  starting transfers between devices: 22.2 us -> 23.4 us
    pallas_call x1, Pallas kernels: 2.74 us -> 0.51 us  [split_columns(): pl.pallas_call(functools.partial(split_kernel, bricks_y), out_shape=[mess...]
    ppermute x6, starting transfers between devices: 12 us -> 13.3 us  [from_other_core(): return lax.ppermute(own, 'core', [(0, 1), (1, 0)])]
where the time goes in v6:
time: 98 us; the launch traced here: 97.7 us
  blocking collectives  34.8 us (36%)
  starting transfers between devices  23.4 us (24%)
  Pallas kernels  20.9 us (21%)
  waiting for transfers between devices  15.7 us (16%)
  local copies, waits for them, and re-layouts  1.99 us (2%)
    all_to_all x1, blocking collectives, sum_over_devices(): total = jnp.sum(lax.all_to_all(values, axes, 0, 0), axis=0)  23.4 us
    ppermute x6, waiting for transfers between devices, exchange(): result.append(lax.ppermute(message, ('mid', 'gy'), perm))  15.7 us
    ppermute x6, starting transfers between devices, from_other_core(): return lax.ppermute(own, 'core', [(0, 1), (1, 0)])  13.3 us
    all_to_all x1, blocking collectives, sum_over_devices(): lax.all_to_all(jnp.broadcast_to(total[None], values.shape), axes, 0, 0)  11.4 us
    pallas_call x1, Pallas kernels, factor_and_rotate(): pl.pallas_call(functools.partial(factor_kernel, math.sqrt(total_cells)),...  11 us
    ppermute x6, starting transfers between devices, exchange(): result.append(lax.ppermute(message, ('mid', 'gy'), perm))  8.13 us
    pallas_call x6, Pallas kernels, plane_part(): pl.pallas_call(plane_kernel, out_shape=jax.ShapeDtypeStruct(own.shape, jn...  4.63 us
    pallas_call x6, Pallas kernels, layer_part(): pl.pallas_call(functools.partial(layer_kernel, before is None, layers, pa...  4.02 us
  transfers between devices with their start and end apart: 15, of which 6 were waited for; matrix products, arithmetic and copies ran while one was open for 0% of the time, Pallas kernels for 8%

profile of v6, /device:TPU:0, one launch (start us, length us, event | category | flops | bytes accessed | tf_op | source)
XLA Modules:
  0.0 97.7 jit_solution(17464384963010675177)
XLA Ops:
  0.6 0.0 copy-start
  0.7 1.2 %copy-done.1 = bf16[6,8,32,256]{3,2,1,0:T(8,128)(2,1)S(1)} copy-done((bf16[6,8,32,256]{3,2,1,0:T(8,128)(2,1)S(1)}, bf16[6,8,32,256]{3,2,1,0:T(8,128)(2,1)}, u32[]{:S(2)}) %copy-start.1) | copy-done | bytes 786456
  1.9 0.7 copy-done.2
  2.6 0.5 shard_map.50
  3.1 3.0 %collective-permute-start = (bf16[416,256]{1,0:T(8,128)(2,1)S(1)}, bf16[416,256]{1,0:T(8,128)(2,1)S(1)}, u32[]{:S(2)}, u32[]{:S(2)}) collective-permute-start(bf16[416,256]{1,0:T(8,128)(2,1)S(1)} %get-tuple-element.19), channel_id=1, source_target_pairs={{0,1},{1,0},{4,5},{5,4},{2,3},{3,2},{6,7},{7,6},{8,9},{9,8},{12,13... | collective-permute-start | bytes 638984 | tf_op jit(solution)/shard_map/ppermute | solution.py:99
  6.2 1.5 %collective-permute-start.1 = (bf16[416,256]{1,0:T(8,128)(2,1)S(1)}, bf16[416,256]{1,0:T(8,128)(2,1)S(1)}, u32[]{:S(2)}, u32[]{:S(2)}) collective-permute-start(bf16[416,256]{1,0:T(8,128)(2,1)S(1)} %get-tuple-element.20), channel_id=1, source_target_pairs={{0,4},{1,5},{4,0},{5,1},{2,6},{3,7},{6,2},{7,3},{8,12},{9,13},{12,... | collective-permute-start | bytes 638984 | tf_op jit(solution)/shard_map/ppermute | solution.py:99
  7.7 0.0 collective-permute-start.2
  7.7 3.7 %collective-permute-done.refs_1_ = bf16[416,256]{1,0:T(8,128)(2,1)S(1)} collective-permute-done((bf16[416,256]{1,0:T(8,128)(2,1)S(1)}, bf16[416,256]{1,0:T(8,128)(2,1)S(1)}, u32[]{:S(2)}, u32[]{:S(2)}) %collective-permute-start) | collective-permute-done | bytes 213024 | tf_op jit(solution)/shard_map/ppermute | solution.py:99
  11.4 2.9 %collective-permute-done.1.refs_2_ = bf16[416,256]{1,0:T(8,128)(2,1)S(1)} collective-permute-done((bf16[416,256]{1,0:T(8,128)(2,1)S(1)}, bf16[416,256]{1,0:T(8,128)(2,1)S(1)}, u32[]{:S(2)}, u32[]{:S(2)}) %collective-permute-start.1) | collective-permute-done | bytes 213024 | tf_op jit(solution)/shard_map/ppermute | solution.py:99
  14.3 2.9 %collective-permute-done.2.refs_3_ = bf16[416,256]{1,0:T(8,128)(2,1)S(1)} collective-permute-done((bf16[416,256]{1,0:T(8,128)(2,1)S(1)}, bf16[416,256]{1,0:T(8,128)(2,1)S(1)}, u32[]{:S(2)}, u32[]{:S(2)}) %collective-permute-start.2) | collective-permute-done | bytes 213024 | tf_op jit(solution)/shard_map/ppermute | solution.py:99
  17.2 0.1 shard_map.51
  17.4 0.1 collective-permute-start.4
  17.4 0.5 collective-permute-start.6
  17.9 0.7 collective-permute-start.3
  18.6 0.8 shard_map.55.partial_ref
  19.4 0.8 shard_map.52.partial_ref
  20.2 0.0 collective-permute-done.4.other_ref.outer_ref
  20.2 0.0 collective-permute-done.6.other_ref
  20.2 0.6 shard_map.56.own_ref.refs_0_
  20.8 3.1 %collective-permute-start.7 = (bf16[2,384,256]{2,1,0:T(8,128)(2,1)S(1)}, bf16[2,384,256]{2,1,0:T(8,128)(2,1)S(1)}, u32[]{:S(2)}, u32[]{:S(2)}) collective-permute-start(bf16[2,384,256]{2,1,0:T(8,128)(2,1)S(1)} %shard_map.56.own_ref.refs_0_), channel_id=1, source_target_pairs={{0,2},{2,0},{1,3},{3,1},{4,6},{6,4},{5,7},{7,5},{8,10},{10,8},{9,1... | collective-permute-start | bytes 1179656 | tf_op jit(solution)/shard_map/ppermute | solution.py:283
  23.9 0.0 collective-permute-done.3.outer_ref
  23.9 0.6 shard_map.53.own_ref.refs_0_
  24.5 3.3 %collective-permute-start.9 = (bf16[2,384,256]{2,1,0:T(8,128)(2,1)S(1)}, bf16[2,384,256]{2,1,0:T(8,128)(2,1)S(1)}, u32[]{:S(2)}, u32[]{:S(2)}) collective-permute-start(bf16[2,384,256]{2,1,0:T(8,128)(2,1)S(1)} %shard_map.53.own_ref.refs_0_), channel_id=1, source_target_pairs={{0,2},{2,0},{1,3},{3,1},{4,6},{6,4},{5,7},{7,5},{8,10},{10,8},{9,1... | collective-permute-start | bytes 1179656 | tf_op jit(solution)/shard_map/ppermute | solution.py:283
  27.8 0.7 collective-permute-start.5
  28.4 0.8 shard_map.59.partial_ref
  29.2 0.8 shard_map.54.partial_ref
  30.0 0.0 collective-permute-done.7.other_ref.outer_ref
  30.0 0.7 shard_map.60.own_ref
  30.7 3.1 %collective-permute-start.10 = (bf16[2,384,256]{2,1,0:T(8,128)(2,1)S(1)}, bf16[2,384,256]{2,1,0:T(8,128)(2,1)S(1)}, u32[]{:S(2)}, u32[]{:S(2)}) collective-permute-start(bf16[2,384,256]{2,1,0:T(8,128)(2,1)S(1)} %shard_map.60.own_ref), channel_id=1, source_target_pairs={{0,2},{2,0},{1,3},{3,1},{4,6},{6,4},{5,7},{7,5},{8,10},{10,8},{9,1... | collective-permute-start | bytes 1179656 | tf_op jit(solution)/shard_map/ppermute | solution.py:283
  33.8 0.6 shard_map.57.own_ref
  34.5 3.2 %collective-permute-start.11 = (bf16[2,384,256]{2,1,0:T(8,128)(2,1)S(1)}, bf16[2,384,256]{2,1,0:T(8,128)(2,1)S(1)}, u32[]{:S(2)}, u32[]{:S(2)}) collective-permute-start(bf16[2,384,256]{2,1,0:T(8,128)(2,1)S(1)} %shard_map.57.own_ref), channel_id=1, source_target_pairs={{0,2},{2,0},{1,3},{3,1},{4,6},{6,4},{5,7},{7,5},{8,10},{10,8},{9,1... | collective-permute-start | bytes 1179656 | tf_op jit(solution)/shard_map/ppermute | solution.py:283
  37.7 0.7 collective-permute-start.8
  38.3 0.8 shard_map.61.partial_ref
  39.1 0.8 shard_map.58.partial_ref
  39.9 0.0 collective-permute-done.10.outer_ref.other_ref
  39.9 0.7 shard_map.62.refs_1_
  40.6 0.9 shard_map.63
  41.5 1.6 %collective-permute-start.12 = (bf16[384,256]{1,0:T(8,128)(2,1)S(1)}, bf16[384,256]{1,0:T(8,128)(2,1)S(1)}, u32[]{:S(2)}, u32[]{:S(2)}) collective-permute-start(bf16[384,256]{1,0:T(8,128)(2,1)S(1)} %get-tuple-element.27), channel_id=1, source_target_pairs={{0,1},{1,0},{4,5},{5,4},{2,3},{3,2},{6,7},{7,6},{8,9},{9,8},{12,13... | collective-permute-start | bytes 589832 | tf_op jit(solution)/shard_map/ppermute | solution.py:99
  43.1 1.5 %collective-permute-start.13 = (bf16[384,256]{1,0:T(8,128)(2,1)S(1)}, bf16[384,256]{1,0:T(8,128)(2,1)S(1)}, u32[]{:S(2)}, u32[]{:S(2)}) collective-permute-start(bf16[384,256]{1,0:T(8,128)(2,1)S(1)} %get-tuple-element.28), channel_id=1, source_target_pairs={{0,4},{1,5},{4,0},{5,1},{2,6},{3,7},{6,2},{7,3},{8,12},{9,13},{12,... | collective-permute-start | bytes 589832 | tf_op jit(solution)/shard_map/ppermute | solution.py:99
  44.6 0.4 collective-permute-start.14
  45.1 2.2 %collective-permute-done.12.refs_1_ = bf16[384,256]{1,0:T(8,128)(2,1)S(1)} collective-permute-done((bf16[384,256]{1,0:T(8,128)(2,1)S(1)}, bf16[384,256]{1,0:T(8,128)(2,1)S(1)}, u32[]{:S(2)}, u32[]{:S(2)}) %collective-permute-start.12) | collective-permute-done | bytes 196640 | tf_op jit(solution)/shard_map/ppermute | solution.py:99
  47.3 1.6 %collective-permute-done.13.refs_2_ = bf16[384,256]{1,0:T(8,128)(2,1)S(1)} collective-permute-done((bf16[384,256]{1,0:T(8,128)(2,1)S(1)}, bf16[384,256]{1,0:T(8,128)(2,1)S(1)}, u32[]{:S(2)}, u32[]{:S(2)}) %collective-permute-start.13) | collective-permute-done | bytes 196640 | tf_op jit(solution)/shard_map/ppermute | solution.py:99
  48.8 2.4 %collective-permute-done.14.refs_3_ = bf16[384,256]{1,0:T(8,128)(2,1)S(1)} collective-permute-done((bf16[384,256]{1,0:T(8,128)(2,1)S(1)}, bf16[384,256]{1,0:T(8,128)(2,1)S(1)}, u32[]{:S(2)}, u32[]{:S(2)}) %collective-permute-start.14) | collective-permute-done | bytes 196640 | tf_op jit(solution)/shard_map/ppermute | solution.py:99
  51.2 0.6 shard_map.64
  51.9 23.4 %all_to_all.10 = f32[32,4,384]{2,1,0:T(4,128)S(1)} all-to-all(f32[32,4,384]{2,1,0:T(4,128)S(1)} %get-tuple-element.30), channel_id=1, replica_groups=mesh['far'=4,'mid'=2,'core'=2,'gy'=2] {'far','mid','core','gy'}, dimensions={0} | all-to-all | bytes 393216 | tf_op jit(solution)/shard_map/all_to_all | solution.py:486
  75.3 0.1 reduce_sum.9
  75.3 11.4 %all_to_all.11.gram_ref = f32[32,4,384]{2,1,0:T(4,128)S(1)} all-to-all(f32[32,4,384]{2,1,0:T(4,128)S(1)} %broadcast_in_dim.2), channel_id=1, replica_groups=mesh['far'=4,'mid'=2,'core'=2,'gy'=2] {'far','mid','core','gy'}, dimensions={0} | all-to-all | bytes 393216 | tf_op jit(solution)/shard_map/all_to_all | solution.py:487
  86.8 11.0 %shard_map.65 = (bf16[1536,256]{1,0:T(8,128)(2,1)}, f32[256,256]{1,0:T(8,128)}) custom-call(f32[32,4,384]{2,1,0:T(4,128)S(1)} %all_to_all.11.gram_ref, bf16[1536,256]{1,0:T(8,128)(2,1)S(1)} %get-tuple-element.31.rows_ref), custom_call_target="tpu_custom_call" | custom-call | tf_op jit(solution)/shard_map/pallas_call | solution.py:468
  (8 shorter events, 0.0 us)
Async XLA Ops:
  0.6 18.0 %copy-start = (bf16[3,3,256,256]{3,2,1,0:T(8,128)(2,1)S(1)}, bf16[3,3,256,256]{3,2,1,0:T(8,128)(2,1)}, u32[]{:S(2)}) copy-start(bf16[3,3,256,256]{3,2,1,0:T(8,128)(2,1)} %constant.4.clone.weights_ref) | copy-start | bytes 3538948
  0.6 1.2 %copy-start.1 = (bf16[6,8,32,256]{3,2,1,0:T(8,128)(2,1)S(1)}, bf16[6,8,32,256]{3,2,1,0:T(8,128)(2,1)}, u32[]{:S(2)}) copy-start(bf16[6,8,32,256]{3,2,1,0:T(8,128)(2,1)} %param.3) | copy-start | bytes 2359300
  1.9 0.7 copy-start.2
  3.1 8.3 %collective-permute-start = (bf16[416,256]{1,0:T(8,128)(2,1)S(1)}, bf16[416,256]{1,0:T(8,128)(2,1)S(1)}, u32[]{:S(2)}, u32[]{:S(2)}) collective-permute-start(bf16[416,256]{1,0:T(8,128)(2,1)S(1)} %get-tuple-element.19), channel_id=1, source_target_pairs={{0,1},{1,0},{4,5},{5,4},{2,3},{3,2},{6,7},{7,6},{8,9},{9,8},{12,13... | collective-permute-start | bytes 638984 | tf_op jit(solution)/shard_map/ppermute | solution.py:99
  6.2 8.2 %collective-permute-start.1 = (bf16[416,256]{1,0:T(8,128)(2,1)S(1)}, bf16[416,256]{1,0:T(8,128)(2,1)S(1)}, u32[]{:S(2)}, u32[]{:S(2)}) collective-permute-start(bf16[416,256]{1,0:T(8,128)(2,1)S(1)} %get-tuple-element.20), channel_id=1, source_target_pairs={{0,4},{1,5},{4,0},{5,1},{2,6},{3,7},{6,2},{7,3},{8,12},{9,13},{12,... | collective-permute-start | bytes 638984 | tf_op jit(solution)/shard_map/ppermute | solution.py:99
  7.7 9.6 %collective-permute-start.2 = (bf16[416,256]{1,0:T(8,128)(2,1)S(1)}, bf16[416,256]{1,0:T(8,128)(2,1)S(1)}, u32[]{:S(2)}, u32[]{:S(2)}) collective-permute-start(bf16[416,256]{1,0:T(8,128)(2,1)S(1)} %get-tuple-element.21), channel_id=1, source_target_pairs={{0,5},{1,4},{4,1},{5,0},{2,7},{3,6},{6,3},{7,2},{8,13},{9,12},{12,... | collective-permute-start | bytes 638984 | tf_op jit(solution)/shard_map/ppermute | solution.py:99
  17.4 2.8 %collective-permute-start.4 = (bf16[2,384,256]{2,1,0:T(8,128)(2,1)S(1)}, bf16[2,384,256]{2,1,0:T(8,128)(2,1)S(1)}, u32[]{:S(2)}, u32[]{:S(2)}) collective-permute-start(bf16[2,384,256]{2,1,0:T(8,128)(2,1)S(1)} %get-tuple-element.24.own_ref.refs_0_), channel_id=1, source_target_pairs={{0,2},{2,0},{1,3},{3,1},{4,6},{6,4},{5,7},{7,5},{8,10},{10,8},{9,1... | collective-permute-start | bytes 1179656 | tf_op jit(solution)/shard_map/ppermute | solution.py:283
  17.4 2.8 %collective-permute-start.6 = (bf16[2,384,256]{2,1,0:T(8,128)(2,1)S(1)}, bf16[2,384,256]{2,1,0:T(8,128)(2,1)S(1)}, u32[]{:S(2)}, u32[]{:S(2)}) collective-permute-start(bf16[2,384,256]{2,1,0:T(8,128)(2,1)S(1)} %get-tuple-element.22.own_ref.refs_0_), channel_id=1, source_target_pairs={{0,2},{2,0},{1,3},{3,1},{4,6},{6,4},{5,7},{7,5},{8,10},{10,8},{9,1... | collective-permute-start | bytes 1179656 | tf_op jit(solution)/shard_map/ppermute | solution.py:283
  17.9 6.0 %collective-permute-start.3 = (bf16[2,384,256]{2,1,0:T(8,128)(2,1)S(1)}, bf16[2,384,256]{2,1,0:T(8,128)(2,1)S(1)}, u32[]{:S(2)}, u32[]{:S(2)}) collective-permute-start(bf16[2,384,256]{2,1,0:T(8,128)(2,1)S(1)} %get-tuple-element.22.own_ref.refs_0_), channel_id=1, source_target_pairs={{2,8},{10,16},{18,24},{8,2},{16,10},{24,18},{3,9},{11,17},{19,25},... | collective-permute-start | bytes 1179656 | tf_op jit(solution)/shard_map/ppermute | solution.py:289
  20.8 9.2 %collective-permute-start.7 = (bf16[2,384,256]{2,1,0:T(8,128)(2,1)S(1)}, bf16[2,384,256]{2,1,0:T(8,128)(2,1)S(1)}, u32[]{:S(2)}, u32[]{:S(2)}) collective-permute-start(bf16[2,384,256]{2,1,0:T(8,128)(2,1)S(1)} %shard_map.56.own_ref.refs_0_), channel_id=1, source_target_pairs={{0,2},{2,0},{1,3},{3,1},{4,6},{6,4},{5,7},{7,5},{8,10},{10,8},{9,1... | collective-permute-start | bytes 1179656 | tf_op jit(solution)/shard_map/ppermute | solution.py:283
  24.5 5.5 %collective-permute-start.9 = (bf16[2,384,256]{2,1,0:T(8,128)(2,1)S(1)}, bf16[2,384,256]{2,1,0:T(8,128)(2,1)S(1)}, u32[]{:S(2)}, u32[]{:S(2)}) collective-permute-start(bf16[2,384,256]{2,1,0:T(8,128)(2,1)S(1)} %shard_map.53.own_ref.refs_0_), channel_id=1, source_target_pairs={{0,2},{2,0},{1,3},{3,1},{4,6},{6,4},{5,7},{7,5},{8,10},{10,8},{9,1... | collective-permute-start | bytes 1179656 | tf_op jit(solution)/shard_map/ppermute | solution.py:283
  27.8 6.1 %collective-permute-start.5 = (bf16[2,384,256]{2,1,0:T(8,128)(2,1)S(1)}, bf16[2,384,256]{2,1,0:T(8,128)(2,1)S(1)}, u32[]{:S(2)}, u32[]{:S(2)}) collective-permute-start(bf16[2,384,256]{2,1,0:T(8,128)(2,1)S(1)} %shard_map.53.own_ref.refs_0_), channel_id=1, source_target_pairs={{2,8},{10,16},{18,24},{8,2},{16,10},{24,18},{3,9},{11,17},{19,25},... | collective-permute-start | bytes 1179656 | tf_op jit(solution)/shard_map/ppermute | solution.py:289
  30.7 9.2 %collective-permute-start.10 = (bf16[2,384,256]{2,1,0:T(8,128)(2,1)S(1)}, bf16[2,384,256]{2,1,0:T(8,128)(2,1)S(1)}, u32[]{:S(2)}, u32[]{:S(2)}) collective-permute-start(bf16[2,384,256]{2,1,0:T(8,128)(2,1)S(1)} %shard_map.60.own_ref), channel_id=1, source_target_pairs={{0,2},{2,0},{1,3},{3,1},{4,6},{6,4},{5,7},{7,5},{8,10},{10,8},{9,1... | collective-permute-start | bytes 1179656 | tf_op jit(solution)/shard_map/ppermute | solution.py:283
  34.5 5.4 %collective-permute-start.11 = (bf16[2,384,256]{2,1,0:T(8,128)(2,1)S(1)}, bf16[2,384,256]{2,1,0:T(8,128)(2,1)S(1)}, u32[]{:S(2)}, u32[]{:S(2)}) collective-permute-start(bf16[2,384,256]{2,1,0:T(8,128)(2,1)S(1)} %shard_map.57.own_ref), channel_id=1, source_target_pairs={{0,2},{2,0},{1,3},{3,1},{4,6},{6,4},{5,7},{7,5},{8,10},{10,8},{9,1... | collective-permute-start | bytes 1179656 | tf_op jit(solution)/shard_map/ppermute | solution.py:283
  37.7 2.9 %collective-permute-start.8 = (bf16[2,384,256]{2,1,0:T(8,128)(2,1)S(1)}, bf16[2,384,256]{2,1,0:T(8,128)(2,1)S(1)}, u32[]{:S(2)}, u32[]{:S(2)}) collective-permute-start(bf16[2,384,256]{2,1,0:T(8,128)(2,1)S(1)} %shard_map.57.own_ref), channel_id=1, source_target_pairs={{2,8},{10,16},{18,24},{8,2},{16,10},{24,18},{3,9},{11,17},{19,25},... | collective-permute-start | bytes 1179656 | tf_op jit(solution)/shard_map/ppermute | solution.py:289
  41.5 5.7 %collective-permute-start.12 = (bf16[384,256]{1,0:T(8,128)(2,1)S(1)}, bf16[384,256]{1,0:T(8,128)(2,1)S(1)}, u32[]{:S(2)}, u32[]{:S(2)}) collective-permute-start(bf16[384,256]{1,0:T(8,128)(2,1)S(1)} %get-tuple-element.27), channel_id=1, source_target_pairs={{0,1},{1,0},{4,5},{5,4},{2,3},{3,2},{6,7},{7,6},{8,9},{9,8},{12,13... | collective-permute-start | bytes 589832 | tf_op jit(solution)/shard_map/ppermute | solution.py:99
  43.1 5.7 %collective-permute-start.13 = (bf16[384,256]{1,0:T(8,128)(2,1)S(1)}, bf16[384,256]{1,0:T(8,128)(2,1)S(1)}, u32[]{:S(2)}, u32[]{:S(2)}) collective-permute-start(bf16[384,256]{1,0:T(8,128)(2,1)S(1)} %get-tuple-element.28), channel_id=1, source_target_pairs={{0,4},{1,5},{4,0},{5,1},{2,6},{3,7},{6,2},{7,3},{8,12},{9,13},{12,... | collective-permute-start | bytes 589832 | tf_op jit(solution)/shard_map/ppermute | solution.py:99
  44.6 6.6 %collective-permute-start.14 = (bf16[384,256]{1,0:T(8,128)(2,1)S(1)}, bf16[384,256]{1,0:T(8,128)(2,1)S(1)}, u32[]{:S(2)}, u32[]{:S(2)}) collective-permute-start(bf16[384,256]{1,0:T(8,128)(2,1)S(1)} %get-tuple-element.29), channel_id=1, source_target_pairs={{0,5},{1,4},{4,1},{5,0},{2,7},{3,6},{6,3},{7,2},{8,13},{9,12},{12,... | collective-permute-start | bytes 589832 | tf_op jit(solution)/shard_map/ppermute | solution.py:99

commit v7 on v6

--- a/solution.py
+++ b/solution.py
@@ -364,21 +364,34 @@
 
 
 def panel_inverse(columns):
+    size = range(panel_rows)
+    entry = {(i, k): row_splat(columns[k], i) for k in size for i in range(k + 1)}
+    scale, multiplier, unit = {}, {}, {}
+    for step in size:
+        scale[step] = 1.0 / entry[step, step]
+        for k in range(step + 1, panel_rows):
+            multiplier[step, k] = entry[step, k] * scale[step]
+            for i in range(step + 1, k + 1):
+                entry[i, k] = entry[i, k] - entry[step, k] * multiplier[step, i]
+        for k in range(step):
+            total = multiplier[k, step]
+            for between in range(k + 1, step):
+                total = total + multiplier[between, step] * unit[between, k]
+            unit[step, k] = -total
     row = lax.broadcasted_iota(jnp.int32, (panel_rows, lanes), 0)
     columns = list(columns)
-    full = [jnp.where(row == k, 1.0, 0.0).astype(jnp.float32) for k in range(panel_rows)]
+    full = [jnp.where(row == k, 1.0, 0.0).astype(jnp.float32) for k in size]
     forward = list(full)
-    scales = jnp.zeros((panel_rows, lanes), jnp.float32)
-    for step in range(panel_rows):
-        scale = 1.0 / row_splat(columns[step], step)
-        scales = jnp.where(row == step, scale, scales)
+    scales = scale[0]
+    for step in size:
         others = jnp.where(row == step, 0.0, columns[step])
+        scales = jnp.where(row == step, scale[step], scales)
         for k in range(step + 1, panel_rows):
-            columns[k] = columns[k] - others * (row_splat(columns[k], step) * scale)
+            columns[k] = columns[k] - others * multiplier[step, k]
         for k in range(step):
-            forward[k] = jnp.where(row == step, full[k], forward[k])
-            full[k] = full[k] - others * (row_splat(full[k], step) * scale)
-        full[step] = full[step] - others * scale
+            forward[k] = jnp.where(row == step, unit[step, k], forward[k])
+            full[k] = full[k] - others * (unit[step, k] * scale[step])
+        full[step] = full[step] - others * scale[step]
     root = jnp.sqrt(scales)
     full = [column * scales for column in full]
     forward = [column * root for column in forward]

time: 98 us -> 98.7 us (level)
  no operation moved by 1% of the time
where the time goes in v7:
time: 98.7 us; the launch traced here: 98.4 us
  blocking collectives  34.8 us (35%)
  starting transfers between devices  23.4 us (24%)
  Pallas kernels  21.6 us (22%)
  waiting for transfers between devices  15.7 us (16%)
  local copies, waits for them, and re-layouts  1.99 us (2%)
    all_to_all x1, blocking collectives, sum_over_devices(): total = jnp.sum(lax.all_to_all(values, axes, 0, 0), axis=0)  23.4 us
    ppermute x6, waiting for transfers between devices, exchange(): result.append(lax.ppermute(message, ('mid', 'gy'), perm))  15.7 us
    ppermute x6, starting transfers between devices, from_other_core(): return lax.ppermute(own, 'core', [(0, 1), (1, 0)])  13.3 us
    pallas_call x1, Pallas kernels, factor_and_rotate(): pl.pallas_call(functools.partial(factor_kernel, math.sqrt(total_cells)),...  11.7 us
    all_to_all x1, blocking collectives, sum_over_devices(): lax.all_to_all(jnp.broadcast_to(total[None], values.shape), axes, 0, 0)  11.4 us
    ppermute x6, starting transfers between devices, exchange(): result.append(lax.ppermute(message, ('mid', 'gy'), perm))  8.13 us
    pallas_call x6, Pallas kernels, plane_part(): pl.pallas_call(plane_kernel, out_shape=jax.ShapeDtypeStruct(own.shape, jn...  4.63 us
    pallas_call x6, Pallas kernels, layer_part(): pl.pallas_call(functools.partial(layer_kernel, before is None, layers, pa...  4.02 us
  transfers between devices with their start and end apart: 15, of which 6 were waited for; matrix products, arithmetic and copies ran while one was open for 0% of the time, Pallas kernels for 8%

profile of v7, /device:TPU:0, one launch (start us, length us, event | category | flops | bytes accessed | tf_op | source)
XLA Modules:
  0.0 98.4 jit_solution(17750607765219689360)
XLA Ops:
  0.6 0.0 copy-start
  0.7 1.2 %copy-done.1 = bf16[6,8,32,256]{3,2,1,0:T(8,128)(2,1)S(1)} copy-done((bf16[6,8,32,256]{3,2,1,0:T(8,128)(2,1)S(1)}, bf16[6,8,32,256]{3,2,1,0:T(8,128)(2,1)}, u32[]{:S(2)}) %copy-start.1) | copy-done | bytes 786456
  1.9 0.7 copy-done.2
  2.6 0.5 shard_map.50
  3.1 3.0 %collective-permute-start = (bf16[416,256]{1,0:T(8,128)(2,1)S(1)}, bf16[416,256]{1,0:T(8,128)(2,1)S(1)}, u32[]{:S(2)}, u32[]{:S(2)}) collective-permute-start(bf16[416,256]{1,0:T(8,128)(2,1)S(1)} %get-tuple-element.19), channel_id=1, source_target_pairs={{0,1},{1,0},{4,5},{5,4},{2,3},{3,2},{6,7},{7,6},{8,9},{9,8},{12,13... | collective-permute-start | bytes 638984 | tf_op jit(solution)/shard_map/ppermute | solution.py:99
  6.2 1.5 %collective-permute-start.1 = (bf16[416,256]{1,0:T(8,128)(2,1)S(1)}, bf16[416,256]{1,0:T(8,128)(2,1)S(1)}, u32[]{:S(2)}, u32[]{:S(2)}) collective-permute-start(bf16[416,256]{1,0:T(8,128)(2,1)S(1)} %get-tuple-element.20), channel_id=1, source_target_pairs={{0,4},{1,5},{4,0},{5,1},{2,6},{3,7},{6,2},{7,3},{8,12},{9,13},{12,... | collective-permute-start | bytes 638984 | tf_op jit(solution)/shard_map/ppermute | solution.py:99
  7.7 0.0 collective-permute-start.2
  7.7 3.7 %collective-permute-done.refs_1_ = bf16[416,256]{1,0:T(8,128)(2,1)S(1)} collective-permute-done((bf16[416,256]{1,0:T(8,128)(2,1)S(1)}, bf16[416,256]{1,0:T(8,128)(2,1)S(1)}, u32[]{:S(2)}, u32[]{:S(2)}) %collective-permute-start) | collective-permute-done | bytes 213024 | tf_op jit(solution)/shard_map/ppermute | solution.py:99
  11.4 2.9 %collective-permute-done.1.refs_2_ = bf16[416,256]{1,0:T(8,128)(2,1)S(1)} collective-permute-done((bf16[416,256]{1,0:T(8,128)(2,1)S(1)}, bf16[416,256]{1,0:T(8,128)(2,1)S(1)}, u32[]{:S(2)}, u32[]{:S(2)}) %collective-permute-start.1) | collective-permute-done | bytes 213024 | tf_op jit(solution)/shard_map/ppermute | solution.py:99
  14.3 2.9 %collective-permute-done.2.refs_3_ = bf16[416,256]{1,0:T(8,128)(2,1)S(1)} collective-permute-done((bf16[416,256]{1,0:T(8,128)(2,1)S(1)}, bf16[416,256]{1,0:T(8,128)(2,1)S(1)}, u32[]{:S(2)}, u32[]{:S(2)}) %collective-permute-start.2) | collective-permute-done | bytes 213024 | tf_op jit(solution)/shard_map/ppermute | solution.py:99
  17.2 0.1 shard_map.51
  17.4 0.1 collective-permute-start.4
  17.4 0.5 collective-permute-start.6
  17.9 0.7 collective-permute-start.3
  18.6 0.8 shard_map.55.partial_ref
  19.4 0.8 shard_map.52.partial_ref
  20.2 0.0 collective-permute-done.4.other_ref.outer_ref
  20.2 0.0 collective-permute-done.6.other_ref
  20.2 0.6 shard_map.56.own_ref.refs_0_
  20.8 3.1 %collective-permute-start.7 = (bf16[2,384,256]{2,1,0:T(8,128)(2,1)S(1)}, bf16[2,384,256]{2,1,0:T(8,128)(2,1)S(1)}, u32[]{:S(2)}, u32[]{:S(2)}) collective-permute-start(bf16[2,384,256]{2,1,0:T(8,128)(2,1)S(1)} %shard_map.56.own_ref.refs_0_), channel_id=1, source_target_pairs={{0,2},{2,0},{1,3},{3,1},{4,6},{6,4},{5,7},{7,5},{8,10},{10,8},{9,1... | collective-permute-start | bytes 1179656 | tf_op jit(solution)/shard_map/ppermute | solution.py:283
  23.9 0.0 collective-permute-done.3.outer_ref
  23.9 0.6 shard_map.53.own_ref.refs_0_
  24.5 3.3 %collective-permute-start.9 = (bf16[2,384,256]{2,1,0:T(8,128)(2,1)S(1)}, bf16[2,384,256]{2,1,0:T(8,128)(2,1)S(1)}, u32[]{:S(2)}, u32[]{:S(2)}) collective-permute-start(bf16[2,384,256]{2,1,0:T(8,128)(2,1)S(1)} %shard_map.53.own_ref.refs_0_), channel_id=1, source_target_pairs={{0,2},{2,0},{1,3},{3,1},{4,6},{6,4},{5,7},{7,5},{8,10},{10,8},{9,1... | collective-permute-start | bytes 1179656 | tf_op jit(solution)/shard_map/ppermute | solution.py:283
  27.8 0.7 collective-permute-start.5
  28.4 0.8 shard_map.59.partial_ref
  29.2 0.8 shard_map.54.partial_ref
  30.0 0.0 collective-permute-done.7.other_ref.outer_ref
  30.0 0.7 shard_map.60.own_ref
  30.7 3.1 %collective-permute-start.10 = (bf16[2,384,256]{2,1,0:T(8,128)(2,1)S(1)}, bf16[2,384,256]{2,1,0:T(8,128)(2,1)S(1)}, u32[]{:S(2)}, u32[]{:S(2)}) collective-permute-start(bf16[2,384,256]{2,1,0:T(8,128)(2,1)S(1)} %shard_map.60.own_ref), channel_id=1, source_target_pairs={{0,2},{2,0},{1,3},{3,1},{4,6},{6,4},{5,7},{7,5},{8,10},{10,8},{9,1... | collective-permute-start | bytes 1179656 | tf_op jit(solution)/shard_map/ppermute | solution.py:283
  33.8 0.6 shard_map.57.own_ref
  34.5 3.2 %collective-permute-start.11 = (bf16[2,384,256]{2,1,0:T(8,128)(2,1)S(1)}, bf16[2,384,256]{2,1,0:T(8,128)(2,1)S(1)}, u32[]{:S(2)}, u32[]{:S(2)}) collective-permute-start(bf16[2,384,256]{2,1,0:T(8,128)(2,1)S(1)} %shard_map.57.own_ref), channel_id=1, source_target_pairs={{0,2},{2,0},{1,3},{3,1},{4,6},{6,4},{5,7},{7,5},{8,10},{10,8},{9,1... | collective-permute-start | bytes 1179656 | tf_op jit(solution)/shard_map/ppermute | solution.py:283
  37.7 0.7 collective-permute-start.8
  38.3 0.8 shard_map.61.partial_ref
  39.1 0.8 shard_map.58.partial_ref
  39.9 0.0 collective-permute-done.10.outer_ref.other_ref
  39.9 0.7 shard_map.62.refs_1_
  40.6 0.9 shard_map.63
  41.5 1.6 %collective-permute-start.12 = (bf16[384,256]{1,0:T(8,128)(2,1)S(1)}, bf16[384,256]{1,0:T(8,128)(2,1)S(1)}, u32[]{:S(2)}, u32[]{:S(2)}) collective-permute-start(bf16[384,256]{1,0:T(8,128)(2,1)S(1)} %get-tuple-element.27), channel_id=1, source_target_pairs={{0,1},{1,0},{4,5},{5,4},{2,3},{3,2},{6,7},{7,6},{8,9},{9,8},{12,13... | collective-permute-start | bytes 589832 | tf_op jit(solution)/shard_map/ppermute | solution.py:99
  43.1 1.5 %collective-permute-start.13 = (bf16[384,256]{1,0:T(8,128)(2,1)S(1)}, bf16[384,256]{1,0:T(8,128)(2,1)S(1)}, u32[]{:S(2)}, u32[]{:S(2)}) collective-permute-start(bf16[384,256]{1,0:T(8,128)(2,1)S(1)} %get-tuple-element.28), channel_id=1, source_target_pairs={{0,4},{1,5},{4,0},{5,1},{2,6},{3,7},{6,2},{7,3},{8,12},{9,13},{12,... | collective-permute-start | bytes 589832 | tf_op jit(solution)/shard_map/ppermute | solution.py:99
  44.6 0.4 collective-permute-start.14
  45.1 2.2 %collective-permute-done.12.refs_1_ = bf16[384,256]{1,0:T(8,128)(2,1)S(1)} collective-permute-done((bf16[384,256]{1,0:T(8,128)(2,1)S(1)}, bf16[384,256]{1,0:T(8,128)(2,1)S(1)}, u32[]{:S(2)}, u32[]{:S(2)}) %collective-permute-start.12) | collective-permute-done | bytes 196640 | tf_op jit(solution)/shard_map/ppermute | solution.py:99
  47.3 1.6 %collective-permute-done.13.refs_2_ = bf16[384,256]{1,0:T(8,128)(2,1)S(1)} collective-permute-done((bf16[384,256]{1,0:T(8,128)(2,1)S(1)}, bf16[384,256]{1,0:T(8,128)(2,1)S(1)}, u32[]{:S(2)}, u32[]{:S(2)}) %collective-permute-start.13) | collective-permute-done | bytes 196640 | tf_op jit(solution)/shard_map/ppermute | solution.py:99
  48.8 2.4 %collective-permute-done.14.refs_3_ = bf16[384,256]{1,0:T(8,128)(2,1)S(1)} collective-permute-done((bf16[384,256]{1,0:T(8,128)(2,1)S(1)}, bf16[384,256]{1,0:T(8,128)(2,1)S(1)}, u32[]{:S(2)}, u32[]{:S(2)}) %collective-permute-start.14) | collective-permute-done | bytes 196640 | tf_op jit(solution)/shard_map/ppermute | solution.py:99
  51.2 0.6 shard_map.64
  51.9 23.4 %all_to_all.10 = f32[32,4,384]{2,1,0:T(4,128)S(1)} all-to-all(f32[32,4,384]{2,1,0:T(4,128)S(1)} %get-tuple-element.30), channel_id=1, replica_groups=mesh['far'=4,'mid'=2,'core'=2,'gy'=2] {'far','mid','core','gy'}, dimensions={0} | all-to-all | bytes 393216 | tf_op jit(solution)/shard_map/all_to_all | solution.py:499
  75.3 0.1 reduce_sum.9
  75.3 11.4 %all_to_all.11.gram_ref = f32[32,4,384]{2,1,0:T(4,128)S(1)} all-to-all(f32[32,4,384]{2,1,0:T(4,128)S(1)} %broadcast_in_dim.2), channel_id=1, replica_groups=mesh['far'=4,'mid'=2,'core'=2,'gy'=2] {'far','mid','core','gy'}, dimensions={0} | all-to-all | bytes 393216 | tf_op jit(solution)/shard_map/all_to_all | solution.py:500
  86.8 11.7 %shard_map.65 = (bf16[1536,256]{1,0:T(8,128)(2,1)}, f32[256,256]{1,0:T(8,128)}) custom-call(f32[32,4,384]{2,1,0:T(4,128)S(1)} %all_to_all.11.gram_ref, bf16[1536,256]{1,0:T(8,128)(2,1)S(1)} %get-tuple-element.31.rows_ref), custom_call_target="tpu_custom_call" | custom-call | tf_op jit(solution)/shard_map/pallas_call | solution.py:481
  (8 shorter events, 0.0 us)
Async XLA Ops:
  0.6 18.0 %copy-start = (bf16[3,3,256,256]{3,2,1,0:T(8,128)(2,1)S(1)}, bf16[3,3,256,256]{3,2,1,0:T(8,128)(2,1)}, u32[]{:S(2)}) copy-start(bf16[3,3,256,256]{3,2,1,0:T(8,128)(2,1)} %constant.4.clone.weights_ref) | copy-start | bytes 3538948
  0.6 1.2 %copy-start.1 = (bf16[6,8,32,256]{3,2,1,0:T(8,128)(2,1)S(1)}, bf16[6,8,32,256]{3,2,1,0:T(8,128)(2,1)}, u32[]{:S(2)}) copy-start(bf16[6,8,32,256]{3,2,1,0:T(8,128)(2,1)} %param.3) | copy-start | bytes 2359300
  1.9 0.7 copy-start.2
  3.1 8.3 %collective-permute-start = (bf16[416,256]{1,0:T(8,128)(2,1)S(1)}, bf16[416,256]{1,0:T(8,128)(2,1)S(1)}, u32[]{:S(2)}, u32[]{:S(2)}) collective-permute-start(bf16[416,256]{1,0:T(8,128)(2,1)S(1)} %get-tuple-element.19), channel_id=1, source_target_pairs={{0,1},{1,0},{4,5},{5,4},{2,3},{3,2},{6,7},{7,6},{8,9},{9,8},{12,13... | collective-permute-start | bytes 638984 | tf_op jit(solution)/shard_map/ppermute | solution.py:99
  6.2 8.2 %collective-permute-start.1 = (bf16[416,256]{1,0:T(8,128)(2,1)S(1)}, bf16[416,256]{1,0:T(8,128)(2,1)S(1)}, u32[]{:S(2)}, u32[]{:S(2)}) collective-permute-start(bf16[416,256]{1,0:T(8,128)(2,1)S(1)} %get-tuple-element.20), channel_id=1, source_target_pairs={{0,4},{1,5},{4,0},{5,1},{2,6},{3,7},{6,2},{7,3},{8,12},{9,13},{12,... | collective-permute-start | bytes 638984 | tf_op jit(solution)/shard_map/ppermute | solution.py:99
  7.7 9.6 %collective-permute-start.2 = (bf16[416,256]{1,0:T(8,128)(2,1)S(1)}, bf16[416,256]{1,0:T(8,128)(2,1)S(1)}, u32[]{:S(2)}, u32[]{:S(2)}) collective-permute-start(bf16[416,256]{1,0:T(8,128)(2,1)S(1)} %get-tuple-element.21), channel_id=1, source_target_pairs={{0,5},{1,4},{4,1},{5,0},{2,7},{3,6},{6,3},{7,2},{8,13},{9,12},{12,... | collective-permute-start | bytes 638984 | tf_op jit(solution)/shard_map/ppermute | solution.py:99
  17.4 2.8 %collective-permute-start.4 = (bf16[2,384,256]{2,1,0:T(8,128)(2,1)S(1)}, bf16[2,384,256]{2,1,0:T(8,128)(2,1)S(1)}, u32[]{:S(2)}, u32[]{:S(2)}) collective-permute-start(bf16[2,384,256]{2,1,0:T(8,128)(2,1)S(1)} %get-tuple-element.24.own_ref.refs_0_), channel_id=1, source_target_pairs={{0,2},{2,0},{1,3},{3,1},{4,6},{6,4},{5,7},{7,5},{8,10},{10,8},{9,1... | collective-permute-start | bytes 1179656 | tf_op jit(solution)/shard_map/ppermute | solution.py:283
  17.4 2.8 %collective-permute-start.6 = (bf16[2,384,256]{2,1,0:T(8,128)(2,1)S(1)}, bf16[2,384,256]{2,1,0:T(8,128)(2,1)S(1)}, u32[]{:S(2)}, u32[]{:S(2)}) collective-permute-start(bf16[2,384,256]{2,1,0:T(8,128)(2,1)S(1)} %get-tuple-element.22.own_ref.refs_0_), channel_id=1, source_target_pairs={{0,2},{2,0},{1,3},{3,1},{4,6},{6,4},{5,7},{7,5},{8,10},{10,8},{9,1... | collective-permute-start | bytes 1179656 | tf_op jit(solution)/shard_map/ppermute | solution.py:283
  17.9 6.0 %collective-permute-start.3 = (bf16[2,384,256]{2,1,0:T(8,128)(2,1)S(1)}, bf16[2,384,256]{2,1,0:T(8,128)(2,1)S(1)}, u32[]{:S(2)}, u32[]{:S(2)}) collective-permute-start(bf16[2,384,256]{2,1,0:T(8,128)(2,1)S(1)} %get-tuple-element.22.own_ref.refs_0_), channel_id=1, source_target_pairs={{2,8},{10,16},{18,24},{8,2},{16,10},{24,18},{3,9},{11,17},{19,25},... | collective-permute-start | bytes 1179656 | tf_op jit(solution)/shard_map/ppermute | solution.py:289
  20.8 9.2 %collective-permute-start.7 = (bf16[2,384,256]{2,1,0:T(8,128)(2,1)S(1)}, bf16[2,384,256]{2,1,0:T(8,128)(2,1)S(1)}, u32[]{:S(2)}, u32[]{:S(2)}) collective-permute-start(bf16[2,384,256]{2,1,0:T(8,128)(2,1)S(1)} %shard_map.56.own_ref.refs_0_), channel_id=1, source_target_pairs={{0,2},{2,0},{1,3},{3,1},{4,6},{6,4},{5,7},{7,5},{8,10},{10,8},{9,1... | collective-permute-start | bytes 1179656 | tf_op jit(solution)/shard_map/ppermute | solution.py:283
  24.5 5.5 %collective-permute-start.9 = (bf16[2,384,256]{2,1,0:T(8,128)(2,1)S(1)}, bf16[2,384,256]{2,1,0:T(8,128)(2,1)S(1)}, u32[]{:S(2)}, u32[]{:S(2)}) collective-permute-start(bf16[2,384,256]{2,1,0:T(8,128)(2,1)S(1)} %shard_map.53.own_ref.refs_0_), channel_id=1, source_target_pairs={{0,2},{2,0},{1,3},{3,1},{4,6},{6,4},{5,7},{7,5},{8,10},{10,8},{9,1... | collective-permute-start | bytes 1179656 | tf_op jit(solution)/shard_map/ppermute | solution.py:283
  27.8 6.1 %collective-permute-start.5 = (bf16[2,384,256]{2,1,0:T(8,128)(2,1)S(1)}, bf16[2,384,256]{2,1,0:T(8,128)(2,1)S(1)}, u32[]{:S(2)}, u32[]{:S(2)}) collective-permute-start(bf16[2,384,256]{2,1,0:T(8,128)(2,1)S(1)} %shard_map.53.own_ref.refs_0_), channel_id=1, source_target_pairs={{2,8},{10,16},{18,24},{8,2},{16,10},{24,18},{3,9},{11,17},{19,25},... | collective-permute-start | bytes 1179656 | tf_op jit(solution)/shard_map/ppermute | solution.py:289
  30.7 9.2 %collective-permute-start.10 = (bf16[2,384,256]{2,1,0:T(8,128)(2,1)S(1)}, bf16[2,384,256]{2,1,0:T(8,128)(2,1)S(1)}, u32[]{:S(2)}, u32[]{:S(2)}) collective-permute-start(bf16[2,384,256]{2,1,0:T(8,128)(2,1)S(1)} %shard_map.60.own_ref), channel_id=1, source_target_pairs={{0,2},{2,0},{1,3},{3,1},{4,6},{6,4},{5,7},{7,5},{8,10},{10,8},{9,1... | collective-permute-start | bytes 1179656 | tf_op jit(solution)/shard_map/ppermute | solution.py:283
  34.5 5.4 %collective-permute-start.11 = (bf16[2,384,256]{2,1,0:T(8,128)(2,1)S(1)}, bf16[2,384,256]{2,1,0:T(8,128)(2,1)S(1)}, u32[]{:S(2)}, u32[]{:S(2)}) collective-permute-start(bf16[2,384,256]{2,1,0:T(8,128)(2,1)S(1)} %shard_map.57.own_ref), channel_id=1, source_target_pairs={{0,2},{2,0},{1,3},{3,1},{4,6},{6,4},{5,7},{7,5},{8,10},{10,8},{9,1... | collective-permute-start | bytes 1179656 | tf_op jit(solution)/shard_map/ppermute | solution.py:283
  37.7 2.9 %collective-permute-start.8 = (bf16[2,384,256]{2,1,0:T(8,128)(2,1)S(1)}, bf16[2,384,256]{2,1,0:T(8,128)(2,1)S(1)}, u32[]{:S(2)}, u32[]{:S(2)}) collective-permute-start(bf16[2,384,256]{2,1,0:T(8,128)(2,1)S(1)} %shard_map.57.own_ref), channel_id=1, source_target_pairs={{2,8},{10,16},{18,24},{8,2},{16,10},{24,18},{3,9},{11,17},{19,25},... | collective-permute-start | bytes 1179656 | tf_op jit(solution)/shard_map/ppermute | solution.py:289
  41.5 5.7 %collective-permute-start.12 = (bf16[384,256]{1,0:T(8,128)(2,1)S(1)}, bf16[384,256]{1,0:T(8,128)(2,1)S(1)}, u32[]{:S(2)}, u32[]{:S(2)}) collective-permute-start(bf16[384,256]{1,0:T(8,128)(2,1)S(1)} %get-tuple-element.27), channel_id=1, source_target_pairs={{0,1},{1,0},{4,5},{5,4},{2,3},{3,2},{6,7},{7,6},{8,9},{9,8},{12,13... | collective-permute-start | bytes 589832 | tf_op jit(solution)/shard_map/ppermute | solution.py:99
  43.1 5.7 %collective-permute-start.13 = (bf16[384,256]{1,0:T(8,128)(2,1)S(1)}, bf16[384,256]{1,0:T(8,128)(2,1)S(1)}, u32[]{:S(2)}, u32[]{:S(2)}) collective-permute-start(bf16[384,256]{1,0:T(8,128)(2,1)S(1)} %get-tuple-element.28), channel_id=1, source_target_pairs={{0,4},{1,5},{4,0},{5,1},{2,6},{3,7},{6,2},{7,3},{8,12},{9,13},{12,... | collective-permute-start | bytes 589832 | tf_op jit(solution)/shard_map/ppermute | solution.py:99
  44.6 6.6 %collective-permute-start.14 = (bf16[384,256]{1,0:T(8,128)(2,1)S(1)}, bf16[384,256]{1,0:T(8,128)(2,1)S(1)}, u32[]{:S(2)}, u32[]{:S(2)}) collective-permute-start(bf16[384,256]{1,0:T(8,128)(2,1)S(1)} %get-tuple-element.29), channel_id=1, source_target_pairs={{0,5},{1,4},{4,1},{5,0},{2,7},{3,6},{6,3},{7,2},{8,13},{9,12},{12,... | collective-permute-start | bytes 589832 | tf_op jit(solution)/shard_map/ppermute | solution.py:99

commit v8 on v6

--- a/solution.py
+++ b/solution.py
@@ -385,11 +385,17 @@
     return full, forward
 
 
-def combine(columns, rows):
+def spread(rows):
+    return [
+        [row_splat(rows[:, left : left + lanes], k) for k in range(panel_rows)]
+        for left in range(0, rows.shape[1], lanes)
+    ]
+
+
+def combine(columns, spread_rows):
     parts = []
-    for left in range(0, rows.shape[1], lanes):
-        piece = rows[:, left : left + lanes]
-        terms = [column * row_splat(piece, k) for k, column in enumerate(columns)]
+    for rows in spread_rows:
+        terms = [column * row for column, row in zip(columns, rows)]
         while len(terms) > 1:
             terms = [a + b for a, b in zip(terms[::2], terms[1::2])]
         parts.append(terms[0])
@@ -433,7 +439,8 @@
             lane = local + index * panel_rows
             rows = groups[index]
             full, forward = panel_inverse([lane_splat(rows, lane + k) for k in range(panel_rows)])
-            step_rows = combine(full, rows)
+            rows = spread(rows)
+            step_rows = spread(combine(full, rows))
             for other in range(index + 1, len(groups)):
                 target = groups[other]
                 columns = [lane_splat(target, lane + k) for k in range(panel_rows)]
@@ -445,20 +452,21 @@
     row = lax.broadcasted_iota(jnp.int32, (order, order), 0)
     col = lax.broadcasted_iota(jnp.int32, (order, order), 1)
     upper_ref[...] = jnp.where(col >= row, factor_ref[...] * (1.0 / scale), 0.0)
-    inverse = jnp.where(col <= row, inverse_ref[...] * scale, 0.0)
-    high = inverse.astype(jnp.bfloat16)
-    rest = inverse - high.astype(jnp.float32)
-    middle = rest.astype(jnp.bfloat16)
-    low = (rest - middle.astype(jnp.float32)).astype(jnp.bfloat16)
+    rest = jnp.where(col <= row, inverse_ref[...] * scale, 0.0).T
+    parts = []
+    for _ in range(3):
+        parts.append(rest.astype(jnp.bfloat16))
+        rest = rest - parts[-1].astype(jnp.float32)
+    stacked = jnp.concatenate(parts, axis=0)
     count = rows_ref.shape[0]
     chunk = math.gcd(count, 512)
     for at in range(0, count, chunk):
         piece = rows_ref[at : at + chunk, :]
-        total = jnp.zeros((chunk, order), jnp.float32)
-        for part in (low, middle, high):
-            total = total + lax.dot_general(
-                piece, part, (((1,), (1,)), ((), ())), preferred_element_type=jnp.float32
-            )
+        total = jnp.dot(
+            jnp.concatenate([piece] * len(parts), axis=1),
+            stacked,
+            preferred_element_type=jnp.float32,
+        )
         rotated_ref[at : at + chunk, :] = total.astype(jnp.bfloat16)
 
 

time: 98 us -> 98 us (level)
  no operation moved by 1% of the time
where the time goes in v8:
time: 98 us; the launch traced here: 97.8 us
  blocking collectives  34.8 us (36%)
  starting transfers between devices  23.4 us (24%)
  Pallas kernels  21 us (21%)
  waiting for transfers between devices  15.7 us (16%)
  local copies, waits for them, and re-layouts  1.99 us (2%)
    all_to_all x1, blocking collectives, sum_over_devices(): total = jnp.sum(lax.all_to_all(values, axes, 0, 0), axis=0)  23.4 us
    ppermute x6, waiting for transfers between devices, exchange(): result.append(lax.ppermute(message, ('mid', 'gy'), perm))  15.7 us
    ppermute x6, starting transfers between devices, from_other_core(): return lax.ppermute(own, 'core', [(0, 1), (1, 0)])  13.3 us
    all_to_all x1, blocking collectives, sum_over_devices(): lax.all_to_all(jnp.broadcast_to(total[None], values.shape), axes, 0, 0)  11.4 us
    pallas_call x1, Pallas kernels, factor_and_rotate(): pl.pallas_call(functools.partial(factor_kernel, math.sqrt(total_cells)),...  11 us
    ppermute x6, starting transfers between devices, exchange(): result.append(lax.ppermute(message, ('mid', 'gy'), perm))  8.13 us
    pallas_call x6, Pallas kernels, plane_part(): pl.pallas_call(plane_kernel, out_shape=jax.ShapeDtypeStruct(own.shape, jn...  4.63 us
    pallas_call x6, Pallas kernels, layer_part(): pl.pallas_call(functools.partial(layer_kernel, before is None, layers, pa...  4.02 us
  transfers between devices with their start and end apart: 15, of which 6 were waited for; matrix products, arithmetic and copies ran while one was open for 0% of the time, Pallas kernels for 8%

profile of v8, /device:TPU:0, one launch (start us, length us, event | category | flops | bytes accessed | tf_op | source)
XLA Modules:
  0.0 97.8 jit_solution(7363068260812198088)
XLA Ops:
  0.6 0.0 copy-start
  0.7 1.2 %copy-done.1 = bf16[6,8,32,256]{3,2,1,0:T(8,128)(2,1)S(1)} copy-done((bf16[6,8,32,256]{3,2,1,0:T(8,128)(2,1)S(1)}, bf16[6,8,32,256]{3,2,1,0:T(8,128)(2,1)}, u32[]{:S(2)}) %copy-start.1) | copy-done | bytes 786456
  1.9 0.7 copy-done.2
  2.6 0.5 shard_map.50
  3.1 3.0 %collective-permute-start = (bf16[416,256]{1,0:T(8,128)(2,1)S(1)}, bf16[416,256]{1,0:T(8,128)(2,1)S(1)}, u32[]{:S(2)}, u32[]{:S(2)}) collective-permute-start(bf16[416,256]{1,0:T(8,128)(2,1)S(1)} %get-tuple-element.19), channel_id=1, source_target_pairs={{0,1},{1,0},{4,5},{5,4},{2,3},{3,2},{6,7},{7,6},{8,9},{9,8},{12,13... | collective-permute-start | bytes 638984 | tf_op jit(solution)/shard_map/ppermute | solution.py:99
  6.2 1.5 %collective-permute-start.1 = (bf16[416,256]{1,0:T(8,128)(2,1)S(1)}, bf16[416,256]{1,0:T(8,128)(2,1)S(1)}, u32[]{:S(2)}, u32[]{:S(2)}) collective-permute-start(bf16[416,256]{1,0:T(8,128)(2,1)S(1)} %get-tuple-element.20), channel_id=1, source_target_pairs={{0,4},{1,5},{4,0},{5,1},{2,6},{3,7},{6,2},{7,3},{8,12},{9,13},{12,... | collective-permute-start | bytes 638984 | tf_op jit(solution)/shard_map/ppermute | solution.py:99
  7.7 0.0 collective-permute-start.2
  7.7 3.7 %collective-permute-done.refs_1_ = bf16[416,256]{1,0:T(8,128)(2,1)S(1)} collective-permute-done((bf16[416,256]{1,0:T(8,128)(2,1)S(1)}, bf16[416,256]{1,0:T(8,128)(2,1)S(1)}, u32[]{:S(2)}, u32[]{:S(2)}) %collective-permute-start) | collective-permute-done | bytes 213024 | tf_op jit(solution)/shard_map/ppermute | solution.py:99
  11.4 2.9 %collective-permute-done.1.refs_2_ = bf16[416,256]{1,0:T(8,128)(2,1)S(1)} collective-permute-done((bf16[416,256]{1,0:T(8,128)(2,1)S(1)}, bf16[416,256]{1,0:T(8,128)(2,1)S(1)}, u32[]{:S(2)}, u32[]{:S(2)}) %collective-permute-start.1) | collective-permute-done | bytes 213024 | tf_op jit(solution)/shard_map/ppermute | solution.py:99
  14.3 2.9 %collective-permute-done.2.refs_3_ = bf16[416,256]{1,0:T(8,128)(2,1)S(1)} collective-permute-done((bf16[416,256]{1,0:T(8,128)(2,1)S(1)}, bf16[416,256]{1,0:T(8,128)(2,1)S(1)}, u32[]{:S(2)}, u32[]{:S(2)}) %collective-permute-start.2) | collective-permute-done | bytes 213024 | tf_op jit(solution)/shard_map/ppermute | solution.py:99
  17.2 0.1 shard_map.51
  17.4 0.1 collective-permute-start.4
  17.4 0.5 collective-permute-start.6
  17.9 0.7 collective-permute-start.3
  18.6 0.8 shard_map.55.partial_ref
  19.4 0.8 shard_map.52.partial_ref
  20.2 0.0 collective-permute-done.4.other_ref.outer_ref
  20.2 0.0 collective-permute-done.6.other_ref
  20.2 0.6 shard_map.56.own_ref.refs_0_
  20.8 3.1 %collective-permute-start.7 = (bf16[2,384,256]{2,1,0:T(8,128)(2,1)S(1)}, bf16[2,384,256]{2,1,0:T(8,128)(2,1)S(1)}, u32[]{:S(2)}, u32[]{:S(2)}) collective-permute-start(bf16[2,384,256]{2,1,0:T(8,128)(2,1)S(1)} %shard_map.56.own_ref.refs_0_), channel_id=1, source_target_pairs={{0,2},{2,0},{1,3},{3,1},{4,6},{6,4},{5,7},{7,5},{8,10},{10,8},{9,1... | collective-permute-start | bytes 1179656 | tf_op jit(solution)/shard_map/ppermute | solution.py:283
  23.9 0.0 collective-permute-done.3.outer_ref
  23.9 0.6 shard_map.53.own_ref.refs_0_
  24.5 3.3 %collective-permute-start.9 = (bf16[2,384,256]{2,1,0:T(8,128)(2,1)S(1)}, bf16[2,384,256]{2,1,0:T(8,128)(2,1)S(1)}, u32[]{:S(2)}, u32[]{:S(2)}) collective-permute-start(bf16[2,384,256]{2,1,0:T(8,128)(2,1)S(1)} %shard_map.53.own_ref.refs_0_), channel_id=1, source_target_pairs={{0,2},{2,0},{1,3},{3,1},{4,6},{6,4},{5,7},{7,5},{8,10},{10,8},{9,1... | collective-permute-start | bytes 1179656 | tf_op jit(solution)/shard_map/ppermute | solution.py:283
  27.8 0.7 collective-permute-start.5
  28.4 0.8 shard_map.59.partial_ref
  29.2 0.8 shard_map.54.partial_ref
  30.0 0.0 collective-permute-done.7.other_ref.outer_ref
  30.0 0.7 shard_map.60.own_ref
  30.7 3.1 %collective-permute-start.10 = (bf16[2,384,256]{2,1,0:T(8,128)(2,1)S(1)}, bf16[2,384,256]{2,1,0:T(8,128)(2,1)S(1)}, u32[]{:S(2)}, u32[]{:S(2)}) collective-permute-start(bf16[2,384,256]{2,1,0:T(8,128)(2,1)S(1)} %shard_map.60.own_ref), channel_id=1, source_target_pairs={{0,2},{2,0},{1,3},{3,1},{4,6},{6,4},{5,7},{7,5},{8,10},{10,8},{9,1... | collective-permute-start | bytes 1179656 | tf_op jit(solution)/shard_map/ppermute | solution.py:283
  33.8 0.6 shard_map.57.own_ref
  34.5 3.2 %collective-permute-start.11 = (bf16[2,384,256]{2,1,0:T(8,128)(2,1)S(1)}, bf16[2,384,256]{2,1,0:T(8,128)(2,1)S(1)}, u32[]{:S(2)}, u32[]{:S(2)}) collective-permute-start(bf16[2,384,256]{2,1,0:T(8,128)(2,1)S(1)} %shard_map.57.own_ref), channel_id=1, source_target_pairs={{0,2},{2,0},{1,3},{3,1},{4,6},{6,4},{5,7},{7,5},{8,10},{10,8},{9,1... | collective-permute-start | bytes 1179656 | tf_op jit(solution)/shard_map/ppermute | solution.py:283
  37.7 0.7 collective-permute-start.8
  38.3 0.8 shard_map.61.partial_ref
  39.1 0.8 shard_map.58.partial_ref
  39.9 0.0 collective-permute-done.10.outer_ref.other_ref
  39.9 0.7 shard_map.62.refs_1_
  40.6 0.9 shard_map.63
  41.5 1.6 %collective-permute-start.12 = (bf16[384,256]{1,0:T(8,128)(2,1)S(1)}, bf16[384,256]{1,0:T(8,128)(2,1)S(1)}, u32[]{:S(2)}, u32[]{:S(2)}) collective-permute-start(bf16[384,256]{1,0:T(8,128)(2,1)S(1)} %get-tuple-element.27), channel_id=1, source_target_pairs={{0,1},{1,0},{4,5},{5,4},{2,3},{3,2},{6,7},{7,6},{8,9},{9,8},{12,13... | collective-permute-start | bytes 589832 | tf_op jit(solution)/shard_map/ppermute | solution.py:99
  43.1 1.5 %collective-permute-start.13 = (bf16[384,256]{1,0:T(8,128)(2,1)S(1)}, bf16[384,256]{1,0:T(8,128)(2,1)S(1)}, u32[]{:S(2)}, u32[]{:S(2)}) collective-permute-start(bf16[384,256]{1,0:T(8,128)(2,1)S(1)} %get-tuple-element.28), channel_id=1, source_target_pairs={{0,4},{1,5},{4,0},{5,1},{2,6},{3,7},{6,2},{7,3},{8,12},{9,13},{12,... | collective-permute-start | bytes 589832 | tf_op jit(solution)/shard_map/ppermute | solution.py:99
  44.6 0.4 collective-permute-start.14
  45.1 2.2 %collective-permute-done.12.refs_1_ = bf16[384,256]{1,0:T(8,128)(2,1)S(1)} collective-permute-done((bf16[384,256]{1,0:T(8,128)(2,1)S(1)}, bf16[384,256]{1,0:T(8,128)(2,1)S(1)}, u32[]{:S(2)}, u32[]{:S(2)}) %collective-permute-start.12) | collective-permute-done | bytes 196640 | tf_op jit(solution)/shard_map/ppermute | solution.py:99
  47.3 1.6 %collective-permute-done.13.refs_2_ = bf16[384,256]{1,0:T(8,128)(2,1)S(1)} collective-permute-done((bf16[384,256]{1,0:T(8,128)(2,1)S(1)}, bf16[384,256]{1,0:T(8,128)(2,1)S(1)}, u32[]{:S(2)}, u32[]{:S(2)}) %collective-permute-start.13) | collective-permute-done | bytes 196640 | tf_op jit(solution)/shard_map/ppermute | solution.py:99
  48.8 2.4 %collective-permute-done.14.refs_3_ = bf16[384,256]{1,0:T(8,128)(2,1)S(1)} collective-permute-done((bf16[384,256]{1,0:T(8,128)(2,1)S(1)}, bf16[384,256]{1,0:T(8,128)(2,1)S(1)}, u32[]{:S(2)}, u32[]{:S(2)}) %collective-permute-start.14) | collective-permute-done | bytes 196640 | tf_op jit(solution)/shard_map/ppermute | solution.py:99
  51.2 0.6 shard_map.64
  51.9 23.4 %all_to_all.10 = f32[32,4,384]{2,1,0:T(4,128)S(1)} all-to-all(f32[32,4,384]{2,1,0:T(4,128)S(1)} %get-tuple-element.30), channel_id=1, replica_groups=mesh['far'=4,'mid'=2,'core'=2,'gy'=2] {'far','mid','core','gy'}, dimensions={0} | all-to-all | bytes 393216 | tf_op jit(solution)/shard_map/all_to_all | solution.py:494
  75.3 0.1 reduce_sum.9
  75.3 11.4 %all_to_all.11.gram_ref = f32[32,4,384]{2,1,0:T(4,128)S(1)} all-to-all(f32[32,4,384]{2,1,0:T(4,128)S(1)} %broadcast_in_dim.2), channel_id=1, replica_groups=mesh['far'=4,'mid'=2,'core'=2,'gy'=2] {'far','mid','core','gy'}, dimensions={0} | all-to-all | bytes 393216 | tf_op jit(solution)/shard_map/all_to_all | solution.py:495
  86.8 11.0 %shard_map.65 = (bf16[1536,256]{1,0:T(8,128)(2,1)}, f32[256,256]{1,0:T(8,128)}) custom-call(f32[32,4,384]{2,1,0:T(4,128)S(1)} %all_to_all.11.gram_ref, bf16[1536,256]{1,0:T(8,128)(2,1)S(1)} %get-tuple-element.31.rows_ref), custom_call_target="tpu_custom_call" | custom-call | tf_op jit(solution)/shard_map/pallas_call | solution.py:476
  (8 shorter events, 0.0 us)
Async XLA Ops:
  0.6 18.0 %copy-start = (bf16[3,3,256,256]{3,2,1,0:T(8,128)(2,1)S(1)}, bf16[3,3,256,256]{3,2,1,0:T(8,128)(2,1)}, u32[]{:S(2)}) copy-start(bf16[3,3,256,256]{3,2,1,0:T(8,128)(2,1)} %constant.4.clone.weights_ref) | copy-start | bytes 3538948
  0.6 1.2 %copy-start.1 = (bf16[6,8,32,256]{3,2,1,0:T(8,128)(2,1)S(1)}, bf16[6,8,32,256]{3,2,1,0:T(8,128)(2,1)}, u32[]{:S(2)}) copy-start(bf16[6,8,32,256]{3,2,1,0:T(8,128)(2,1)} %param.3) | copy-start | bytes 2359300
  1.9 0.7 copy-start.2
  3.1 8.3 %collective-permute-start = (bf16[416,256]{1,0:T(8,128)(2,1)S(1)}, bf16[416,256]{1,0:T(8,128)(2,1)S(1)}, u32[]{:S(2)}, u32[]{:S(2)}) collective-permute-start(bf16[416,256]{1,0:T(8,128)(2,1)S(1)} %get-tuple-element.19), channel_id=1, source_target_pairs={{0,1},{1,0},{4,5},{5,4},{2,3},{3,2},{6,7},{7,6},{8,9},{9,8},{12,13... | collective-permute-start | bytes 638984 | tf_op jit(solution)/shard_map/ppermute | solution.py:99
  6.2 8.2 %collective-permute-start.1 = (bf16[416,256]{1,0:T(8,128)(2,1)S(1)}, bf16[416,256]{1,0:T(8,128)(2,1)S(1)}, u32[]{:S(2)}, u32[]{:S(2)}) collective-permute-start(bf16[416,256]{1,0:T(8,128)(2,1)S(1)} %get-tuple-element.20), channel_id=1, source_target_pairs={{0,4},{1,5},{4,0},{5,1},{2,6},{3,7},{6,2},{7,3},{8,12},{9,13},{12,... | collective-permute-start | bytes 638984 | tf_op jit(solution)/shard_map/ppermute | solution.py:99
  7.7 9.6 %collective-permute-start.2 = (bf16[416,256]{1,0:T(8,128)(2,1)S(1)}, bf16[416,256]{1,0:T(8,128)(2,1)S(1)}, u32[]{:S(2)}, u32[]{:S(2)}) collective-permute-start(bf16[416,256]{1,0:T(8,128)(2,1)S(1)} %get-tuple-element.21), channel_id=1, source_target_pairs={{0,5},{1,4},{4,1},{5,0},{2,7},{3,6},{6,3},{7,2},{8,13},{9,12},{12,... | collective-permute-start | bytes 638984 | tf_op jit(solution)/shard_map/ppermute | solution.py:99
  17.4 2.8 %collective-permute-start.4 = (bf16[2,384,256]{2,1,0:T(8,128)(2,1)S(1)}, bf16[2,384,256]{2,1,0:T(8,128)(2,1)S(1)}, u32[]{:S(2)}, u32[]{:S(2)}) collective-permute-start(bf16[2,384,256]{2,1,0:T(8,128)(2,1)S(1)} %get-tuple-element.24.own_ref.refs_0_), channel_id=1, source_target_pairs={{0,2},{2,0},{1,3},{3,1},{4,6},{6,4},{5,7},{7,5},{8,10},{10,8},{9,1... | collective-permute-start | bytes 1179656 | tf_op jit(solution)/shard_map/ppermute | solution.py:283
  17.4 2.8 %collective-permute-start.6 = (bf16[2,384,256]{2,1,0:T(8,128)(2,1)S(1)}, bf16[2,384,256]{2,1,0:T(8,128)(2,1)S(1)}, u32[]{:S(2)}, u32[]{:S(2)}) collective-permute-start(bf16[2,384,256]{2,1,0:T(8,128)(2,1)S(1)} %get-tuple-element.22.own_ref.refs_0_), channel_id=1, source_target_pairs={{0,2},{2,0},{1,3},{3,1},{4,6},{6,4},{5,7},{7,5},{8,10},{10,8},{9,1... | collective-permute-start | bytes 1179656 | tf_op jit(solution)/shard_map/ppermute | solution.py:283
  17.9 6.0 %collective-permute-start.3 = (bf16[2,384,256]{2,1,0:T(8,128)(2,1)S(1)}, bf16[2,384,256]{2,1,0:T(8,128)(2,1)S(1)}, u32[]{:S(2)}, u32[]{:S(2)}) collective-permute-start(bf16[2,384,256]{2,1,0:T(8,128)(2,1)S(1)} %get-tuple-element.22.own_ref.refs_0_), channel_id=1, source_target_pairs={{2,8},{10,16},{18,24},{8,2},{16,10},{24,18},{3,9},{11,17},{19,25},... | collective-permute-start | bytes 1179656 | tf_op jit(solution)/shard_map/ppermute | solution.py:289
  20.8 9.2 %collective-permute-start.7 = (bf16[2,384,256]{2,1,0:T(8,128)(2,1)S(1)}, bf16[2,384,256]{2,1,0:T(8,128)(2,1)S(1)}, u32[]{:S(2)}, u32[]{:S(2)}) collective-permute-start(bf16[2,384,256]{2,1,0:T(8,128)(2,1)S(1)} %shard_map.56.own_ref.refs_0_), channel_id=1, source_target_pairs={{0,2},{2,0},{1,3},{3,1},{4,6},{6,4},{5,7},{7,5},{8,10},{10,8},{9,1... | collective-permute-start | bytes 1179656 | tf_op jit(solution)/shard_map/ppermute | solution.py:283
  24.5 5.5 %collective-permute-start.9 = (bf16[2,384,256]{2,1,0:T(8,128)(2,1)S(1)}, bf16[2,384,256]{2,1,0:T(8,128)(2,1)S(1)}, u32[]{:S(2)}, u32[]{:S(2)}) collective-permute-start(bf16[2,384,256]{2,1,0:T(8,128)(2,1)S(1)} %shard_map.53.own_ref.refs_0_), channel_id=1, source_target_pairs={{0,2},{2,0},{1,3},{3,1},{4,6},{6,4},{5,7},{7,5},{8,10},{10,8},{9,1... | collective-permute-start | bytes 1179656 | tf_op jit(solution)/shard_map/ppermute | solution.py:283
  27.8 6.1 %collective-permute-start.5 = (bf16[2,384,256]{2,1,0:T(8,128)(2,1)S(1)}, bf16[2,384,256]{2,1,0:T(8,128)(2,1)S(1)}, u32[]{:S(2)}, u32[]{:S(2)}) collective-permute-start(bf16[2,384,256]{2,1,0:T(8,128)(2,1)S(1)} %shard_map.53.own_ref.refs_0_), channel_id=1, source_target_pairs={{2,8},{10,16},{18,24},{8,2},{16,10},{24,18},{3,9},{11,17},{19,25},... | collective-permute-start | bytes 1179656 | tf_op jit(solution)/shard_map/ppermute | solution.py:289
  30.7 9.2 %collective-permute-start.10 = (bf16[2,384,256]{2,1,0:T(8,128)(2,1)S(1)}, bf16[2,384,256]{2,1,0:T(8,128)(2,1)S(1)}, u32[]{:S(2)}, u32[]{:S(2)}) collective-permute-start(bf16[2,384,256]{2,1,0:T(8,128)(2,1)S(1)} %shard_map.60.own_ref), channel_id=1, source_target_pairs={{0,2},{2,0},{1,3},{3,1},{4,6},{6,4},{5,7},{7,5},{8,10},{10,8},{9,1... | collective-permute-start | bytes 1179656 | tf_op jit(solution)/shard_map/ppermute | solution.py:283
  34.5 5.4 %collective-permute-start.11 = (bf16[2,384,256]{2,1,0:T(8,128)(2,1)S(1)}, bf16[2,384,256]{2,1,0:T(8,128)(2,1)S(1)}, u32[]{:S(2)}, u32[]{:S(2)}) collective-permute-start(bf16[2,384,256]{2,1,0:T(8,128)(2,1)S(1)} %shard_map.57.own_ref), channel_id=1, source_target_pairs={{0,2},{2,0},{1,3},{3,1},{4,6},{6,4},{5,7},{7,5},{8,10},{10,8},{9,1... | collective-permute-start | bytes 1179656 | tf_op jit(solution)/shard_map/ppermute | solution.py:283
  37.7 2.9 %collective-permute-start.8 = (bf16[2,384,256]{2,1,0:T(8,128)(2,1)S(1)}, bf16[2,384,256]{2,1,0:T(8,128)(2,1)S(1)}, u32[]{:S(2)}, u32[]{:S(2)}) collective-permute-start(bf16[2,384,256]{2,1,0:T(8,128)(2,1)S(1)} %shard_map.57.own_ref), channel_id=1, source_target_pairs={{2,8},{10,16},{18,24},{8,2},{16,10},{24,18},{3,9},{11,17},{19,25},... | collective-permute-start | bytes 1179656 | tf_op jit(solution)/shard_map/ppermute | solution.py:289
  41.5 5.7 %collective-permute-start.12 = (bf16[384,256]{1,0:T(8,128)(2,1)S(1)}, bf16[384,256]{1,0:T(8,128)(2,1)S(1)}, u32[]{:S(2)}, u32[]{:S(2)}) collective-permute-start(bf16[384,256]{1,0:T(8,128)(2,1)S(1)} %get-tuple-element.27), channel_id=1, source_target_pairs={{0,1},{1,0},{4,5},{5,4},{2,3},{3,2},{6,7},{7,6},{8,9},{9,8},{12,13... | collective-permute-start | bytes 589832 | tf_op jit(solution)/shard_map/ppermute | solution.py:99
  43.1 5.7 %collective-permute-start.13 = (bf16[384,256]{1,0:T(8,128)(2,1)S(1)}, bf16[384,256]{1,0:T(8,128)(2,1)S(1)}, u32[]{:S(2)}, u32[]{:S(2)}) collective-permute-start(bf16[384,256]{1,0:T(8,128)(2,1)S(1)} %get-tuple-element.28), channel_id=1, source_target_pairs={{0,4},{1,5},{4,0},{5,1},{2,6},{3,7},{6,2},{7,3},{8,12},{9,13},{12,... | collective-permute-start | bytes 589832 | tf_op jit(solution)/shard_map/ppermute | solution.py:99
  44.6 6.6 %collective-permute-start.14 = (bf16[384,256]{1,0:T(8,128)(2,1)S(1)}, bf16[384,256]{1,0:T(8,128)(2,1)S(1)}, u32[]{:S(2)}, u32[]{:S(2)}) collective-permute-start(bf16[384,256]{1,0:T(8,128)(2,1)S(1)} %get-tuple-element.29), channel_id=1, source_target_pairs={{0,5},{1,4},{4,1},{5,0},{2,7},{3,6},{6,3},{7,2},{8,13},{9,12},{12,... | collective-permute-start | bytes 589832 | tf_op jit(solution)/shard_map/ppermute | solution.py:99

commit v9 on v6

--- a/solution.py
+++ b/solution.py
@@ -100,16 +100,20 @@
     return result
 
 
-def split_kernel(bricks_y, cells_ref, potential_ref, *refs):
+def level_kernel(potential_ref, level_ref):
+    potential = jnp.concatenate(
+        [potential_ref[:, at, :] for at in range(potential_ref.shape[1])], axis=1
+    )
+    level_ref[...] = level_rows(potential, level_ref.shape[0])
+
+
+def split_kernel(bricks_y, cells_ref, level_ref, *refs):
     sent_refs, block_ref = refs[:-1], refs[-1]
     mid, y = lax.axis_index("mid"), lax.axis_index("gy")
     columns, plane = block_ref.shape
     share = columns // len(sent_refs)
     layers = cells_ref.shape[0] // plane
-    potential = jnp.concatenate(
-        [potential_ref[:, at, :] for at in range(potential_ref.shape[1])], axis=1
-    )
-    extra = level_rows(potential, sent_refs[0].shape[0] - layers * share)
+    extra = level_ref[...]
     for sent_ref in sent_refs:
         sent_ref[layers * share :, :] = extra
     for layer in range(layers):
@@ -130,12 +134,17 @@
     message = jax.ShapeDtypeStruct(
         (layers * (columns // parts) + level_room(layers), plane), jnp.bfloat16
     )
+    level = pl.pallas_call(
+        level_kernel,
+        out_shape=jax.ShapeDtypeStruct((level_room(layers), plane), jnp.bfloat16),
+        compiler_params=pltpu.CompilerParams(vmem_limit_bytes=vmem_limit),
+    )(potential)
     return pl.pallas_call(
         functools.partial(split_kernel, bricks_y),
         out_shape=[message] * parts,
         scratch_shapes=[pltpu.VMEM((columns, plane), jnp.float32)],
         compiler_params=pltpu.CompilerParams(vmem_limit_bytes=vmem_limit),
-    )(cells, potential)
+    )(cells, level)
 
 
 def place_kernel(bricks_y, *refs):

time: 98 us -> 98 us (level)
  no operation moved by 1% of the time
where the time goes in v9:
time: 98 us; the launch traced here: 97.8 us
  blocking collectives  34.8 us (36%)
  starting transfers between devices  23.4 us (24%)
  Pallas kernels  21 us (21%)
  waiting for transfers between devices  15.7 us (16%)
  local copies, waits for them, and re-layouts  1.99 us (2%)
    all_to_all x1, blocking collectives, sum_over_devices(): total = jnp.sum(lax.all_to_all(values, axes, 0, 0), axis=0)  23.4 us
    ppermute x6, waiting for transfers between devices, exchange(): result.append(lax.ppermute(message, ('mid', 'gy'), perm))  15.7 us
    ppermute x6, starting transfers between devices, from_other_core(): return lax.ppermute(own, 'core', [(0, 1), (1, 0)])  13.3 us
    all_to_all x1, blocking collectives, sum_over_devices(): lax.all_to_all(jnp.broadcast_to(total[None], values.shape), axes, 0, 0)  11.4 us
    pallas_call x1, Pallas kernels, factor_and_rotate(): pl.pallas_call(functools.partial(factor_kernel, math.sqrt(total_cells)),...  11 us
    ppermute x6, starting transfers between devices, exchange(): result.append(lax.ppermute(message, ('mid', 'gy'), perm))  8.13 us
    pallas_call x6, Pallas kernels, plane_part(): pl.pallas_call(plane_kernel, out_shape=jax.ShapeDtypeStruct(own.shape, jn...  4.63 us
    pallas_call x6, Pallas kernels, layer_part(): pl.pallas_call(functools.partial(layer_kernel, before is None, layers, pa...  4.02 us
  transfers between devices with their start and end apart: 15, of which 6 were waited for; matrix products, arithmetic and copies ran while one was open for 0% of the time, Pallas kernels for 8%

profile of v9, /device:TPU:0, one launch (start us, length us, event | category | flops | bytes accessed | tf_op | source)
XLA Modules:
  0.0 97.8 jit_solution(2388944172262961150)
XLA Ops:
  0.6 0.0 copy-start
  0.7 0.8 copy-done.2
  1.5 0.1 shard_map.50.level_ref
  1.6 0.0 copy-start.1
  1.6 1.1 %copy-done.1 = bf16[6,8,32,256]{3,2,1,0:T(8,128)(2,1)S(1)} copy-done((bf16[6,8,32,256]{3,2,1,0:T(8,128)(2,1)S(1)}, bf16[6,8,32,256]{3,2,1,0:T(8,128)(2,1)}, u32[]{:S(2)}) %copy-start.1) | copy-done | bytes 786456
  2.7 0.5 shard_map.51
  3.2 3.0 %collective-permute-start = (bf16[416,256]{1,0:T(8,128)(2,1)S(1)}, bf16[416,256]{1,0:T(8,128)(2,1)S(1)}, u32[]{:S(2)}, u32[]{:S(2)}) collective-permute-start(bf16[416,256]{1,0:T(8,128)(2,1)S(1)} %get-tuple-element.19), channel_id=1, source_target_pairs={{0,1},{1,0},{4,5},{5,4},{2,3},{3,2},{6,7},{7,6},{8,9},{9,8},{12,13... | collective-permute-start | bytes 638984 | tf_op jit(solution)/shard_map/ppermute | solution.py:99
  6.2 1.5 %collective-permute-start.1 = (bf16[416,256]{1,0:T(8,128)(2,1)S(1)}, bf16[416,256]{1,0:T(8,128)(2,1)S(1)}, u32[]{:S(2)}, u32[]{:S(2)}) collective-permute-start(bf16[416,256]{1,0:T(8,128)(2,1)S(1)} %get-tuple-element.20), channel_id=1, source_target_pairs={{0,4},{1,5},{4,0},{5,1},{2,6},{3,7},{6,2},{7,3},{8,12},{9,13},{12,... | collective-permute-start | bytes 638984 | tf_op jit(solution)/shard_map/ppermute | solution.py:99
  7.7 0.0 collective-permute-start.2
  7.8 3.7 %collective-permute-done.refs_1_ = bf16[416,256]{1,0:T(8,128)(2,1)S(1)} collective-permute-done((bf16[416,256]{1,0:T(8,128)(2,1)S(1)}, bf16[416,256]{1,0:T(8,128)(2,1)S(1)}, u32[]{:S(2)}, u32[]{:S(2)}) %collective-permute-start) | collective-permute-done | bytes 213024 | tf_op jit(solution)/shard_map/ppermute | solution.py:99
  11.5 2.9 %collective-permute-done.1.refs_2_ = bf16[416,256]{1,0:T(8,128)(2,1)S(1)} collective-permute-done((bf16[416,256]{1,0:T(8,128)(2,1)S(1)}, bf16[416,256]{1,0:T(8,128)(2,1)S(1)}, u32[]{:S(2)}, u32[]{:S(2)}) %collective-permute-start.1) | collective-permute-done | bytes 213024 | tf_op jit(solution)/shard_map/ppermute | solution.py:99
  14.4 2.9 %collective-permute-done.2.refs_3_ = bf16[416,256]{1,0:T(8,128)(2,1)S(1)} collective-permute-done((bf16[416,256]{1,0:T(8,128)(2,1)S(1)}, bf16[416,256]{1,0:T(8,128)(2,1)S(1)}, u32[]{:S(2)}, u32[]{:S(2)}) %collective-permute-start.2) | collective-permute-done | bytes 213024 | tf_op jit(solution)/shard_map/ppermute | solution.py:99
  17.3 0.1 shard_map.52
  17.4 0.1 collective-permute-start.4
  17.5 0.5 collective-permute-start.6
  18.0 0.7 collective-permute-start.3
  18.7 0.8 shard_map.56.partial_ref
  19.5 0.8 shard_map.53.partial_ref
  20.3 0.0 collective-permute-done.4.other_ref.outer_ref
  20.3 0.0 collective-permute-done.6.other_ref
  20.3 0.6 shard_map.57.own_ref.refs_0_
  20.9 3.1 %collective-permute-start.7 = (bf16[2,384,256]{2,1,0:T(8,128)(2,1)S(1)}, bf16[2,384,256]{2,1,0:T(8,128)(2,1)S(1)}, u32[]{:S(2)}, u32[]{:S(2)}) collective-permute-start(bf16[2,384,256]{2,1,0:T(8,128)(2,1)S(1)} %shard_map.57.own_ref.refs_0_), channel_id=1, source_target_pairs={{0,2},{2,0},{1,3},{3,1},{4,6},{6,4},{5,7},{7,5},{8,10},{10,8},{9,1... | collective-permute-start | bytes 1179656 | tf_op jit(solution)/shard_map/ppermute | solution.py:292
  24.0 0.0 collective-permute-done.3.outer_ref
  24.0 0.6 shard_map.54.own_ref.refs_0_
  24.6 3.3 %collective-permute-start.9 = (bf16[2,384,256]{2,1,0:T(8,128)(2,1)S(1)}, bf16[2,384,256]{2,1,0:T(8,128)(2,1)S(1)}, u32[]{:S(2)}, u32[]{:S(2)}) collective-permute-start(bf16[2,384,256]{2,1,0:T(8,128)(2,1)S(1)} %shard_map.54.own_ref.refs_0_), channel_id=1, source_target_pairs={{0,2},{2,0},{1,3},{3,1},{4,6},{6,4},{5,7},{7,5},{8,10},{10,8},{9,1... | collective-permute-start | bytes 1179656 | tf_op jit(solution)/shard_map/ppermute | solution.py:292
  27.8 0.7 collective-permute-start.5
  28.5 0.8 shard_map.60.partial_ref
  29.3 0.8 shard_map.55.partial_ref
  30.1 0.7 shard_map.61.own_ref
  30.8 3.1 %collective-permute-start.10 = (bf16[2,384,256]{2,1,0:T(8,128)(2,1)S(1)}, bf16[2,384,256]{2,1,0:T(8,128)(2,1)S(1)}, u32[]{:S(2)}, u32[]{:S(2)}) collective-permute-start(bf16[2,384,256]{2,1,0:T(8,128)(2,1)S(1)} %shard_map.61.own_ref), channel_id=1, source_target_pairs={{0,2},{2,0},{1,3},{3,1},{4,6},{6,4},{5,7},{7,5},{8,10},{10,8},{9,1... | collective-permute-start | bytes 1179656 | tf_op jit(solution)/shard_map/ppermute | solution.py:292
  33.9 0.6 shard_map.58.own_ref
  34.5 3.2 %collective-permute-start.11 = (bf16[2,384,256]{2,1,0:T(8,128)(2,1)S(1)}, bf16[2,384,256]{2,1,0:T(8,128)(2,1)S(1)}, u32[]{:S(2)}, u32[]{:S(2)}) collective-permute-start(bf16[2,384,256]{2,1,0:T(8,128)(2,1)S(1)} %shard_map.58.own_ref), channel_id=1, source_target_pairs={{0,2},{2,0},{1,3},{3,1},{4,6},{6,4},{5,7},{7,5},{8,10},{10,8},{9,1... | collective-permute-start | bytes 1179656 | tf_op jit(solution)/shard_map/ppermute | solution.py:292
  37.7 0.7 collective-permute-start.8
  38.4 0.8 shard_map.62.partial_ref
  39.2 0.8 shard_map.59.partial_ref
  40.0 0.7 shard_map.63.refs_1_
  40.7 0.9 shard_map.64
  41.6 1.6 %collective-permute-start.12 = (bf16[384,256]{1,0:T(8,128)(2,1)S(1)}, bf16[384,256]{1,0:T(8,128)(2,1)S(1)}, u32[]{:S(2)}, u32[]{:S(2)}) collective-permute-start(bf16[384,256]{1,0:T(8,128)(2,1)S(1)} %get-tuple-element.27), channel_id=1, source_target_pairs={{0,1},{1,0},{4,5},{5,4},{2,3},{3,2},{6,7},{7,6},{8,9},{9,8},{12,13... | collective-permute-start | bytes 589832 | tf_op jit(solution)/shard_map/ppermute | solution.py:99
  43.2 1.5 %collective-permute-start.13 = (bf16[384,256]{1,0:T(8,128)(2,1)S(1)}, bf16[384,256]{1,0:T(8,128)(2,1)S(1)}, u32[]{:S(2)}, u32[]{:S(2)}) collective-permute-start(bf16[384,256]{1,0:T(8,128)(2,1)S(1)} %get-tuple-element.28), channel_id=1, source_target_pairs={{0,4},{1,5},{4,0},{5,1},{2,6},{3,7},{6,2},{7,3},{8,12},{9,13},{12,... | collective-permute-start | bytes 589832 | tf_op jit(solution)/shard_map/ppermute | solution.py:99
  44.7 0.4 collective-permute-start.14
  45.2 2.2 %collective-permute-done.12.refs_1_ = bf16[384,256]{1,0:T(8,128)(2,1)S(1)} collective-permute-done((bf16[384,256]{1,0:T(8,128)(2,1)S(1)}, bf16[384,256]{1,0:T(8,128)(2,1)S(1)}, u32[]{:S(2)}, u32[]{:S(2)}) %collective-permute-start.12) | collective-permute-done | bytes 196640 | tf_op jit(solution)/shard_map/ppermute | solution.py:99
  47.3 1.6 %collective-permute-done.13.refs_2_ = bf16[384,256]{1,0:T(8,128)(2,1)S(1)} collective-permute-done((bf16[384,256]{1,0:T(8,128)(2,1)S(1)}, bf16[384,256]{1,0:T(8,128)(2,1)S(1)}, u32[]{:S(2)}, u32[]{:S(2)}) %collective-permute-start.13) | collective-permute-done | bytes 196640 | tf_op jit(solution)/shard_map/ppermute | solution.py:99
  48.9 2.4 %collective-permute-done.14.refs_3_ = bf16[384,256]{1,0:T(8,128)(2,1)S(1)} collective-permute-done((bf16[384,256]{1,0:T(8,128)(2,1)S(1)}, bf16[384,256]{1,0:T(8,128)(2,1)S(1)}, u32[]{:S(2)}, u32[]{:S(2)}) %collective-permute-start.14) | collective-permute-done | bytes 196640 | tf_op jit(solution)/shard_map/ppermute | solution.py:99
  51.3 0.6 shard_map.65
  52.0 23.4 %all_to_all.10 = f32[32,4,384]{2,1,0:T(4,128)S(1)} all-to-all(f32[32,4,384]{2,1,0:T(4,128)S(1)} %get-tuple-element.30), channel_id=1, replica_groups=mesh['far'=4,'mid'=2,'core'=2,'gy'=2] {'far','mid','core','gy'}, dimensions={0} | all-to-all | bytes 393216 | tf_op jit(solution)/shard_map/all_to_all | solution.py:495
  75.3 0.1 reduce_sum.9
  75.4 11.4 %all_to_all.11.gram_ref = f32[32,4,384]{2,1,0:T(4,128)S(1)} all-to-all(f32[32,4,384]{2,1,0:T(4,128)S(1)} %broadcast_in_dim.2), channel_id=1, replica_groups=mesh['far'=4,'mid'=2,'core'=2,'gy'=2] {'far','mid','core','gy'}, dimensions={0} | all-to-all | bytes 393216 | tf_op jit(solution)/shard_map/all_to_all | solution.py:496
  86.8 11.0 %shard_map.66 = (bf16[1536,256]{1,0:T(8,128)(2,1)}, f32[256,256]{1,0:T(8,128)}) custom-call(f32[32,4,384]{2,1,0:T(4,128)S(1)} %all_to_all.11.gram_ref, bf16[1536,256]{1,0:T(8,128)(2,1)S(1)} %get-tuple-element.31.rows_ref), custom_call_target="tpu_custom_call" | custom-call | tf_op jit(solution)/shard_map/pallas_call | solution.py:477
  (9 shorter events, 0.1 us)
Async XLA Ops:
  0.6 18.1 %copy-start = (bf16[3,3,256,256]{3,2,1,0:T(8,128)(2,1)S(1)}, bf16[3,3,256,256]{3,2,1,0:T(8,128)(2,1)}, u32[]{:S(2)}) copy-start(bf16[3,3,256,256]{3,2,1,0:T(8,128)(2,1)} %constant.4.clone.weights_ref) | copy-start | bytes 3538948
  0.6 0.8 copy-start.2
  1.6 1.1 %copy-start.1 = (bf16[6,8,32,256]{3,2,1,0:T(8,128)(2,1)S(1)}, bf16[6,8,32,256]{3,2,1,0:T(8,128)(2,1)}, u32[]{:S(2)}) copy-start(bf16[6,8,32,256]{3,2,1,0:T(8,128)(2,1)} %param.3) | copy-start | bytes 2359300
  3.2 8.3 %collective-permute-start = (bf16[416,256]{1,0:T(8,128)(2,1)S(1)}, bf16[416,256]{1,0:T(8,128)(2,1)S(1)}, u32[]{:S(2)}, u32[]{:S(2)}) collective-permute-start(bf16[416,256]{1,0:T(8,128)(2,1)S(1)} %get-tuple-element.19), channel_id=1, source_target_pairs={{0,1},{1,0},{4,5},{5,4},{2,3},{3,2},{6,7},{7,6},{8,9},{9,8},{12,13... | collective-permute-start | bytes 638984 | tf_op jit(solution)/shard_map/ppermute | solution.py:99
  6.2 8.2 %collective-permute-start.1 = (bf16[416,256]{1,0:T(8,128)(2,1)S(1)}, bf16[416,256]{1,0:T(8,128)(2,1)S(1)}, u32[]{:S(2)}, u32[]{:S(2)}) collective-permute-start(bf16[416,256]{1,0:T(8,128)(2,1)S(1)} %get-tuple-element.20), channel_id=1, source_target_pairs={{0,4},{1,5},{4,0},{5,1},{2,6},{3,7},{6,2},{7,3},{8,12},{9,13},{12,... | collective-permute-start | bytes 638984 | tf_op jit(solution)/shard_map/ppermute | solution.py:99
  7.7 9.6 %collective-permute-start.2 = (bf16[416,256]{1,0:T(8,128)(2,1)S(1)}, bf16[416,256]{1,0:T(8,128)(2,1)S(1)}, u32[]{:S(2)}, u32[]{:S(2)}) collective-permute-start(bf16[416,256]{1,0:T(8,128)(2,1)S(1)} %get-tuple-element.21), channel_id=1, source_target_pairs={{0,5},{1,4},{4,1},{5,0},{2,7},{3,6},{6,3},{7,2},{8,13},{9,12},{12,... | collective-permute-start | bytes 638984 | tf_op jit(solution)/shard_map/ppermute | solution.py:99
  17.4 2.8 %collective-permute-start.4 = (bf16[2,384,256]{2,1,0:T(8,128)(2,1)S(1)}, bf16[2,384,256]{2,1,0:T(8,128)(2,1)S(1)}, u32[]{:S(2)}, u32[]{:S(2)}) collective-permute-start(bf16[2,384,256]{2,1,0:T(8,128)(2,1)S(1)} %get-tuple-element.24.own_ref.refs_0_), channel_id=1, source_target_pairs={{0,2},{2,0},{1,3},{3,1},{4,6},{6,4},{5,7},{7,5},{8,10},{10,8},{9,1... | collective-permute-start | bytes 1179656 | tf_op jit(solution)/shard_map/ppermute | solution.py:292
  17.5 2.8 %collective-permute-start.6 = (bf16[2,384,256]{2,1,0:T(8,128)(2,1)S(1)}, bf16[2,384,256]{2,1,0:T(8,128)(2,1)S(1)}, u32[]{:S(2)}, u32[]{:S(2)}) collective-permute-start(bf16[2,384,256]{2,1,0:T(8,128)(2,1)S(1)} %get-tuple-element.22.own_ref.refs_0_), channel_id=1, source_target_pairs={{0,2},{2,0},{1,3},{3,1},{4,6},{6,4},{5,7},{7,5},{8,10},{10,8},{9,1... | collective-permute-start | bytes 1179656 | tf_op jit(solution)/shard_map/ppermute | solution.py:292
  18.0 6.0 %collective-permute-start.3 = (bf16[2,384,256]{2,1,0:T(8,128)(2,1)S(1)}, bf16[2,384,256]{2,1,0:T(8,128)(2,1)S(1)}, u32[]{:S(2)}, u32[]{:S(2)}) collective-permute-start(bf16[2,384,256]{2,1,0:T(8,128)(2,1)S(1)} %get-tuple-element.22.own_ref.refs_0_), channel_id=1, source_target_pairs={{2,8},{10,16},{18,24},{8,2},{16,10},{24,18},{3,9},{11,17},{19,25},... | collective-permute-start | bytes 1179656 | tf_op jit(solution)/shard_map/ppermute | solution.py:298
  20.9 9.2 %collective-permute-start.7 = (bf16[2,384,256]{2,1,0:T(8,128)(2,1)S(1)}, bf16[2,384,256]{2,1,0:T(8,128)(2,1)S(1)}, u32[]{:S(2)}, u32[]{:S(2)}) collective-permute-start(bf16[2,384,256]{2,1,0:T(8,128)(2,1)S(1)} %shard_map.57.own_ref.refs_0_), channel_id=1, source_target_pairs={{0,2},{2,0},{1,3},{3,1},{4,6},{6,4},{5,7},{7,5},{8,10},{10,8},{9,1... | collective-permute-start | bytes 1179656 | tf_op jit(solution)/shard_map/ppermute | solution.py:292
  24.6 5.5 %collective-permute-start.9 = (bf16[2,384,256]{2,1,0:T(8,128)(2,1)S(1)}, bf16[2,384,256]{2,1,0:T(8,128)(2,1)S(1)}, u32[]{:S(2)}, u32[]{:S(2)}) collective-permute-start(bf16[2,384,256]{2,1,0:T(8,128)(2,1)S(1)} %shard_map.54.own_ref.refs_0_), channel_id=1, source_target_pairs={{0,2},{2,0},{1,3},{3,1},{4,6},{6,4},{5,7},{7,5},{8,10},{10,8},{9,1... | collective-permute-start | bytes 1179656 | tf_op jit(solution)/shard_map/ppermute | solution.py:292
  27.8 6.1 %collective-permute-start.5 = (bf16[2,384,256]{2,1,0:T(8,128)(2,1)S(1)}, bf16[2,384,256]{2,1,0:T(8,128)(2,1)S(1)}, u32[]{:S(2)}, u32[]{:S(2)}) collective-permute-start(bf16[2,384,256]{2,1,0:T(8,128)(2,1)S(1)} %shard_map.54.own_ref.refs_0_), channel_id=1, source_target_pairs={{2,8},{10,16},{18,24},{8,2},{16,10},{24,18},{3,9},{11,17},{19,25},... | collective-permute-start | bytes 1179656 | tf_op jit(solution)/shard_map/ppermute | solution.py:298
  30.8 9.2 %collective-permute-start.10 = (bf16[2,384,256]{2,1,0:T(8,128)(2,1)S(1)}, bf16[2,384,256]{2,1,0:T(8,128)(2,1)S(1)}, u32[]{:S(2)}, u32[]{:S(2)}) collective-permute-start(bf16[2,384,256]{2,1,0:T(8,128)(2,1)S(1)} %shard_map.61.own_ref), channel_id=1, source_target_pairs={{0,2},{2,0},{1,3},{3,1},{4,6},{6,4},{5,7},{7,5},{8,10},{10,8},{9,1... | collective-permute-start | bytes 1179656 | tf_op jit(solution)/shard_map/ppermute | solution.py:292
  34.5 5.4 %collective-permute-start.11 = (bf16[2,384,256]{2,1,0:T(8,128)(2,1)S(1)}, bf16[2,384,256]{2,1,0:T(8,128)(2,1)S(1)}, u32[]{:S(2)}, u32[]{:S(2)}) collective-permute-start(bf16[2,384,256]{2,1,0:T(8,128)(2,1)S(1)} %shard_map.58.own_ref), channel_id=1, source_target_pairs={{0,2},{2,0},{1,3},{3,1},{4,6},{6,4},{5,7},{7,5},{8,10},{10,8},{9,1... | collective-permute-start | bytes 1179656 | tf_op jit(solution)/shard_map/ppermute | solution.py:292
  37.7 2.9 %collective-permute-start.8 = (bf16[2,384,256]{2,1,0:T(8,128)(2,1)S(1)}, bf16[2,384,256]{2,1,0:T(8,128)(2,1)S(1)}, u32[]{:S(2)}, u32[]{:S(2)}) collective-permute-start(bf16[2,384,256]{2,1,0:T(8,128)(2,1)S(1)} %shard_map.58.own_ref), channel_id=1, source_target_pairs={{2,8},{10,16},{18,24},{8,2},{16,10},{24,18},{3,9},{11,17},{19,25},... | collective-permute-start | bytes 1179656 | tf_op jit(solution)/shard_map/ppermute | solution.py:298
  41.6 5.7 %collective-permute-start.12 = (bf16[384,256]{1,0:T(8,128)(2,1)S(1)}, bf16[384,256]{1,0:T(8,128)(2,1)S(1)}, u32[]{:S(2)}, u32[]{:S(2)}) collective-permute-start(bf16[384,256]{1,0:T(8,128)(2,1)S(1)} %get-tuple-element.27), channel_id=1, source_target_pairs={{0,1},{1,0},{4,5},{5,4},{2,3},{3,2},{6,7},{7,6},{8,9},{9,8},{12,13... | collective-permute-start | bytes 589832 | tf_op jit(solution)/shard_map/ppermute | solution.py:99
  43.2 5.7 %collective-permute-start.13 = (bf16[384,256]{1,0:T(8,128)(2,1)S(1)}, bf16[384,256]{1,0:T(8,128)(2,1)S(1)}, u32[]{:S(2)}, u32[]{:S(2)}) collective-permute-start(bf16[384,256]{1,0:T(8,128)(2,1)S(1)} %get-tuple-element.28), channel_id=1, source_target_pairs={{0,4},{1,5},{4,0},{5,1},{2,6},{3,7},{6,2},{7,3},{8,12},{9,13},{12,... | collective-permute-start | bytes 589832 | tf_op jit(solution)/shard_map/ppermute | solution.py:99
  44.7 6.6 %collective-permute-start.14 = (bf16[384,256]{1,0:T(8,128)(2,1)S(1)}, bf16[384,256]{1,0:T(8,128)(2,1)S(1)}, u32[]{:S(2)}, u32[]{:S(2)}) collective-permute-start(bf16[384,256]{1,0:T(8,128)(2,1)S(1)} %get-tuple-element.29), channel_id=1, source_target_pairs={{0,5},{1,4},{4,1},{5,0},{2,7},{3,6},{6,3},{7,2},{8,13},{9,12},{12,... | collective-permute-start | bytes 589832 | tf_op jit(solution)/shard_map/ppermute | solution.py:99
